TPU v7x, 512 devices: a whole 4x4x16 slice. The times are simulated.
512 devices in a mesh: pop: 64 (over z, x_lo, core), tensor: 8 (over y, x_hi).
Axes of the slice: x: 4 (x_hi: 2, x_lo: 2; x = x_hi * 2 + x_lo), y: 4, z: 16, core: 2. Of those that a mesh axis runs over, the one named last changes fastest.
Arguments:
- tokens: bfloat16 [12288, 5120], P('pop', 'tensor'), may hold values from -6 to 6
- base_weight: float32 [5120, 5120], P('tensor', 'pop'), may hold values from -0.078125 to 0.078125
- left_factors: float32 [512, 4, 5120], P('pop', None, 'tensor'), may hold values from -0.078125 to 0.078125
- right_factors: float32 [512, 4, 5120], P('pop'), may hold values from -6 to 6
- member_of: int32 [64, 192], P('pop'), may hold values from 0 to 7, never falling along the last dimension, each value on 1 to 96 neighbouring positions
- ranks: int32 [512], P('pop'), may hold values from 0 to 63
Outputs:
- outputs: float32 [12288, 5120], P('pop', 'tensor')
- update: float32 [5120, 5120], P('tensor', 'pop')
Inputs may be any that keep to these rules, and one draw needn't show every extreme that they name: A row g * 192 + r belongs to member g * 8 + member_of[g, r]; within each g the values never fall, every member has 1 to 96 rows and one has exactly 96.
All inputs are finite; a program needn't handle non-finite values.
Results may differ from a plain program's by a relative error of at most 0.0026.
Values may be sent and summed in bfloat16 or wider, within the bound.
No kernel may reach another device: no remote copies, remote signals or barrier semaphores. Data moves between devices by JAX's collectives and lax.ppermute only.
A program may use at most 128 MiB of HBM per device.

v0:
```python
import math

import jax
import jax.numpy as jnp
from jax import lax
from jax.sharding import PartitionSpec as P

D = 5120
RANK = 4
M_DEV = 8


perturb_scale = 0.5


def base_product(tokens, base_weight):
    base_half = base_weight.astype(jnp.bfloat16)
    partial_value = jnp.dot(
        tokens,
        lax.all_gather(base_half, "pop", axis=1, tiled=True),
        preferred_element_type=jnp.float32,
    )
    return lax.psum_scatter(partial_value, "tensor", scatter_dimension=1, tiled=True)


def forward(tokens, base_weight, left_factors, right_factors, member_of):
    base_out = base_product(tokens, base_weight)
    width = tokens.shape[1]
    selector = (member_of[0][:, None] == jnp.arange(M_DEV, dtype=jnp.int32)[None, :]).astype(
        jnp.float32
    )
    projected = jnp.einsum(
        "rd,mkd->mkr", tokens.astype(jnp.float32), left_factors, precision=lax.Precision.HIGHEST
    )
    local_coeffs = jnp.sum(projected * selector.T[:, None, :], axis=0)
    coefficient = lax.psum(local_coeffs, "tensor")
    offset = lax.axis_index("tensor") * width
    right_local = lax.dynamic_slice_in_dim(right_factors, offset, width, 2)
    weighted = coefficient[None, :, :] * selector.T[:, None, :]
    low_rank = jnp.einsum("mkr,mkd->rd", weighted, right_local, precision=lax.Precision.HIGHEST)
    return base_out + perturb_scale / math.sqrt(RANK) * low_rank


def rank_statistics(rank_values, members):
    overall = lax.psum(jnp.sum(rank_values), "pop")
    rank_mean = overall / members
    spread = lax.psum(jnp.sum((rank_values - rank_mean) ** 2), "pop")
    variance = spread / members
    return (rank_mean, lax.rsqrt(variance + 1e-05))


def update_block(left_factors, right_factors, ranks):
    members = left_factors.shape[0] * lax.axis_size("pop")
    update_scale = math.sqrt(D / (members * RANK))
    rank_values = ranks.astype(jnp.float32)
    blocks = lax.all_to_all(right_factors, "pop", split_axis=2, concat_axis=0, tiled=True)
    rank_mean, inv_spread = rank_statistics(rank_values, members)
    fitness = (rank_values - rank_mean) * inv_spread
    scaled_left = fitness[:, None, None] * left_factors
    summed = jnp.einsum(
        "mki,mkj->ij",
        lax.all_gather(scaled_left, "pop", axis=0, tiled=True),
        blocks,
        precision=lax.Precision.HIGHEST,
    )
    return update_scale * summed


def on_device(tokens, base_weight, left_factors, right_factors, member_of, ranks):
    outputs = forward(tokens, base_weight, left_factors, right_factors, member_of)
    update = update_block(left_factors, right_factors, ranks)
    return (outputs, update)


def solution(mesh):
    return jax.shard_map(
        on_device,
        mesh=mesh,
        in_specs=(
            P("pop", "tensor"),
            P("tensor", "pop"),
            P("pop", None, "tensor"),
            P("pop", None, None),
            P("pop", None),
            P("pop"),
        ),
        out_specs=(P("pop", "tensor"), P("tensor", "pop")),
        check_vma=False,
    )
```

profile of v0, /device:TPU:1, one launch (start us, length us, event | category | flops | bytes accessed | tf_op | source)
XLA Modules:
  0.0 478.9 jit_solution(8874829743283824201)
XLA Ops:
  7.2 1.6 convert_element_type.15
  8.9 0.0 all-gather.5.cloned.1.call-start
  8.9 1.3 convert_reduce_fusion
  10.2 113.4 %psum.22 = f32[]{:T(128)} all-reduce(f32[]{:T(128)} %convert_reduce_fusion), channel_id=1, replica_groups=mesh['pop'=64,'tensor'=8] {'pop'}, use_global_device_ids=true, to_apply=%region_4.0 | all-reduce | flops 1 | bytes 8 | tf_op jit(solution)/shard_map/psum | solution.py:45
  124.2 1.3 multiply_reduce_fusion
  125.5 108.6 %psum.23 = f32[]{:T(128)} all-reduce(f32[]{:T(128)} %multiply_reduce_fusion), channel_id=1, replica_groups=mesh['pop'=64,'tensor'=8] {'pop'}, use_global_device_ids=true, to_apply=%region_6.0 | all-reduce | flops 1 | bytes 8 | tf_op jit(solution)/shard_map/psum | solution.py:47
  234.7 0.7 fusion.11
  235.4 1.6 copy_multiply_fusion
  237.0 0.0 reduce-scatter.2.cloned.1.call-start
  237.1 7.2 %fusion.13 = f32[192,5120]{1,0:T(8,128)} fusion(bf16[192,640]{1,0:T(8,128)(2,1)S(1)} %copy-done, bf16[640,5120]{0,1:T(8,128)(2,1)} %all-gather.3.cloned.1.call-done), kind=kOutput, calls=%fused_computation.21 | convolution fusion | flops 1258291200 | bytes 10731520 | tf_op jit(solution)/shard_map/dot_general | solution.py:18
  244.3 6.5 %copy.22 = f32[8,4,5120]{0,1,2:T(4,128)} copy(f32[8,4,5120]{2,1,0:T(4,128)S(1)} %copy-done.1) | data formatting | bytes 1310720 | tf_op args[3]
  250.8 14.3 %reshape.29 = f32[64,1,2560]{2,1,0:T(1,128)} reshape(f32[5120,4,8]{2,1,0:T(4,128)} %bitcast.27) | data formatting | bytes 1310720
  265.1 6.6 %all-to-all-start = ((f32[64,1,2560]{2,1,0:T(1,128)}), f32[64,1,2560]{2,1,0:T(1,128)S(1)}, u32[]{:S(2)}, u32[]{:S(2)}) async-start(f32[64,1,2560]{2,1,0:T(1,128)} %reshape.29), calls=%async_computation.1 | async-start | bytes 1310720 | tf_op jit(solution)/shard_map/all_to_all | solution.py:56
  271.7 0.4 fusion.3
  272.1 21.8 %psum.21 = f32[4,192]{1,0:T(4,128)S(1)} all-reduce(f32[4,192]{1,0:T(4,128)S(1)} %fusion.3), channel_id=1, replica_groups=mesh['pop'=64,'tensor'=8] {'tensor'}, use_global_device_ids=true, to_apply=%region_2.0 | all-reduce | flops 768 | bytes 6144 | tf_op jit(solution)/shard_map/psum | solution.py:36
  293.9 21.6 %all-to-all-done = f32[64,1,2560]{2,1,0:T(1,128)S(1)} async-done(((f32[64,1,2560]{2,1,0:T(1,128)}), f32[64,1,2560]{2,1,0:T(1,128)S(1)}, u32[]{:S(2)}, u32[]{:S(2)}) %all-to-all-start) | async-done | bytes 655392 | tf_op jit(solution)/shard_map/all_to_all | solution.py:56
  315.5 0.5 broadcast.13
  316.0 2.2 reduce
  318.2 14.1 %reshape.30 = f32[5120,4,8]{2,1,0:T(4,128)} reshape(f32[64,2560]{1,0:T(8,128)S(1)} %reduce) | data formatting | bytes 1310720
  332.3 7.5 %copy.23 = f32[8,4,64,80]{3,0,2,1:T(8,128)S(1)} copy(f32[8,4,64,80]{0,1,3,2:T(4,128)} %bitcast.26) | data formatting | bytes 1310720 | tf_op jit(solution)/shard_map/all_to_all | solution.py:56
  339.8 32.4 %all-gather.5.cloned.1.call-done = f32[512,4,640]{2,0,1:T(8,128)} async-done(((f32[8,4,640]{2,0,1:T(8,128)}), f32[512,4,640]{2,0,1:T(8,128)}) %all-gather.5.cloned.1.call-update) | async-done | bytes 5242896 | tf_op jit(solution)/shard_map/all_gather | solution.py:62
  372.2 6.6 %fusion.2 = f32[640,80]{0,1:T(8,128)} fusion(f32[512,4,640]{2,0,1:T(8,128)} %all-gather.5.cloned.1.call-done, f32[8,4,64,80]{3,0,2,1:T(8,128)S(1)} %copy.23), kind=kOutput, calls=%fused_computation.4 | convolution fusion | flops 1258342400 | bytes 6103040 | tf_op jit(solution)/shard_map/mki,mkj->ij/dot_general | solution.py:60
  378.7 91.1 %reduce-scatter.2.cloned.1.call-done = f32[192,640]{1,0:T(8,128)} async-done(((f32[192,5120]{1,0:T(8,128)}), f32[192,640]{1,0:T(8,128)}) %reduce-scatter.2.cloned.1.call-update) | async-done | bytes 491536 | tf_op jit(solution)/shard_map/reduce_scatter | solution.py:23
  469.9 2.5 fusion.1
  (14 shorter events, 0.1 us)
Async XLA Ops:
  7.2 230.0 %copy-start = (bf16[192,640]{1,0:T(8,128)(2,1)S(1)}, bf16[192,640]{1,0:T(8,128)(2,1)}, u32[]{:S(2)}) copy-start(bf16[192,640]{1,0:T(8,128)(2,1)} %param.6) | copy-start | bytes 737284
  7.2 229.9 %all-gather.3.cloned.1.call-start = ((), (), s32[]{:S(2)}) async-start(), calls=%async_computation.2 | async-start | bytes 6656000 | tf_op jit(solution)/shard_map/all_gather | solution.py:20
  8.9 363.3 %all-gather.5.cloned.1.call-start = ((), (), s32[]{:S(2)}) async-start(), calls=%async_computation.4 | async-start | bytes 5324800 | tf_op jit(solution)/shard_map/all_gather | solution.py:62
  237.0 7.3 %copy-start.1 = (f32[8,4,5120]{2,1,0:T(4,128)S(1)}, f32[8,4,5120]{2,1,0:T(4,128)}, u32[]{:S(2)}) copy-start(f32[8,4,5120]{2,1,0:T(4,128)} %param.9) | copy-start | bytes 1966084
  237.0 232.8 %reduce-scatter.2.cloned.1.call-start = ((), (), s32[]{:S(2)}) async-start(), calls=%async_computation.3 | async-start | bytes 4423680 | tf_op jit(solution)/shard_map/reduce_scatter | solution.py:23
  250.8 20.8 %copy-start.3 = (s32[1,192]{1,0:T(1,128)S(1)}, s32[1,192]{1,0:T(1,128)}, u32[]{:S(2)}) copy-start(s32[1,192]{1,0:T(1,128)} %param.10) | copy-start | bytes 2308
  250.8 20.9 %copy-start.2 = (f32[8,4,640]{2,1,0:T(4,128)S(1)}, f32[8,4,640]{2,1,0:T(4,128)}, u32[]{:S(2)}) copy-start(f32[8,4,640]{2,1,0:T(4,128)} %param.8) | copy-start | bytes 245764
  265.1 50.4 %all-to-all-start = ((f32[64,1,2560]{2,1,0:T(1,128)}), f32[64,1,2560]{2,1,0:T(1,128)S(1)}, u32[]{:S(2)}, u32[]{:S(2)}) async-start(f32[64,1,2560]{2,1,0:T(1,128)} %reshape.29), calls=%async_computation.1 | async-start | bytes 1310720 | tf_op jit(solution)/shard_map/all_to_all | solution.py:56
Sparse Core Ops, SparseCore 0:
  10.7 132.9 all-gather.2
  237.1 134.9 all-gather.4
  377.0 92.8 reduce-scatter.1
where the time goes:
time: 480 us; the launch traced here: 479 us
  blocking collectives  244 us (51%)
  waiting for transfers between devices  145 us (30%)
  local copies, waits for them, and re-layouts  42.9 us (9%)
  matrix products  16.6 us (3%)
  between operations  15.2 us (3%)
  other arithmetic  8.63 us (2%)
  starting transfers between devices  6.69 us (1%)
    psum x1, blocking collectives, rank_statistics(): overall = lax.psum(jnp.sum(rank_values), 'pop')  113 us
    psum x1, blocking collectives, rank_statistics(): spread = lax.psum(jnp.sum((rank_values - rank_mean) ** 2), 'pop')  109 us
    reduce_scatter x1, waiting for transfers between devices, base_product(): lax.psum_scatter(partial_value, 'tensor', scatter_dimension=1, tiled=True)  91.1 us
    unnamed x11, local copies, waits for them, and re-layouts  34.8 us
    all_gather x1, waiting for transfers between devices, update_block(): lax.all_gather(scaled_left, 'pop', axis=0, tiled=True)  32.4 us
    psum x1, blocking collectives, forward(): coefficient = lax.psum(local_coeffs, 'tensor')  21.8 us
    all_to_all x1, waiting for transfers between devices, update_block(): lax.all_to_all(right_factors, 'pop', split_axis=2, concat_axis=0, tiled=T...  21.6 us
  transfers between devices with their start and end apart: 4, of which 3 were waited for; matrix products, arithmetic and copies ran while one was open for 13% of the time, Pallas kernels for 0%

commit v1 on v0

v1 whole, which is shorter than its diff:
```python
import functools
import itertools
import math

import jax
import jax.numpy as jnp
from jax import lax
from jax.experimental import pallas as pl
from jax.experimental.pallas import tpu as pltpu
from jax.sharding import Mesh
from jax.sharding import PartitionSpec as P

D = 5120
RANK = 4
M_DEV = 8
ROWS = 192
IN_BLOCK = 640
OUT_BLOCK = 80
EXTRA = 112

perturb_scale = 0.5

SIZES = {"z": 16, "xl": 2, "core": 2, "y": 4, "xh": 2}
AXES = tuple(SIZES)
POP = ("z", "xl", "core")
TENSOR = ("y", "xh")
BF16 = jnp.bfloat16
F32 = jnp.float32


def flat(place):
    index = 0
    for value, size in zip(place, SIZES.values()):
        index = index * size + value % size
    return index


def move(value, target):
    places = itertools.product(*(range(n) for n in SIZES.values()))
    return lax.ppermute(value, AXES, [(flat(p), flat(target(*p))) for p in places])


def weight_target(shift, z, xl, core, y, xh):
    owner = z // 2
    to_y, to_xh = owner // 2, owner % 2
    column = (z % 2) * 4 + xl * 2 + core
    near = (y - to_y) % 4
    return ((near // 2) * 8 + column + shift, xh, near % 2, to_y, to_xh)


def right_target(flip, z, xl, core, y, xh):
    half = z // 2
    return (2 * (2 * y + xh) + ((z % 2) ^ flip), half // 4, core, half % 4, xl)


def rows_target(flip, z, xl, core, y, xh):
    return (z, xh, core, y, xl ^ flip)


def ring_target(z, xl, core, y, xh):
    return (z + (1 if core == 0 else -1), xl, core, y, xh)


def core_target(z, xl, core, y, xh):
    return (z, xl, 1 - core, y, xh)


def xl_target(z, xl, core, y, xh):
    return (z, 1 - xl, core, y, xh)


def y_target(step, z, xl, core, y, xh):
    return (z, xl, core, y + step, xh)


def y_far_target(z, xl, core, y, xh):
    return (z, xl, core, y + (1 if core == 0 else -1), xh)


def nt_dot(a, b):
    return lax.dot_general(a, b, (((1,), (1,)), ((), ())), preferred_element_type=F32)


def split(value):
    high = lax.reduce_precision(value, 8, 7)
    return high.astype(BF16), (value - high).astype(BF16)


def product_kernel(
    place, q, r1, r2, r3, s1, s2, s3, r4, s4, t0, t1, t2, t3, mine, mine_proj, give, weights, total, proj
):
    z, core, own = place[0], place[1], place[2]
    sign = 2 * core - 1

    def put(near, column, block):
        rows = pl.ds(pl.multiple_of(column * OUT_BLOCK, 16), OUT_BLOCK)
        weights[near, rows, :] = block

    def put_all(offset, ref):
        column = lax.rem(z + 16 + offset, 8)
        for near in range(4):
            put(near, column, ref[near * OUT_BLOCK : (near + 1) * OUT_BLOCK, :])

    put_all(0, q)
    for step, (ring, swapped) in enumerate(((r1, s1), (r2, s2), (r3, s3)), 1):
        put_all(sign * step, ring)
        put_all(-sign * step, swapped)
    last = lax.rem(z + 4, 8)
    for i in range(2):
        put(2 * core + i, last, r4[i * OUT_BLOCK : (i + 1) * OUT_BLOCK, :])
        put(2 * (1 - core) + i, last, s4[i * OUT_BLOCK : (i + 1) * OUT_BLOCK, :])

    for near, rows in enumerate((t0, t1, t2, t3)):
        part = nt_dot(rows[: 2 * ROWS, :], weights[near])
        total[...] = part if near == 0 else total[...] + part
        for m in range(2):
            left = rows[2 * ROWS + m * EXTRA : 2 * ROWS + m * EXTRA + 32, :]
            part = nt_dot(rows[m * ROWS : (m + 1) * ROWS, :], left)
            block = slice(m * ROWS, (m + 1) * ROWS)
            proj[block, :] = part if near == 0 else proj[block, :] + part
    here = pl.ds(pl.multiple_of(own * ROWS, ROWS), ROWS)
    there = pl.ds(pl.multiple_of((1 - own) * ROWS, ROWS), ROWS)
    mine[...] = total[here, :]
    mine_proj[...] = proj[here, :]
    give[:, :IN_BLOCK] = total[there, :].astype(BF16)
    give[:, IN_BLOCK:] = jnp.zeros((ROWS, 256), BF16)
    high = proj[there, :].astype(BF16)
    give[:, IN_BLOCK : IN_BLOCK + 32] = high
    give[:, IN_BLOCK + 128 : IN_BLOCK + 160] = (proj[there, :] - high.astype(F32)).astype(BF16)


def product(place, *arrays):
    vmem = pl.BlockSpec(memory_space=pltpu.VMEM)
    return pl.pallas_call(
        product_kernel,
        out_shape=(
            jax.ShapeDtypeStruct((ROWS, IN_BLOCK), F32),
            jax.ShapeDtypeStruct((ROWS, 32), F32),
            jax.ShapeDtypeStruct((ROWS, IN_BLOCK + 256), BF16),
        ),
        in_specs=[pl.BlockSpec(memory_space=pltpu.SMEM)] + [vmem] * len(arrays),
        out_specs=(vmem, vmem, vmem),
        scratch_shapes=[
            pltpu.VMEM((4, IN_BLOCK, IN_BLOCK), BF16),
            pltpu.VMEM((2 * ROWS, IN_BLOCK), F32),
            pltpu.VMEM((2 * ROWS, 32), F32),
        ],
        compiler_params=pltpu.CompilerParams(vmem_limit_bytes=40 * 2**20),
        cost_estimate=pl.CostEstimate(
            flops=2 * 384 * 640 * 2560, bytes_accessed=8 * 2**20, transcendentals=0
        ),
    )(place, *arrays)


def spread_weights(base_weight, z, core):
    piece = base_weight.T.astype(BF16)
    first = move(piece, functools.partial(weight_target, 0))
    second = move(piece, functools.partial(weight_target, 8))
    pair = jnp.where(z < 8, jnp.stack([first, second]), jnp.stack([second, first]))
    other = move(pair, core_target)
    whole = jnp.where(core == 0, jnp.stack([pair, other], 1), jnp.stack([other, pair], 1))
    return whole.reshape(4 * OUT_BLOCK, IN_BLOCK)


def ring(whole, core):
    held, swapped = [], []
    block = whole
    for step in range(4):
        if step == 3:
            half = 2 * OUT_BLOCK
            block = jnp.where(core == 0, block[:half], block[half:])
        block = move(block, ring_target)
        held.append(block)
        swapped.append(move(block, core_target))
    return held, swapped


def spread_right(right_local, ranks, z):
    chunks = right_local.reshape(32, 2, 320)
    levels = jnp.zeros((16, 320), BF16).at[0, :M_DEV].set(ranks.astype(BF16))
    parity = z % 2
    parts = []
    for flip in range(2):
        chunk = jnp.where(parity == flip, chunks[:, 0], chunks[:, 1])
        high, low = split(chunk)
        sent = jnp.concatenate([high, low, levels])
        parts.append(move(sent, functools.partial(right_target, flip)))
    return jnp.concatenate(parts, 1)


def spread_rows(payload, core):
    a = move(payload, functools.partial(rows_target, 0))
    b = move(payload, functools.partial(rows_target, 1))
    near = jnp.concatenate([a[:ROWS], b[:ROWS], a[ROWS:], b[ROWS:]])
    above = move(near, functools.partial(y_target, -1))
    below = move(near, functools.partial(y_target, 1))
    far = move(jnp.where(core == 0, below, above), y_far_target)
    return near, above, far, below


def scaled_right(blocks, z, y, xh, members):
    extra = jnp.stack([b[2 * ROWS :].reshape(2, EXTRA, 2, 320) for b in blocks])
    high, low, levels = extra[:, :, 32:64], extra[:, :, 64:96], extra[:, :, 96, :, :M_DEV]
    right = (high.astype(F32) + low.astype(F32)).transpose(0, 1, 3, 2, 4)
    levels = levels.astype(F32)
    own = jnp.pad(levels.reshape(16, M_DEV), ((0, 0), (0, 120)))
    core_side = move(own, core_target)
    both = jnp.concatenate([own[:, :M_DEV], core_side[:, :M_DEV]], 1)
    xl_side = move(jnp.pad(both, ((0, 0), (0, 112))), xl_target)
    every = jnp.concatenate([both, xl_side[:, : 2 * M_DEV]], 1)
    rank_mean = jnp.sum(every) / members
    variance = jnp.sum((every - rank_mean) ** 2) / members
    fitness = (levels - rank_mean) * lax.rsqrt(variance + 1e-05)
    scaled = jnp.repeat(fitness, RANK, axis=3)[..., None] * right
    scaled = jnp.where(xh == 0, scaled, scaled[:, ::-1])
    scaled = jnp.where(z % 2 == 0, scaled, scaled[:, :, ::-1])
    scaled = lax.dynamic_slice_in_dim(jnp.concatenate([scaled, scaled]), 4 - y, 4, 0)
    scaled = scaled.transpose(1, 0, 2, 3, 4).reshape(16 * 32, 320)
    return jnp.concatenate(split(scaled), 1)


def update_block(left_all, scaled, xl, core, members):
    product_t = lax.dot_general(
        scaled, left_all, (((0,), (0,)), ((), ())), preferred_element_type=F32
    )
    product_t = (product_t[:320] + product_t[320:]).reshape(2, 2, OUT_BLOCK, IN_BLOCK)
    keep = jnp.where(core == 0, product_t[:, 0], product_t[:, 1])
    give = jnp.where(core == 0, product_t[:, 1], product_t[:, 0])
    keep = keep + move(give, core_target)
    give = jnp.where(xl == 0, keep[1], keep[0])
    keep = jnp.where(xl == 0, keep[0], keep[1])
    total = keep + move(give, xl_target)
    return (math.sqrt(D / (members * RANK)) * total).T


def on_device(tokens, base_weight, left_factors, right_factors, member_of, ranks):
    z, xl, core, y, xh = (lax.axis_index(name) for name in AXES)
    members = M_DEV * 64
    left = left_factors.astype(BF16).reshape(32, IN_BLOCK)
    left_all = lax.all_gather(left, "z", axis=0, tiled=True)

    offset = (y * 2 + xh) * IN_BLOCK
    right_local = lax.dynamic_slice_in_dim(right_factors, offset, IN_BLOCK, 2).reshape(32, IN_BLOCK)
    whole = spread_weights(base_weight, z, core)
    right = spread_right(right_local, ranks, z)
    held, swapped = ring(whole, core)
    blocks = spread_rows(jnp.concatenate([tokens, left, right]), core)

    place = jnp.stack([z, core, xl ^ xh]).astype(jnp.int32)
    mine, mine_proj, give = product(
        place, whole, *held[:3], *swapped[:3], held[3], swapped[3], *blocks
    )
    got = move(give, xl_target).astype(F32)
    proj = mine_proj + got[:, IN_BLOCK : IN_BLOCK + 32] + got[:, IN_BLOCK + 128 : IN_BLOCK + 160]
    factor = jnp.arange(32, dtype=jnp.int32) // RANK
    mask = member_of[0][:, None] == factor[None, :]
    coefficient = jnp.where(mask, proj, 0.0) * (perturb_scale / math.sqrt(RANK))
    low_rank = jnp.dot(coefficient, right_local, precision=lax.Precision.HIGHEST)
    outputs = mine + got[:, :IN_BLOCK] + low_rank

    scaled = scaled_right(blocks, z, y, xh, members)
    update = update_block(left_all, scaled, xl, core, members)
    return (outputs, update)


def solution(mesh):
    fine = Mesh(mesh.devices.reshape(tuple(SIZES.values())), AXES)
    return jax.shard_map(
        on_device,
        mesh=fine,
        in_specs=(
            P(POP, TENSOR),
            P(TENSOR, POP),
            P(POP, None, TENSOR),
            P(POP, None, None),
            P(POP, None),
            P(POP),
        ),
        out_specs=(P(POP, TENSOR), P(TENSOR, POP)),
        check_vma=False,
    )
```

time: 480 us -> 207 us (0.43)
  blocking collectives: 244 us -> 28 us
  waiting for transfers between devices: 145 us -> 17 us
  starting transfers between devices: 6.69 us -> 106 us
  local copies, waits for them, and re-layouts: 42.9 us -> 24.9 us
  matrix products: 16.6 us -> 1.47 us
  between operations: 15.2 us -> 3.97 us
  other arithmetic: 8.63 us -> 18.8 us
  Pallas kernels: 0 us -> 5.44 us
    psum x3 -> x0, blocking collectives: 244 us -> none  [the longest x1 113 us: rank_statistics(): overall = lax.psum(jnp.sum(rank_values), 'pop')]
    ppermute x0 -> x23, starting transfers between devices: none -> 106 us  [move(): lax.ppermute(value, AXES, [(flat(p), flat(target(*p))) for p in places])]
    reduce_scatter x1 -> x0, waiting for transfers between devices: 91.1 us -> none  [base_product(): lax.psum_scatter(partial_value, 'tensor', scatter_dimension=1, tiled=True)]
    all_gather x2 -> x0, waiting for transfers between devices: 32.4 us -> none  [the longest x1 32.4 us: update_block(): lax.all_gather(scaled_left, 'pop', axis=0, tiled=True)]
    all_gather x0 -> x1, blocking collectives: none -> 28 us  [on_device(): left_all = lax.all_gather(left, 'z', axis=0, tiled=True)]
    unnamed x11 -> x29, local copies, waits for them, and re-layouts: 34.8 us -> 9.09 us
    all_to_all x1 -> x0, waiting for transfers between devices: 21.6 us -> none  [update_block(): lax.all_to_all(right_factors, 'pop', split_axis=2, concat_axis=0, tiled=T...]
    ppermute x0 -> x23, waiting for transfers between devices: none -> 17 us  [move(): lax.ppermute(value, AXES, [(flat(p), flat(target(*p))) for p in places])]
  transfers between devices with their start and end apart: 4 -> 23, of which waited for: 3 -> 5; matrix products, arithmetic and copies ran while one was open for 13% -> 19% of each run, Pallas kernels for 0% -> 3%
where the time goes in v1:
time: 207 us; the launch traced here: 205 us
  starting transfers between devices  106 us (51%)
  blocking collectives  28 us (14%)
  local copies, waits for them, and re-layouts  24.9 us (12%)
  other arithmetic  18.8 us (9%)
  waiting for transfers between devices  17 us (8%)
  Pallas kernels  5.44 us (3%)
  between operations  3.97 us (2%)
    ppermute x23, starting transfers between devices, move(): lax.ppermute(value, AXES, [(flat(p), flat(target(*p))) for p in places])  106 us
    all_gather x1, blocking collectives, on_device(): left_all = lax.all_gather(left, 'z', axis=0, tiled=True)  28 us
    ppermute x23, waiting for transfers between devices, move(): lax.ppermute(value, AXES, [(flat(p), flat(target(*p))) for p in places])  17 us
    another operation x5, local copies, waits for them, and re-layouts, scaled_right(): extra = jnp.stack([b[2 * ROWS:].reshape(2, EXTRA, 2, 320) for b in blocks])  9.91 us
    unnamed x29, local copies, waits for them, and re-layouts  9.09 us
    pallas_call x1, Pallas kernels, product(): pl.pallas_call(product_kernel, out_shape=(jax.ShapeDtypeStruct((ROWS, IN_...  5.44 us
  transfers between devices with their start and end apart: 23, of which 5 were waited for; matrix products, arithmetic and copies ran while one was open for 19% of the time, Pallas kernels for 3%

profile of v1, /device:TPU:1, one launch (start us, length us, event | category | flops | bytes accessed | tf_op | source)
XLA Modules:
  0.0 205.2 jit_solution(12203908531120619260)
XLA Ops:
  3.4 4.4 %collective-permute-start.12 = (bf16[80,320]{1,0:T(8,128)(2,1)S(1)}, bf16[80,320]{1,0:T(8,128)(2,1)S(1)}, u32[]{:S(2)}, u32[]{:S(2)}) collective-permute-start(bf16[80,320]{1,0:T(8,128)(2,1)S(1)} %get-tuple-element.33), channel_id=1, source_target_pairs={{0,32},{1,96},{2,160},{3,224},{4,288},{5,352},{6,416},{7,480},{8,4... | collective-permute-start | bytes 153608 | tf_op jit(solution)/shard_map/ppermute | solution.py:40
  8.7 8.0 %collective-permute-start = (bf16[80,640]{1,0:T(8,128)(2,1)S(1)}, bf16[80,640]{1,0:T(8,128)(2,1)S(1)}, u32[]{:S(2)}, u32[]{:S(2)}) collective-permute-start(bf16[80,640]{1,0:T(8,128)(2,1)S(1)} %convert_bitcast_fusion), channel_id=1, source_target_pairs={{0,0},{1,16},{2,8},{3,24},{4,256},{5,272},{6,264},{7,280},{8,32},{... | collective-permute-start | bytes 307208 | tf_op jit(solution)/shard_map/ppermute | solution.py:40
  16.6 19.6 %collective-permute-start.1 = (bf16[80,640]{1,0:T(8,128)(2,1)S(1)}, bf16[80,640]{1,0:T(8,128)(2,1)S(1)}, u32[]{:S(2)}, u32[]{:S(2)}) collective-permute-start(bf16[80,640]{1,0:T(8,128)(2,1)S(1)} %convert_bitcast_fusion), channel_id=1, source_target_pairs={{0,256},{1,272},{2,264},{3,280},{4,0},{5,16},{6,8},{7,24},{8,288},... | collective-permute-start | bytes 307208 | tf_op jit(solution)/shard_map/ppermute | solution.py:40
  37.1 10.1 %collective-permute-start.14 = (bf16[304,640]{1,0:T(8,128)(2,1)S(1)}, bf16[304,640]{1,0:T(8,128)(2,1)S(1)}, u32[]{:S(2)}, u32[]{:S(2)}) collective-permute-start(bf16[304,640]{1,0:T(8,128)(2,1)S(1)} %maximum_maximum_fusion), channel_id=1, source_target_pairs={{0,1},{1,17},{2,3},{3,19},{4,5},{5,21},{6,7},{7,23},{8,9},{9,25},{... | collective-permute-start | bytes 1167368 | tf_op jit(solution)/shard_map/ppermute | solution.py:40
  50.7 8.0 %collective-permute-start.3 = (bf16[320,640]{1,0:T(8,128)(2,1)S(1)}, bf16[320,640]{1,0:T(8,128)(2,1)S(1)}, u32[]{:S(2)}, u32[]{:S(2)}) collective-permute-start(bf16[320,640]{1,0:T(8,128)(2,1)S(1)} %bitcast.60), channel_id=1, source_target_pairs={{0,32},{1,33},{2,34},{3,35},{4,36},{5,37},{6,38},{7,39},{8,488},{9... | collective-permute-start | bytes 1228808 | tf_op jit(solution)/shard_map/ppermute | solution.py:40
  61.3 4.7 %collective-permute-start.16 = (bf16[608,640]{1,0:T(8,128)(2,1)S(1)}, bf16[608,640]{1,0:T(8,128)(2,1)S(1)}, u32[]{:S(2)}, u32[]{:S(2)}) collective-permute-start(bf16[608,640]{1,0:T(8,128)(2,1)S(1)} %pad_maximum_fusion.t0), channel_id=1, source_target_pairs={{0,2},{1,3},{2,4},{3,5},{4,6},{5,7},{6,0},{7,1},{8,10},{9,11},{10,... | collective-permute-start | bytes 2334728 | tf_op jit(solution)/shard_map/ppermute | solution.py:40
  66.1 2.5 %collective-permute-start.4 = (bf16[320,640]{1,0:T(8,128)(2,1)S(1)}, bf16[320,640]{1,0:T(8,128)(2,1)}, u32[]{:S(2)}, u32[]{:S(2)}) collective-permute-start(bf16[320,640]{1,0:T(8,128)(2,1)S(1)} %collective-permute-done.3.r1), channel_id=1, source_target_pairs={{0,32},{1,33},{2,34},{3,35},{4,36},{5,37},{6,38},{7,39},{8,488},{9... | collective-permute-start | bytes 1228808 | tf_op jit(solution)/shard_map/ppermute | solution.py:40
  68.6 6.5 %collective-permute-done.4.r2 = bf16[320,640]{1,0:T(8,128)(2,1)} collective-permute-done((bf16[320,640]{1,0:T(8,128)(2,1)S(1)}, bf16[320,640]{1,0:T(8,128)(2,1)}, u32[]{:S(2)}, u32[]{:S(2)}) %collective-permute-start.4) | collective-permute-done | bytes 409632 | tf_op jit(solution)/shard_map/ppermute | solution.py:40
  75.2 3.6 %collective-permute-start.5 = (bf16[320,640]{1,0:T(8,128)(2,1)}, bf16[320,640]{1,0:T(8,128)(2,1)}, u32[]{:S(2)}, u32[]{:S(2)}) collective-permute-start(bf16[320,640]{1,0:T(8,128)(2,1)} %collective-permute-done.4.r2), channel_id=1, source_target_pairs={{0,32},{1,33},{2,34},{3,35},{4,36},{5,37},{6,38},{7,39},{8,488},{9... | collective-permute-start | bytes 1228808 | tf_op jit(solution)/shard_map/ppermute | solution.py:40
  78.8 4.7 %collective-permute-done.16.t3 = bf16[608,640]{1,0:T(8,128)(2,1)S(1)} collective-permute-done((bf16[608,640]{1,0:T(8,128)(2,1)S(1)}, bf16[608,640]{1,0:T(8,128)(2,1)S(1)}, u32[]{:S(2)}, u32[]{:S(2)}) %collective-permute-start.16) | collective-permute-done | bytes 778272 | tf_op jit(solution)/shard_map/ppermute | solution.py:40
  84.5 4.5 %collective-permute-start.17 = (bf16[608,640]{1,0:T(8,128)(2,1)}, bf16[608,640]{1,0:T(8,128)(2,1)}, u32[]{:S(2)}, u32[]{:S(2)}) collective-permute-start(bf16[608,640]{1,0:T(8,128)(2,1)} %broadcast_select_fusion.1), channel_id=1, source_target_pairs={{0,2},{1,3},{2,4},{3,5},{4,6},{5,7},{6,0},{7,1},{8,14},{9,15},{10,... | collective-permute-start | bytes 2334728 | tf_op jit(solution)/shard_map/ppermute | solution.py:40
  89.0 28.0 %all_gather.3 = bf16[512,640]{1,0:T(8,128)(2,1)} all-gather(bf16[32,640]{1,0:T(8,128)(2,1)S(1)} %reshape.146), channel_id=1, replica_groups=mesh['z'=16,'xl'=2,'core'=2,'y'=4,'xh'=2] {'z'}, dimensions={0}, use_global_device_ids=true | all-gather | bytes 696320 | tf_op jit(solution)/shard_map/all_gather | solution.py:240
  118.8 2.0 stack_reshape.12
  126.4 9.0 %collective-permute-start.6 = (bf16[320,640]{1,0:T(8,128)(2,1)}, bf16[320,640]{1,0:T(8,128)(2,1)}, u32[]{:S(2)}, u32[]{:S(2)}) collective-permute-start(bf16[320,640]{1,0:T(8,128)(2,1)} %copy-done.3), channel_id=1, source_target_pairs={{0,8},{1,9},{2,10},{3,11},{4,12},{5,13},{6,14},{7,15},{8,0},{9,1},... | collective-permute-start | bytes 1228808 | tf_op jit(solution)/shard_map/ppermute | solution.py:40
  138.0 2.0 stack_reshape.13
  144.7 2.4 %collective-permute-start.8 = (bf16[320,640]{1,0:T(8,128)(2,1)}, bf16[320,640]{1,0:T(8,128)(2,1)}, u32[]{:S(2)}, u32[]{:S(2)}) collective-permute-start(bf16[320,640]{1,0:T(8,128)(2,1)} %collective-permute-done.5.r3), channel_id=1, source_target_pairs={{0,8},{1,9},{2,10},{3,11},{4,12},{5,13},{6,14},{7,15},{8,0},{9,1},... | collective-permute-start | bytes 1228808 | tf_op jit(solution)/shard_map/ppermute | solution.py:40
  152.7 2.0 constant_dynamic-update-slice_fusion.1
  157.4 2.4 %collective-permute-start.19 = (f32[16,128]{1,0:T(8,128)S(1)}, f32[16,128]{1,0:T(8,128)S(1)}, u32[]{:S(2)}, u32[]{:S(2)}) collective-permute-start(f32[16,128]{1,0:T(8,128)S(1)} %pad.13), channel_id=1, source_target_pairs={{0,8},{1,9},{2,10},{3,11},{4,12},{5,13},{6,14},{7,15},{8,0},{9,1},... | collective-permute-start | bytes 24584 | tf_op jit(solution)/shard_map/ppermute | solution.py:40
  159.8 5.4 %shard_map.77 = (f32[192,640]{1,0:T(8,128)S(1)}, f32[192,32]{1,0:T(8,128)S(1)}, bf16[192,896]{1,0:T(8,128)(2,1)}) custom-call(s32[3]{0:T(128)S(1)} %pad_add_fusion.place, bf16[320,640]{1,0:T(8,128)(2,1)S(1)} %bitcast.61, bf16[320,640]{1,0:T(8,128)(2,1)S(1)} %copy-done.4, bf16[320,640]{1,0:T(8,128)(2,1)} %collective-permute-done.4.r2, ...), custom_call_target="tpu_custom_call" | custom-call | flops 1258291200 | bytes 8388608 | tf_op jit(solution)/shard_map/pallas_call | solution.py:134
  166.7 7.8 %collective-permute-start.20 = (f32[16,128]{1,0:T(8,128)S(1)}, f32[16,128]{1,0:T(8,128)S(1)}, u32[]{:S(2)}, u32[]{:S(2)}) collective-permute-start(f32[16,128]{1,0:T(8,128)S(1)} %select_maximum_fusion), channel_id=1, source_target_pairs={{0,16},{1,17},{2,18},{3,19},{4,20},{5,21},{6,22},{7,23},{8,24},{9,... | collective-permute-start | bytes 24584 | tf_op jit(solution)/shard_map/ppermute | solution.py:40
  184.5 2.1 %rev.7 = f32[4,2,2,32,320]{4,2,3,1,0:T(2,128)S(1)} reverse(f32[4,2,2,32,320]{4,2,3,1,0:T(2,128)S(1)} %reverse_select_fusion), dimensions={2} | reverse | bytes 1310720 | tf_op jit(solution)/shard_map/rev | solution.py:216
  190.6 2.2 %collective-permute-start.21 = (f32[2,80,640]{2,1,0:T(8,128)}, f32[2,80,640]{2,1,0:T(8,128)}, u32[]{:S(2)}, u32[]{:S(2)}) collective-permute-start(f32[2,80,640]{2,1,0:T(8,128)} %select_bitcast_fusion), channel_id=1, source_target_pairs={{0,8},{1,9},{2,10},{3,11},{4,12},{5,13},{6,14},{7,15},{8,0},{9,1},... | collective-permute-start | bytes 1228808 | tf_op jit(solution)/shard_map/ppermute | solution.py:40
  195.7 3.6 %collective-permute-start.22 = (f32[80,640]{1,0:T(8,128)S(1)}, f32[80,640]{1,0:T(8,128)S(1)}, u32[]{:S(2)}, u32[]{:S(2)}) collective-permute-start(f32[80,640]{1,0:T(8,128)S(1)} %select_bitcast_fusion.1), channel_id=1, source_target_pairs={{0,16},{1,17},{2,18},{3,19},{4,20},{5,21},{6,22},{7,23},{8,24},{9,... | collective-permute-start | bytes 614408 | tf_op jit(solution)/shard_map/ppermute | solution.py:40
  200.2 4.3 %collective-permute-done.22 = f32[80,640]{1,0:T(8,128)S(1)} collective-permute-done((f32[80,640]{1,0:T(8,128)S(1)}, f32[80,640]{1,0:T(8,128)S(1)}, u32[]{:S(2)}, u32[]{:S(2)}) %collective-permute-start.22) | collective-permute-done | bytes 204832 | tf_op jit(solution)/shard_map/ppermute | solution.py:40
  (112 shorter events, 51.4 us)
Async XLA Ops:
  1.7 47.5 %copy-start.8 = (f32[8,4,640]{2,1,0:T(4,128)}, f32[8,4,640]{2,1,0:T(4,128)S(1)}, u32[]{:S(2)}) copy-start(f32[8,4,640]{2,1,0:T(4,128)S(1)} %constant_dynamic-slice_fusion) | copy-start | bytes 245764
  2.7 33.6 %collective-permute-start.11 = (bf16[80,320]{1,0:T(8,128)(2,1)S(1)}, bf16[80,320]{1,0:T(8,128)(2,1)S(1)}, u32[]{:S(2)}, u32[]{:S(2)}) collective-permute-start(bf16[80,320]{1,0:T(8,128)(2,1)S(1)} %get-tuple-element.32), channel_id=1, source_target_pairs={{0,0},{1,64},{2,128},{3,192},{4,256},{5,320},{6,384},{7,448},{8,8}... | collective-permute-start | bytes 153608 | tf_op jit(solution)/shard_map/ppermute | solution.py:40
  3.4 33.0 %collective-permute-start.12 = (bf16[80,320]{1,0:T(8,128)(2,1)S(1)}, bf16[80,320]{1,0:T(8,128)(2,1)S(1)}, u32[]{:S(2)}, u32[]{:S(2)}) collective-permute-start(bf16[80,320]{1,0:T(8,128)(2,1)S(1)} %get-tuple-element.33), channel_id=1, source_target_pairs={{0,32},{1,96},{2,160},{3,224},{4,288},{5,352},{6,416},{7,480},{8,4... | collective-permute-start | bytes 153608 | tf_op jit(solution)/shard_map/ppermute | solution.py:40
  8.7 38.5 %collective-permute-start = (bf16[80,640]{1,0:T(8,128)(2,1)S(1)}, bf16[80,640]{1,0:T(8,128)(2,1)S(1)}, u32[]{:S(2)}, u32[]{:S(2)}) collective-permute-start(bf16[80,640]{1,0:T(8,128)(2,1)S(1)} %convert_bitcast_fusion), channel_id=1, source_target_pairs={{0,0},{1,16},{2,8},{3,24},{4,256},{5,272},{6,264},{7,280},{8,32},{... | collective-permute-start | bytes 307208 | tf_op jit(solution)/shard_map/ppermute | solution.py:40
  16.6 30.6 %collective-permute-start.1 = (bf16[80,640]{1,0:T(8,128)(2,1)S(1)}, bf16[80,640]{1,0:T(8,128)(2,1)S(1)}, u32[]{:S(2)}, u32[]{:S(2)}) collective-permute-start(bf16[80,640]{1,0:T(8,128)(2,1)S(1)} %convert_bitcast_fusion), channel_id=1, source_target_pairs={{0,256},{1,272},{2,264},{3,280},{4,0},{5,16},{6,8},{7,24},{8,288},... | collective-permute-start | bytes 307208 | tf_op jit(solution)/shard_map/ppermute | solution.py:40
  36.4 22.3 %collective-permute-start.13 = (bf16[304,640]{1,0:T(8,128)(2,1)S(1)}, bf16[304,640]{1,0:T(8,128)(2,1)S(1)}, u32[]{:S(2)}, u32[]{:S(2)}) collective-permute-start(bf16[304,640]{1,0:T(8,128)(2,1)S(1)} %maximum_maximum_fusion), channel_id=1, source_target_pairs={{0,0},{1,16},{2,2},{3,18},{4,4},{5,20},{6,6},{7,22},{8,8},{9,24},{... | collective-permute-start | bytes 1167368 | tf_op jit(solution)/shard_map/ppermute | solution.py:40
  37.1 21.7 %collective-permute-start.14 = (bf16[304,640]{1,0:T(8,128)(2,1)S(1)}, bf16[304,640]{1,0:T(8,128)(2,1)S(1)}, u32[]{:S(2)}, u32[]{:S(2)}) collective-permute-start(bf16[304,640]{1,0:T(8,128)(2,1)S(1)} %maximum_maximum_fusion), channel_id=1, source_target_pairs={{0,1},{1,17},{2,3},{3,19},{4,5},{5,21},{6,7},{7,23},{8,9},{9,25},{... | collective-permute-start | bytes 1167368 | tf_op jit(solution)/shard_map/ppermute | solution.py:40
  47.3 3.3 %collective-permute-start.2 = (bf16[2,80,640]{2,1,0:T(8,128)(2,1)S(1)}, bf16[2,80,640]{2,1,0:T(8,128)(2,1)S(1)}, u32[]{:S(2)}, u32[]{:S(2)}) collective-permute-start(bf16[2,80,640]{2,1,0:T(8,128)(2,1)S(1)} %maximum_select_fusion.2), channel_id=1, source_target_pairs={{0,8},{1,9},{2,10},{3,11},{4,12},{5,13},{6,14},{7,15},{8,0},{9,1},... | collective-permute-start | bytes 614408 | tf_op jit(solution)/shard_map/ppermute | solution.py:40
  50.7 15.3 %collective-permute-start.3 = (bf16[320,640]{1,0:T(8,128)(2,1)S(1)}, bf16[320,640]{1,0:T(8,128)(2,1)S(1)}, u32[]{:S(2)}, u32[]{:S(2)}) collective-permute-start(bf16[320,640]{1,0:T(8,128)(2,1)S(1)} %bitcast.60), channel_id=1, source_target_pairs={{0,32},{1,33},{2,34},{3,35},{4,36},{5,37},{6,38},{7,39},{8,488},{9... | collective-permute-start | bytes 1228808 | tf_op jit(solution)/shard_map/ppermute | solution.py:40
  59.4 19.4 %collective-permute-start.15 = (bf16[608,640]{1,0:T(8,128)(2,1)S(1)}, bf16[608,640]{1,0:T(8,128)(2,1)S(1)}, u32[]{:S(2)}, u32[]{:S(2)}) collective-permute-start(bf16[608,640]{1,0:T(8,128)(2,1)S(1)} %pad_maximum_fusion.t0), channel_id=1, source_target_pairs={{0,6},{1,7},{2,0},{3,1},{4,2},{5,3},{6,4},{7,5},{8,14},{9,15},{10,... | collective-permute-start | bytes 2334728 | tf_op jit(solution)/shard_map/ppermute | solution.py:40
  61.3 22.2 %collective-permute-start.16 = (bf16[608,640]{1,0:T(8,128)(2,1)S(1)}, bf16[608,640]{1,0:T(8,128)(2,1)S(1)}, u32[]{:S(2)}, u32[]{:S(2)}) collective-permute-start(bf16[608,640]{1,0:T(8,128)(2,1)S(1)} %pad_maximum_fusion.t0), channel_id=1, source_target_pairs={{0,2},{1,3},{2,4},{3,5},{4,6},{5,7},{6,0},{7,1},{8,10},{9,11},{10,... | collective-permute-start | bytes 2334728 | tf_op jit(solution)/shard_map/ppermute | solution.py:40
  66.1 9.1 %collective-permute-start.4 = (bf16[320,640]{1,0:T(8,128)(2,1)S(1)}, bf16[320,640]{1,0:T(8,128)(2,1)}, u32[]{:S(2)}, u32[]{:S(2)}) collective-permute-start(bf16[320,640]{1,0:T(8,128)(2,1)S(1)} %collective-permute-done.3.r1), channel_id=1, source_target_pairs={{0,32},{1,33},{2,34},{3,35},{4,36},{5,37},{6,38},{7,39},{8,488},{9... | collective-permute-start | bytes 1228808 | tf_op jit(solution)/shard_map/ppermute | solution.py:40
  75.2 45.6 %collective-permute-start.5 = (bf16[320,640]{1,0:T(8,128)(2,1)}, bf16[320,640]{1,0:T(8,128)(2,1)}, u32[]{:S(2)}, u32[]{:S(2)}) collective-permute-start(bf16[320,640]{1,0:T(8,128)(2,1)} %collective-permute-done.4.r2), channel_id=1, source_target_pairs={{0,32},{1,33},{2,34},{3,35},{4,36},{5,37},{6,38},{7,39},{8,488},{9... | collective-permute-start | bytes 1228808 | tf_op jit(solution)/shard_map/ppermute | solution.py:40
  84.5 64.5 %collective-permute-start.17 = (bf16[608,640]{1,0:T(8,128)(2,1)}, bf16[608,640]{1,0:T(8,128)(2,1)}, u32[]{:S(2)}, u32[]{:S(2)}) collective-permute-start(bf16[608,640]{1,0:T(8,128)(2,1)} %broadcast_select_fusion.1), channel_id=1, source_target_pairs={{0,2},{1,3},{2,4},{3,5},{4,6},{5,7},{6,0},{7,1},{8,14},{9,15},{10,... | collective-permute-start | bytes 2334728 | tf_op jit(solution)/shard_map/ppermute | solution.py:40
  122.5 24.6 %collective-permute-start.9 = (bf16[160,640]{1,0:T(8,128)(2,1)}, bf16[160,640]{1,0:T(8,128)(2,1)}, u32[]{:S(2)}, u32[]{:S(2)}) collective-permute-start(bf16[160,640]{1,0:T(8,128)(2,1)} %slice_select_fusion), channel_id=1, source_target_pairs={{0,32},{1,33},{2,34},{3,35},{4,36},{5,37},{6,38},{7,39},{8,488},{9... | collective-permute-start | bytes 614408 | tf_op jit(solution)/shard_map/ppermute | solution.py:40
  126.4 33.4 %collective-permute-start.6 = (bf16[320,640]{1,0:T(8,128)(2,1)}, bf16[320,640]{1,0:T(8,128)(2,1)}, u32[]{:S(2)}, u32[]{:S(2)}) collective-permute-start(bf16[320,640]{1,0:T(8,128)(2,1)} %copy-done.3), channel_id=1, source_target_pairs={{0,8},{1,9},{2,10},{3,11},{4,12},{5,13},{6,14},{7,15},{8,0},{9,1},... | collective-permute-start | bytes 1228808 | tf_op jit(solution)/shard_map/ppermute | solution.py:40
  135.4 24.4 %collective-permute-start.7 = (bf16[320,640]{1,0:T(8,128)(2,1)}, bf16[320,640]{1,0:T(8,128)(2,1)}, u32[]{:S(2)}, u32[]{:S(2)}) collective-permute-start(bf16[320,640]{1,0:T(8,128)(2,1)} %collective-permute-done.4.r2), channel_id=1, source_target_pairs={{0,8},{1,9},{2,10},{3,11},{4,12},{5,13},{6,14},{7,15},{8,0},{9,1},... | collective-permute-start | bytes 1228808 | tf_op jit(solution)/shard_map/ppermute | solution.py:40
  144.7 15.1 %collective-permute-start.8 = (bf16[320,640]{1,0:T(8,128)(2,1)}, bf16[320,640]{1,0:T(8,128)(2,1)}, u32[]{:S(2)}, u32[]{:S(2)}) collective-permute-start(bf16[320,640]{1,0:T(8,128)(2,1)} %collective-permute-done.5.r3), channel_id=1, source_target_pairs={{0,8},{1,9},{2,10},{3,11},{4,12},{5,13},{6,14},{7,15},{8,0},{9,1},... | collective-permute-start | bytes 1228808 | tf_op jit(solution)/shard_map/ppermute | solution.py:40
  147.1 12.7 %collective-permute-start.10 = (bf16[160,640]{1,0:T(8,128)(2,1)}, bf16[160,640]{1,0:T(8,128)(2,1)}, u32[]{:S(2)}, u32[]{:S(2)}) collective-permute-start(bf16[160,640]{1,0:T(8,128)(2,1)} %collective-permute-done.9.r4), channel_id=1, source_target_pairs={{0,8},{1,9},{2,10},{3,11},{4,12},{5,13},{6,14},{7,15},{8,0},{9,1},... | collective-permute-start | bytes 614408 | tf_op jit(solution)/shard_map/ppermute | solution.py:40
  157.4 8.7 %collective-permute-start.19 = (f32[16,128]{1,0:T(8,128)S(1)}, f32[16,128]{1,0:T(8,128)S(1)}, u32[]{:S(2)}, u32[]{:S(2)}) collective-permute-start(f32[16,128]{1,0:T(8,128)S(1)} %pad.13), channel_id=1, source_target_pairs={{0,8},{1,9},{2,10},{3,11},{4,12},{5,13},{6,14},{7,15},{8,0},{9,1},... | collective-permute-start | bytes 24584 | tf_op jit(solution)/shard_map/ppermute | solution.py:40
  166.7 12.4 %collective-permute-start.20 = (f32[16,128]{1,0:T(8,128)S(1)}, f32[16,128]{1,0:T(8,128)S(1)}, u32[]{:S(2)}, u32[]{:S(2)}) collective-permute-start(f32[16,128]{1,0:T(8,128)S(1)} %select_maximum_fusion), channel_id=1, source_target_pairs={{0,16},{1,17},{2,18},{3,19},{4,20},{5,21},{6,22},{7,23},{8,24},{9,... | collective-permute-start | bytes 24584 | tf_op jit(solution)/shard_map/ppermute | solution.py:40
  175.9 17.0 %collective-permute-start.18 = (bf16[192,896]{1,0:T(8,128)(2,1)}, bf16[192,896]{1,0:T(8,128)(2,1)}, u32[]{:S(2)}, u32[]{:S(2)}) collective-permute-start(bf16[192,896]{1,0:T(8,128)(2,1)} %get-tuple-element.18), channel_id=1, source_target_pairs={{0,16},{1,17},{2,18},{3,19},{4,20},{5,21},{6,22},{7,23},{8,24},{9,... | collective-permute-start | bytes 1032200 | tf_op jit(solution)/shard_map/ppermute | solution.py:40
  190.6 4.0 %collective-permute-start.21 = (f32[2,80,640]{2,1,0:T(8,128)}, f32[2,80,640]{2,1,0:T(8,128)}, u32[]{:S(2)}, u32[]{:S(2)}) collective-permute-start(f32[2,80,640]{2,1,0:T(8,128)} %select_bitcast_fusion), channel_id=1, source_target_pairs={{0,8},{1,9},{2,10},{3,11},{4,12},{5,13},{6,14},{7,15},{8,0},{9,1},... | collective-permute-start | bytes 1228808 | tf_op jit(solution)/shard_map/ppermute | solution.py:40
  195.7 8.8 %collective-permute-start.22 = (f32[80,640]{1,0:T(8,128)S(1)}, f32[80,640]{1,0:T(8,128)S(1)}, u32[]{:S(2)}, u32[]{:S(2)}) collective-permute-start(f32[80,640]{1,0:T(8,128)S(1)} %select_bitcast_fusion.1), channel_id=1, source_target_pairs={{0,16},{1,17},{2,18},{3,19},{4,20},{5,21},{6,22},{7,23},{8,24},{9,... | collective-permute-start | bytes 614408 | tf_op jit(solution)/shard_map/ppermute | solution.py:40
  (12 other events, 137.8 us)

commit v2 on v1

--- a/solution.py
+++ b/solution.py
@@ -16,7 +16,7 @@
 ROWS = 192
 IN_BLOCK = 640
 OUT_BLOCK = 80
-EXTRA = 112
+EXTRA = 64
 
 perturb_scale = 0.5
 
@@ -175,16 +175,13 @@
     return held, swapped
 
 
-def spread_right(right_local, ranks, z):
-    chunks = right_local.reshape(32, 2, 320)
-    levels = jnp.zeros((16, 320), BF16).at[0, :M_DEV].set(ranks.astype(BF16))
+def spread_right(right_local, z):
     parity = z % 2
+    right = right_local.astype(BF16)
     parts = []
     for flip in range(2):
-        chunk = jnp.where(parity == flip, chunks[:, 0], chunks[:, 1])
-        high, low = split(chunk)
-        sent = jnp.concatenate([high, low, levels])
-        parts.append(move(sent, functools.partial(right_target, flip)))
+        chunk = jnp.where(parity == flip, right[:, :320], right[:, 320:])
+        parts.append(move(chunk, functools.partial(right_target, flip)))
     return jnp.concatenate(parts, 1)
 
 
@@ -198,68 +195,135 @@
     return near, above, far, below
 
 
-def scaled_right(blocks, z, y, xh, members):
-    extra = jnp.stack([b[2 * ROWS :].reshape(2, EXTRA, 2, 320) for b in blocks])
-    high, low, levels = extra[:, :, 32:64], extra[:, :, 64:96], extra[:, :, 96, :, :M_DEV]
-    right = (high.astype(F32) + low.astype(F32)).transpose(0, 1, 3, 2, 4)
-    levels = levels.astype(F32)
-    own = jnp.pad(levels.reshape(16, M_DEV), ((0, 0), (0, 120)))
-    core_side = move(own, core_target)
-    both = jnp.concatenate([own[:, :M_DEV], core_side[:, :M_DEV]], 1)
-    xl_side = move(jnp.pad(both, ((0, 0), (0, 112))), xl_target)
-    every = jnp.concatenate([both, xl_side[:, : 2 * M_DEV]], 1)
-    rank_mean = jnp.sum(every) / members
-    variance = jnp.sum((every - rank_mean) ** 2) / members
-    fitness = (levels - rank_mean) * lax.rsqrt(variance + 1e-05)
-    scaled = jnp.repeat(fitness, RANK, axis=3)[..., None] * right
-    scaled = jnp.where(xh == 0, scaled, scaled[:, ::-1])
-    scaled = jnp.where(z % 2 == 0, scaled, scaled[:, :, ::-1])
-    scaled = lax.dynamic_slice_in_dim(jnp.concatenate([scaled, scaled]), 4 - y, 4, 0)
-    scaled = scaled.transpose(1, 0, 2, 3, 4).reshape(16 * 32, 320)
-    return jnp.concatenate(split(scaled), 1)
-
-
-def update_block(left_all, scaled, xl, core, members):
-    product_t = lax.dot_general(
-        scaled, left_all, (((0,), (0,)), ((), ())), preferred_element_type=F32
-    )
-    product_t = (product_t[:320] + product_t[320:]).reshape(2, 2, OUT_BLOCK, IN_BLOCK)
-    keep = jnp.where(core == 0, product_t[:, 0], product_t[:, 1])
-    give = jnp.where(core == 0, product_t[:, 1], product_t[:, 0])
+def rank_rows(ranks):
+    own = jnp.pad(ranks.astype(F32)[None, :], ((0, 7), (0, 120)))
+    both = jnp.concatenate([own[:, :M_DEV], move(own, core_target)[:, :M_DEV]], 1)
+    both = jnp.pad(both, ((0, 0), (0, 112)))
+    every = jnp.concatenate([both[:, : 2 * M_DEV], move(both, xl_target)[:, : 2 * M_DEV]], 1)
+    return jnp.pad(every, ((0, 0), (0, IN_BLOCK - 4 * M_DEV)))
+
+
+def update_kernel(members, place, left, t0, t1, t2, t3, keep, give, right, high, low, total):
+    z, core, y, xh = place[0], place[1], place[3], place[4]
+    lanes = lax.broadcasted_iota(jnp.int32, (8, 128), 1)
+    rows = lax.broadcasted_iota(jnp.int32, (8, 128), 0)
+    valid = jnp.logical_and(rows == 0, lanes < 4 * M_DEV)
+    tiles = [left[i * 40 + 32 : i * 40 + 40, :128] for i in range(16)]
+    rank_sum = tiles[0]
+    for tile in tiles[1:]:
+        rank_sum = rank_sum + tile
+    rank_mean = jnp.sum(rank_sum) / members
+    spread = jnp.zeros((8, 128), F32)
+    for tile in tiles:
+        spread = spread + jnp.where(valid, (tile - rank_mean) ** 2, 0.0)
+    variance = jnp.full((8, 128), jnp.sum(spread) / members)
+    scale = lax.rsqrt(variance + 1e-05)[:1, :1] * math.sqrt(D / (members * RANK))
+
+    wide_lane = lax.broadcasted_iota(jnp.int32, (32, 128), 1)
+    wide_member = lax.broadcasted_iota(jnp.int32, (32, 128), 0) // RANK
+    for near, extra in enumerate((t0, t1, t2, t3)):
+        for m in range(2):
+            slot = (near * 2 + m) * 32
+            right[slot : slot + 32, :] = extra[m * EXTRA + 32 : m * EXTRA + 64, :]
+            pair = (xh ^ m) * 4 + lax.rem(y + near, 4)
+            for flip in range(2):
+                start = pl.multiple_of((2 * pair + (lax.rem(z, 2) ^ flip)) * 40, 8)
+                levels = left[pl.ds(start + 32, 8), :128][:1, :]
+                level = jnp.sum(
+                    jnp.where(wide_lane == wide_member, levels, 0.0), axis=1, keepdims=True
+                )
+                scaled = left[pl.ds(start, 32), :] * ((level - rank_mean) * scale)
+                part = scaled.astype(BF16)
+                high[flip, slot : slot + 32, :] = part
+                low[flip, slot : slot + 32, :] = (scaled - part.astype(F32)).astype(BF16)
+
+    def tn_dot(a, b):
+        return lax.dot_general(a, b, (((0,), (0,)), ((), ())), preferred_element_type=F32)
+
+    first, second = right[:, :384], right[:, 256:]
+    total[...] = (tn_dot(first, high[0]) + tn_dot(first, low[0]))[:320]
+    total[...] += (tn_dot(second, high[1]) + tn_dot(second, low[1]))[64:]
+    for i in range(2):
+        here = pl.ds(pl.multiple_of((2 * i + core) * OUT_BLOCK, 8), OUT_BLOCK)
+        there = pl.ds(pl.multiple_of((2 * i + 1 - core) * OUT_BLOCK, 8), OUT_BLOCK)
+        keep[i] = total[here, :]
+        give[i] = total[there, :]
+
+
+def update_block(place, left_all, blocks, xl, members):
+    vmem = pl.BlockSpec(memory_space=pltpu.VMEM)
+    extra = pl.BlockSpec((2 * EXTRA, IN_BLOCK), lambda i: (2 * ROWS // (2 * EXTRA), 0))
+    shape = jax.ShapeDtypeStruct((2, OUT_BLOCK, IN_BLOCK), F32)
+    keep, give = pl.pallas_call(
+        functools.partial(update_kernel, members),
+        out_shape=(shape, shape),
+        grid=(1,),
+        in_specs=[pl.BlockSpec(memory_space=pltpu.SMEM), vmem] + [extra] * 4,
+        out_specs=(vmem, vmem),
+        scratch_shapes=[
+            pltpu.VMEM((256, IN_BLOCK), BF16),
+            pltpu.VMEM((2, 256, IN_BLOCK), BF16),
+            pltpu.VMEM((2, 256, IN_BLOCK), BF16),
+            pltpu.VMEM((320, IN_BLOCK), F32),
+        ],
+        compiler_params=pltpu.CompilerParams(vmem_limit_bytes=32 * 2**20),
+        cost_estimate=pl.CostEstimate(
+            flops=8 * 384 * 256 * 640, bytes_accessed=4 * 2**20, transcendentals=0
+        ),
+    )(place, left_all, *blocks)
     keep = keep + move(give, core_target)
     give = jnp.where(xl == 0, keep[1], keep[0])
     keep = jnp.where(xl == 0, keep[0], keep[1])
-    total = keep + move(give, xl_target)
-    return (math.sqrt(D / (members * RANK)) * total).T
+    return (keep + move(give, xl_target)).T
+
+
+def output_kernel(scale, mine, mine_proj, got, right, member, out):
+    proj = mine_proj[...]
+    proj += got[:, IN_BLOCK : IN_BLOCK + 32].astype(F32)
+    proj += got[:, IN_BLOCK + 128 : IN_BLOCK + 160].astype(F32)
+    factor = lax.broadcasted_iota(jnp.int32, (ROWS, 32), 1) // RANK
+    coefficient = jnp.where(member[...] == factor, proj, 0.0) * scale
+    low_rank = jnp.dot(
+        coefficient, right[...], precision=lax.Precision.HIGHEST, preferred_element_type=F32
+    )
+    out[...] = mine[...] + got[:, :IN_BLOCK].astype(F32) + low_rank
+
+
+def output_block(mine, mine_proj, got, right_local, member_of):
+    vmem = pl.BlockSpec(memory_space=pltpu.VMEM)
+    return pl.pallas_call(
+        functools.partial(output_kernel, perturb_scale / math.sqrt(RANK)),
+        out_shape=jax.ShapeDtypeStruct((ROWS, IN_BLOCK), F32),
+        in_specs=[vmem] * 5,
+        out_specs=vmem,
+        cost_estimate=pl.CostEstimate(
+            flops=12 * ROWS * 32 * IN_BLOCK, bytes_accessed=2 * 2**20, transcendentals=0
+        ),
+    )(mine, mine_proj, got, right_local, member_of.reshape(ROWS, 1))
 
 
 def on_device(tokens, base_weight, left_factors, right_factors, member_of, ranks):
     z, xl, core, y, xh = (lax.axis_index(name) for name in AXES)
     members = M_DEV * 64
-    left = left_factors.astype(BF16).reshape(32, IN_BLOCK)
-    left_all = lax.all_gather(left, "z", axis=0, tiled=True)
+    left = left_factors.reshape(32, IN_BLOCK)
+    left_all = lax.all_gather(
+        jnp.concatenate([left, rank_rows(ranks)]), "z", axis=0, tiled=True
+    )
 
     offset = (y * 2 + xh) * IN_BLOCK
     right_local = lax.dynamic_slice_in_dim(right_factors, offset, IN_BLOCK, 2).reshape(32, IN_BLOCK)
     whole = spread_weights(base_weight, z, core)
-    right = spread_right(right_local, ranks, z)
+    right = spread_right(right_local, z)
     held, swapped = ring(whole, core)
-    blocks = spread_rows(jnp.concatenate([tokens, left, right]), core)
-
-    place = jnp.stack([z, core, xl ^ xh]).astype(jnp.int32)
+    blocks = spread_rows(jnp.concatenate([tokens, left.astype(BF16), right]), core)
+
+    place = jnp.stack([z, core, xl ^ xh, y, xh]).astype(jnp.int32)
     mine, mine_proj, give = product(
         place, whole, *held[:3], *swapped[:3], held[3], swapped[3], *blocks
     )
-    got = move(give, xl_target).astype(F32)
-    proj = mine_proj + got[:, IN_BLOCK : IN_BLOCK + 32] + got[:, IN_BLOCK + 128 : IN_BLOCK + 160]
-    factor = jnp.arange(32, dtype=jnp.int32) // RANK
-    mask = member_of[0][:, None] == factor[None, :]
-    coefficient = jnp.where(mask, proj, 0.0) * (perturb_scale / math.sqrt(RANK))
-    low_rank = jnp.dot(coefficient, right_local, precision=lax.Precision.HIGHEST)
-    outputs = mine + got[:, :IN_BLOCK] + low_rank
-
-    scaled = scaled_right(blocks, z, y, xh, members)
-    update = update_block(left_all, scaled, xl, core, members)
+    got = move(give, xl_target)
+    outputs = output_block(mine, mine_proj, got, right_local, member_of)
+    update = update_block(place, left_all, blocks, xl, members)
     return (outputs, update)
 
 

time: 207 us -> 162 us (0.78)
  blocking collectives: 28 us -> 0 us
  local copies, waits for them, and re-layouts: 24.9 us -> 6.66 us
  other arithmetic: 18.8 us -> 7.3 us
  between operations: 3.97 us -> 14.6 us
  Pallas kernels: 5.44 us -> 10.5 us
  starting transfers between devices: 106 us -> 101 us
  waiting for transfers between devices: 17 us -> 20.4 us
    all_gather x1 -> x0, blocking collectives: 28 us -> none  [on_device(): left_all = lax.all_gather(left, 'z', axis=0, tiled=True)]
    another operation x6 -> x1, local copies, waits for them, and re-layouts: 10 us -> 0.09 us  [on_device(): place = jnp.stack([z, core, xl ^ xh, y, xh]).astype(jnp.int32)]
    pallas_call x0 -> x2, Pallas kernels: none -> 5.25 us  [the longest x1 2.65 us: update_block(): pl.pallas_call(functools.partial(update_kernel, members), out_shape=(shap...]
    ppermute x23, starting transfers between devices: 106 us -> 101 us  [move(): lax.ppermute(value, AXES, [(flat(p), flat(target(*p))) for p in places])]
    unnamed x29 -> x24, local copies, waits for them, and re-layouts: 9.09 us -> 4.74 us
    ppermute x23, waiting for transfers between devices: 17 us -> 20.4 us  [move(): lax.ppermute(value, AXES, [(flat(p), flat(target(*p))) for p in places])]
    slice x4 -> x1, local copies, waits for them, and re-layouts: 3.25 us -> 0.01 us  [rank_rows(): own[:, :M_DEV]]
    reduce_sum x4 -> x0, other arithmetic: 3.2 us -> none  [the longest x3 2.52 us: scaled_right(): rank_mean = jnp.sum(every) / members]
  transfers between devices with their start and end apart: 23 -> 24, of which waited for: 5 -> 9; matrix products, arithmetic and copies ran while one was open for 19% -> 4% of each run, Pallas kernels for 3% -> 7%
where the time goes in v2:
time: 162 us; the launch traced here: 161 us
  starting transfers between devices  101 us (62%)
  waiting for transfers between devices  20.4 us (13%)
  between operations  14.6 us (9%)
  Pallas kernels  10.5 us (6%)
  other arithmetic  7.3 us (5%)
  local copies, waits for them, and re-layouts  6.66 us (4%)
    ppermute x23, starting transfers between devices, move(): lax.ppermute(value, AXES, [(flat(p), flat(target(*p))) for p in places])  101 us
    ppermute x23, waiting for transfers between devices, move(): lax.ppermute(value, AXES, [(flat(p), flat(target(*p))) for p in places])  20.4 us
    pallas_call x1, Pallas kernels, product(): pl.pallas_call(product_kernel, out_shape=(jax.ShapeDtypeStruct((ROWS, IN_...  5.28 us
    unnamed x24, local copies, waits for them, and re-layouts  4.74 us
  transfers between devices with their start and end apart: 24, of which 9 were waited for; matrix products, arithmetic and copies ran while one was open for 4% of the time, Pallas kernels for 7%

profile of v2, /device:TPU:1, one launch (start us, length us, event | category | flops | bytes accessed | tf_op | source)
XLA Modules:
  0.0 160.5 jit_solution(4841299433612966901)
XLA Ops:
  8.0 8.8 %collective-permute-start.19 = (f32[8,128]{1,0:T(8,128)S(1)}, f32[8,128]{1,0:T(8,128)S(1)}, u32[]{:S(2)}, u32[]{:S(2)}) collective-permute-start(f32[8,128]{1,0:T(8,128)S(1)} %pad.12), channel_id=1, source_target_pairs={{0,8},{1,9},{2,10},{3,11},{4,12},{5,13},{6,14},{7,15},{8,0},{9,1},... | collective-permute-start | bytes 12296 | tf_op jit(solution)/shard_map/ppermute | solution.py:40
  23.7 11.0 %collective-permute-start.1 = (bf16[80,640]{1,0:T(8,128)(2,1)S(1)}, bf16[80,640]{1,0:T(8,128)(2,1)S(1)}, u32[]{:S(2)}, u32[]{:S(2)}) collective-permute-start(bf16[80,640]{1,0:T(8,128)(2,1)S(1)} %convert_bitcast_fusion), channel_id=1, source_target_pairs={{0,256},{1,272},{2,264},{3,280},{4,0},{5,16},{6,8},{7,24},{8,288},... | collective-permute-start | bytes 307208 | tf_op jit(solution)/shard_map/ppermute | solution.py:40
  36.8 1.9 %collective-permute-start.12 = (bf16[32,320]{1,0:T(8,128)(2,1)S(1)}, bf16[32,320]{1,0:T(8,128)(2,1)S(1)}, u32[]{:S(2)}, u32[]{:S(2)}) collective-permute-start(bf16[32,320]{1,0:T(8,128)(2,1)S(1)} %get-tuple-element.13), channel_id=1, source_target_pairs={{0,32},{1,96},{2,160},{3,224},{4,288},{5,352},{6,416},{7,480},{8,4... | collective-permute-start | bytes 61448 | tf_op jit(solution)/shard_map/ppermute | solution.py:40
  39.4 2.3 %collective-permute-done = bf16[80,640]{1,0:T(8,128)(2,1)S(1)} collective-permute-done((bf16[80,640]{1,0:T(8,128)(2,1)S(1)}, bf16[80,640]{1,0:T(8,128)(2,1)S(1)}, u32[]{:S(2)}, u32[]{:S(2)}) %collective-permute-start) | collective-permute-done | bytes 102432 | tf_op jit(solution)/shard_map/ppermute | solution.py:40
  41.7 1.9 %collective-permute-start.2 = (bf16[2,80,640]{2,1,0:T(8,128)(2,1)S(1)}, bf16[2,80,640]{2,1,0:T(8,128)(2,1)S(1)}, u32[]{:S(2)}, u32[]{:S(2)}) collective-permute-start(bf16[2,80,640]{2,1,0:T(8,128)(2,1)S(1)} %maximum_select_fusion.2), channel_id=1, source_target_pairs={{0,8},{1,9},{2,10},{3,11},{4,12},{5,13},{6,14},{7,15},{8,0},{9,1},... | collective-permute-start | bytes 614408 | tf_op jit(solution)/shard_map/ppermute | solution.py:40
  44.2 10.1 %collective-permute-start.14 = (bf16[256,640]{1,0:T(8,128)(2,1)S(1)}, bf16[256,640]{1,0:T(8,128)(2,1)S(1)}, u32[]{:S(2)}, u32[]{:S(2)}) collective-permute-start(bf16[256,640]{1,0:T(8,128)(2,1)S(1)} %maximum_maximum_fusion), channel_id=1, source_target_pairs={{0,1},{1,17},{2,3},{3,19},{4,5},{5,21},{6,7},{7,23},{8,9},{9,25},{... | collective-permute-start | bytes 983048 | tf_op jit(solution)/shard_map/ppermute | solution.py:40
  55.2 17.0 %collective-permute-start.3 = (bf16[320,640]{1,0:T(8,128)(2,1)S(1)}, bf16[320,640]{1,0:T(8,128)(2,1)}, u32[]{:S(2)}, u32[]{:S(2)}) collective-permute-start(bf16[320,640]{1,0:T(8,128)(2,1)S(1)} %bitcast.26), channel_id=1, source_target_pairs={{0,32},{1,33},{2,34},{3,35},{4,36},{5,37},{6,38},{7,39},{8,488},{9... | collective-permute-start | bytes 1228808 | tf_op jit(solution)/shard_map/ppermute | solution.py:40
  72.4 2.1 %collective-permute-start.15 = (bf16[512,640]{1,0:T(8,128)(2,1)S(1)}, bf16[512,640]{1,0:T(8,128)(2,1)S(1)}, u32[]{:S(2)}, u32[]{:S(2)}) collective-permute-start(bf16[512,640]{1,0:T(8,128)(2,1)S(1)} %pad_maximum_fusion.t0), channel_id=1, source_target_pairs={{0,6},{1,7},{2,0},{3,1},{4,2},{5,3},{6,4},{7,5},{8,14},{9,15},{10,... | collective-permute-start | bytes 1966088 | tf_op jit(solution)/shard_map/ppermute | solution.py:40
  74.5 3.2 %collective-permute-start.16 = (bf16[512,640]{1,0:T(8,128)(2,1)S(1)}, bf16[512,640]{1,0:T(8,128)(2,1)S(1)}, u32[]{:S(2)}, u32[]{:S(2)}) collective-permute-start(bf16[512,640]{1,0:T(8,128)(2,1)S(1)} %pad_maximum_fusion.t0), channel_id=1, source_target_pairs={{0,2},{1,3},{2,4},{3,5},{4,6},{5,7},{6,0},{7,1},{8,10},{9,11},{10,... | collective-permute-start | bytes 1966088 | tf_op jit(solution)/shard_map/ppermute | solution.py:40
  79.4 5.3 %collective-permute-start.4 = (bf16[320,640]{1,0:T(8,128)(2,1)}, bf16[320,640]{1,0:T(8,128)(2,1)}, u32[]{:S(2)}, u32[]{:S(2)}) collective-permute-start(bf16[320,640]{1,0:T(8,128)(2,1)} %collective-permute-done.3.r1), channel_id=1, source_target_pairs={{0,32},{1,33},{2,34},{3,35},{4,36},{5,37},{6,38},{7,39},{8,488},{9... | collective-permute-start | bytes 1228808 | tf_op jit(solution)/shard_map/ppermute | solution.py:40
  84.7 6.4 %collective-permute-done.4.r2 = bf16[320,640]{1,0:T(8,128)(2,1)} collective-permute-done((bf16[320,640]{1,0:T(8,128)(2,1)}, bf16[320,640]{1,0:T(8,128)(2,1)}, u32[]{:S(2)}, u32[]{:S(2)}) %collective-permute-start.4) | collective-permute-done | bytes 409632 | tf_op jit(solution)/shard_map/ppermute | solution.py:40
  91.1 5.3 %collective-permute-start.5 = (bf16[320,640]{1,0:T(8,128)(2,1)}, bf16[320,640]{1,0:T(8,128)(2,1)}, u32[]{:S(2)}, u32[]{:S(2)}) collective-permute-start(bf16[320,640]{1,0:T(8,128)(2,1)} %collective-permute-done.4.r2), channel_id=1, source_target_pairs={{0,32},{1,33},{2,34},{3,35},{4,36},{5,37},{6,38},{7,39},{8,488},{9... | collective-permute-start | bytes 1228808 | tf_op jit(solution)/shard_map/ppermute | solution.py:40
  97.4 3.5 %collective-permute-start.17 = (bf16[512,640]{1,0:T(8,128)(2,1)}, bf16[512,640]{1,0:T(8,128)(2,1)S(1)}, u32[]{:S(2)}, u32[]{:S(2)}) collective-permute-start(bf16[512,640]{1,0:T(8,128)(2,1)} %broadcast_select_fusion), channel_id=1, source_target_pairs={{0,2},{1,3},{2,4},{3,5},{4,6},{5,7},{6,0},{7,1},{8,14},{9,15},{10,... | collective-permute-start | bytes 1966088 | tf_op jit(solution)/shard_map/ppermute | solution.py:40
  100.8 1.9 %collective-permute-start.6 = (bf16[320,640]{1,0:T(8,128)(2,1)}, bf16[320,640]{1,0:T(8,128)(2,1)}, u32[]{:S(2)}, u32[]{:S(2)}) collective-permute-start(bf16[320,640]{1,0:T(8,128)(2,1)} %collective-permute-done.3.r1), channel_id=1, source_target_pairs={{0,8},{1,9},{2,10},{3,11},{4,12},{5,13},{6,14},{7,15},{8,0},{9,1},... | collective-permute-start | bytes 1228808 | tf_op jit(solution)/shard_map/ppermute | solution.py:40
  102.8 2.4 %collective-permute-start.7 = (bf16[320,640]{1,0:T(8,128)(2,1)}, bf16[320,640]{1,0:T(8,128)(2,1)}, u32[]{:S(2)}, u32[]{:S(2)}) collective-permute-start(bf16[320,640]{1,0:T(8,128)(2,1)} %collective-permute-done.4.r2), channel_id=1, source_target_pairs={{0,8},{1,9},{2,10},{3,11},{4,12},{5,13},{6,14},{7,15},{8,0},{9,1},... | collective-permute-start | bytes 1228808 | tf_op jit(solution)/shard_map/ppermute | solution.py:40
  106.9 2.8 %collective-permute-start.9 = (bf16[160,640]{1,0:T(8,128)(2,1)}, bf16[160,640]{1,0:T(8,128)(2,1)S(1)}, u32[]{:S(2)}, u32[]{:S(2)}) collective-permute-start(bf16[160,640]{1,0:T(8,128)(2,1)} %slice_select_fusion), channel_id=1, source_target_pairs={{0,32},{1,33},{2,34},{3,35},{4,36},{5,37},{6,38},{7,39},{8,488},{9... | collective-permute-start | bytes 614408 | tf_op jit(solution)/shard_map/ppermute | solution.py:40
  109.8 1.9 %collective-permute-start.8 = (bf16[320,640]{1,0:T(8,128)(2,1)}, bf16[320,640]{1,0:T(8,128)(2,1)}, u32[]{:S(2)}, u32[]{:S(2)}) collective-permute-start(bf16[320,640]{1,0:T(8,128)(2,1)} %collective-permute-done.5.r3), channel_id=1, source_target_pairs={{0,8},{1,9},{2,10},{3,11},{4,12},{5,13},{6,14},{7,15},{8,0},{9,1},... | collective-permute-start | bytes 1228808 | tf_op jit(solution)/shard_map/ppermute | solution.py:40
  113.3 2.7 %shard_map.79 = (f32[2,80,640]{2,1,0:T(8,128)S(1)}, f32[2,80,640]{2,1,0:T(8,128)}) custom-call(s32[5]{0:T(128)S(1)} %stack.57.place, f32[640,640]{1,0:T(8,128)S(1)} %copy-done.3, bf16[512,640]{1,0:T(8,128)(2,1)S(1)} %pad_maximum_fusion.t0, bf16[512,640]{1,0:T(8,128)(2,1)S(1)} %collective-permute-done.15.t1, bf16[512,640]{1,0:T(8,128)(2,1)S(1)} %collective-permute-done.17.t2, ...), custom_call_target="tpu_custom_call" | custom-call | flops 503316480 | bytes 4194304 | tf_op jit(solution)/shard_map/pallas_call | solution.py:257
  116.6 2.4 %collective-permute-start.21 = (f32[2,80,640]{2,1,0:T(8,128)}, f32[2,80,640]{2,1,0:T(8,128)}, u32[]{:S(2)}, u32[]{:S(2)}) collective-permute-start(f32[2,80,640]{2,1,0:T(8,128)} %get-tuple-element.11), channel_id=1, source_target_pairs={{0,8},{1,9},{2,10},{3,11},{4,12},{5,13},{6,14},{7,15},{8,0},{9,1},... | collective-permute-start | bytes 1228808 | tf_op jit(solution)/shard_map/ppermute | solution.py:40
  119.1 1.9 %collective-permute-start.10 = (bf16[160,640]{1,0:T(8,128)(2,1)S(1)}, bf16[160,640]{1,0:T(8,128)(2,1)}, u32[]{:S(2)}, u32[]{:S(2)}) collective-permute-start(bf16[160,640]{1,0:T(8,128)(2,1)S(1)} %collective-permute-done.9.r4), channel_id=1, source_target_pairs={{0,8},{1,9},{2,10},{3,11},{4,12},{5,13},{6,14},{7,15},{8,0},{9,1},... | collective-permute-start | bytes 614408 | tf_op jit(solution)/shard_map/ppermute | solution.py:40
  123.5 5.3 %shard_map.77 = (f32[192,640]{1,0:T(8,128)S(1)}, f32[192,32]{1,0:T(8,128)S(1)}, bf16[192,896]{1,0:T(8,128)(2,1)}) custom-call(s32[5]{0:T(128)S(1)} %stack.57.place, bf16[320,640]{1,0:T(8,128)(2,1)S(1)} %bitcast.27, bf16[320,640]{1,0:T(8,128)(2,1)} %collective-permute-done.3.r1, bf16[320,640]{1,0:T(8,128)(2,1)} %collective-permute-done.4.r2, ...), custom_call_target="tpu_custom_call" | custom-call | flops 1258291200 | bytes 8388608 | tf_op jit(solution)/shard_map/pallas_call | solution.py:134
  129.6 10.4 %collective-permute-start.18 = (bf16[192,896]{1,0:T(8,128)(2,1)}, bf16[192,896]{1,0:T(8,128)(2,1)S(1)}, u32[]{:S(2)}, u32[]{:S(2)}) collective-permute-start(bf16[192,896]{1,0:T(8,128)(2,1)} %get-tuple-element.9), channel_id=1, source_target_pairs={{0,16},{1,17},{2,18},{3,19},{4,20},{5,21},{6,22},{7,23},{8,24},{9,... | collective-permute-start | bytes 1032200 | tf_op jit(solution)/shard_map/ppermute | solution.py:40
  143.9 4.7 %collective-permute-done.18.got = bf16[192,896]{1,0:T(8,128)(2,1)S(1)} collective-permute-done((bf16[192,896]{1,0:T(8,128)(2,1)}, bf16[192,896]{1,0:T(8,128)(2,1)S(1)}, u32[]{:S(2)}, u32[]{:S(2)}) %collective-permute-start.18) | collective-permute-done | bytes 344096 | tf_op jit(solution)/shard_map/ppermute | solution.py:40
  149.3 2.6 %shard_map.78 = f32[192,640]{1,0:T(8,128)} custom-call(f32[192,640]{1,0:T(8,128)} %copy-done.4, f32[192,32]{1,0:T(8,128)} %copy-done.7, bf16[192,896]{1,0:T(8,128)(2,1)} %copy-done.9, f32[32,640]{1,0:T(8,128)} %copy-done.8, s32[192,1]{1,0:T(8,128)} %copy.10.member), custom_call_target="tpu_custom_call" | custom-call | flops 47185920 | bytes 2097152 | tf_op jit(solution)/shard_map/pallas_call | solution.py:294
  (82 shorter events, 28.2 us)
Async XLA Ops:
  7.2 104.6 %all-gather.2.cloned.1.call-start = ((), (), s32[]{:S(2)}) async-start(), calls=%async_computation | async-start | bytes 1740800 | tf_op jit(solution)/shard_map/all_gather | solution.py:309
  8.0 9.6 %collective-permute-start.19 = (f32[8,128]{1,0:T(8,128)S(1)}, f32[8,128]{1,0:T(8,128)S(1)}, u32[]{:S(2)}, u32[]{:S(2)}) collective-permute-start(f32[8,128]{1,0:T(8,128)S(1)} %pad.12), channel_id=1, source_target_pairs={{0,8},{1,9},{2,10},{3,11},{4,12},{5,13},{6,14},{7,15},{8,0},{9,1},... | collective-permute-start | bytes 12296 | tf_op jit(solution)/shard_map/ppermute | solution.py:40
  17.6 4.3 %collective-permute-start.20 = (f32[8,128]{1,0:T(8,128)S(1)}, f32[8,128]{1,0:T(8,128)S(1)}, u32[]{:S(2)}, u32[]{:S(2)}) collective-permute-start(f32[8,128]{1,0:T(8,128)S(1)} %select_maximum_fusion.2), channel_id=1, source_target_pairs={{0,16},{1,17},{2,18},{3,19},{4,20},{5,21},{6,22},{7,23},{8,24},{9,... | collective-permute-start | bytes 12296 | tf_op jit(solution)/shard_map/ppermute | solution.py:40
  23.7 15.8 %collective-permute-start.1 = (bf16[80,640]{1,0:T(8,128)(2,1)S(1)}, bf16[80,640]{1,0:T(8,128)(2,1)S(1)}, u32[]{:S(2)}, u32[]{:S(2)}) collective-permute-start(bf16[80,640]{1,0:T(8,128)(2,1)S(1)} %convert_bitcast_fusion), channel_id=1, source_target_pairs={{0,256},{1,272},{2,264},{3,280},{4,0},{5,16},{6,8},{7,24},{8,288},... | collective-permute-start | bytes 307208 | tf_op jit(solution)/shard_map/ppermute | solution.py:40
  34.7 7.0 %collective-permute-start = (bf16[80,640]{1,0:T(8,128)(2,1)S(1)}, bf16[80,640]{1,0:T(8,128)(2,1)S(1)}, u32[]{:S(2)}, u32[]{:S(2)}) collective-permute-start(bf16[80,640]{1,0:T(8,128)(2,1)S(1)} %convert_bitcast_fusion), channel_id=1, source_target_pairs={{0,0},{1,16},{2,8},{3,24},{4,256},{5,272},{6,264},{7,280},{8,32},{... | collective-permute-start | bytes 307208 | tf_op jit(solution)/shard_map/ppermute | solution.py:40
  36.8 7.3 %collective-permute-start.12 = (bf16[32,320]{1,0:T(8,128)(2,1)S(1)}, bf16[32,320]{1,0:T(8,128)(2,1)S(1)}, u32[]{:S(2)}, u32[]{:S(2)}) collective-permute-start(bf16[32,320]{1,0:T(8,128)(2,1)S(1)} %get-tuple-element.13), channel_id=1, source_target_pairs={{0,32},{1,96},{2,160},{3,224},{4,288},{5,352},{6,416},{7,480},{8,4... | collective-permute-start | bytes 61448 | tf_op jit(solution)/shard_map/ppermute | solution.py:40
  38.7 5.4 %collective-permute-start.11 = (bf16[32,320]{1,0:T(8,128)(2,1)S(1)}, bf16[32,320]{1,0:T(8,128)(2,1)S(1)}, u32[]{:S(2)}, u32[]{:S(2)}) collective-permute-start(bf16[32,320]{1,0:T(8,128)(2,1)S(1)} %get-tuple-element.12), channel_id=1, source_target_pairs={{0,0},{1,64},{2,128},{3,192},{4,256},{5,320},{6,384},{7,448},{8,8}... | collective-permute-start | bytes 61448 | tf_op jit(solution)/shard_map/ppermute | solution.py:40
  41.7 13.3 %collective-permute-start.2 = (bf16[2,80,640]{2,1,0:T(8,128)(2,1)S(1)}, bf16[2,80,640]{2,1,0:T(8,128)(2,1)S(1)}, u32[]{:S(2)}, u32[]{:S(2)}) collective-permute-start(bf16[2,80,640]{2,1,0:T(8,128)(2,1)S(1)} %maximum_select_fusion.2), channel_id=1, source_target_pairs={{0,8},{1,9},{2,10},{3,11},{4,12},{5,13},{6,14},{7,15},{8,0},{9,1},... | collective-permute-start | bytes 614408 | tf_op jit(solution)/shard_map/ppermute | solution.py:40
  44.2 28.0 %collective-permute-start.14 = (bf16[256,640]{1,0:T(8,128)(2,1)S(1)}, bf16[256,640]{1,0:T(8,128)(2,1)S(1)}, u32[]{:S(2)}, u32[]{:S(2)}) collective-permute-start(bf16[256,640]{1,0:T(8,128)(2,1)S(1)} %maximum_maximum_fusion), channel_id=1, source_target_pairs={{0,1},{1,17},{2,3},{3,19},{4,5},{5,21},{6,7},{7,23},{8,9},{9,25},{... | collective-permute-start | bytes 983048 | tf_op jit(solution)/shard_map/ppermute | solution.py:40
  54.3 17.9 %collective-permute-start.13 = (bf16[256,640]{1,0:T(8,128)(2,1)S(1)}, bf16[256,640]{1,0:T(8,128)(2,1)S(1)}, u32[]{:S(2)}, u32[]{:S(2)}) collective-permute-start(bf16[256,640]{1,0:T(8,128)(2,1)S(1)} %maximum_maximum_fusion), channel_id=1, source_target_pairs={{0,0},{1,16},{2,2},{3,18},{4,4},{5,20},{6,6},{7,22},{8,8},{9,24},{... | collective-permute-start | bytes 983048 | tf_op jit(solution)/shard_map/ppermute | solution.py:40
  55.2 24.2 %collective-permute-start.3 = (bf16[320,640]{1,0:T(8,128)(2,1)S(1)}, bf16[320,640]{1,0:T(8,128)(2,1)}, u32[]{:S(2)}, u32[]{:S(2)}) collective-permute-start(bf16[320,640]{1,0:T(8,128)(2,1)S(1)} %bitcast.26), channel_id=1, source_target_pairs={{0,32},{1,33},{2,34},{3,35},{4,36},{5,37},{6,38},{7,39},{8,488},{9... | collective-permute-start | bytes 1228808 | tf_op jit(solution)/shard_map/ppermute | solution.py:40
  72.4 24.0 %collective-permute-start.15 = (bf16[512,640]{1,0:T(8,128)(2,1)S(1)}, bf16[512,640]{1,0:T(8,128)(2,1)S(1)}, u32[]{:S(2)}, u32[]{:S(2)}) collective-permute-start(bf16[512,640]{1,0:T(8,128)(2,1)S(1)} %pad_maximum_fusion.t0), channel_id=1, source_target_pairs={{0,6},{1,7},{2,0},{3,1},{4,2},{5,3},{6,4},{7,5},{8,14},{9,15},{10,... | collective-permute-start | bytes 1966088 | tf_op jit(solution)/shard_map/ppermute | solution.py:40
  74.5 22.0 %collective-permute-start.16 = (bf16[512,640]{1,0:T(8,128)(2,1)S(1)}, bf16[512,640]{1,0:T(8,128)(2,1)S(1)}, u32[]{:S(2)}, u32[]{:S(2)}) collective-permute-start(bf16[512,640]{1,0:T(8,128)(2,1)S(1)} %pad_maximum_fusion.t0), channel_id=1, source_target_pairs={{0,2},{1,3},{2,4},{3,5},{4,6},{5,7},{6,0},{7,1},{8,10},{9,11},{10,... | collective-permute-start | bytes 1966088 | tf_op jit(solution)/shard_map/ppermute | solution.py:40
  79.4 11.7 %collective-permute-start.4 = (bf16[320,640]{1,0:T(8,128)(2,1)}, bf16[320,640]{1,0:T(8,128)(2,1)}, u32[]{:S(2)}, u32[]{:S(2)}) collective-permute-start(bf16[320,640]{1,0:T(8,128)(2,1)} %collective-permute-done.3.r1), channel_id=1, source_target_pairs={{0,32},{1,33},{2,34},{3,35},{4,36},{5,37},{6,38},{7,39},{8,488},{9... | collective-permute-start | bytes 1228808 | tf_op jit(solution)/shard_map/ppermute | solution.py:40
  91.1 14.1 %collective-permute-start.5 = (bf16[320,640]{1,0:T(8,128)(2,1)}, bf16[320,640]{1,0:T(8,128)(2,1)}, u32[]{:S(2)}, u32[]{:S(2)}) collective-permute-start(bf16[320,640]{1,0:T(8,128)(2,1)} %collective-permute-done.4.r2), channel_id=1, source_target_pairs={{0,32},{1,33},{2,34},{3,35},{4,36},{5,37},{6,38},{7,39},{8,488},{9... | collective-permute-start | bytes 1228808 | tf_op jit(solution)/shard_map/ppermute | solution.py:40
  97.4 14.5 %collective-permute-start.17 = (bf16[512,640]{1,0:T(8,128)(2,1)}, bf16[512,640]{1,0:T(8,128)(2,1)S(1)}, u32[]{:S(2)}, u32[]{:S(2)}) collective-permute-start(bf16[512,640]{1,0:T(8,128)(2,1)} %broadcast_select_fusion), channel_id=1, source_target_pairs={{0,2},{1,3},{2,4},{3,5},{4,6},{5,7},{6,0},{7,1},{8,14},{9,15},{10,... | collective-permute-start | bytes 1966088 | tf_op jit(solution)/shard_map/ppermute | solution.py:40
  100.8 20.2 %collective-permute-start.6 = (bf16[320,640]{1,0:T(8,128)(2,1)}, bf16[320,640]{1,0:T(8,128)(2,1)}, u32[]{:S(2)}, u32[]{:S(2)}) collective-permute-start(bf16[320,640]{1,0:T(8,128)(2,1)} %collective-permute-done.3.r1), channel_id=1, source_target_pairs={{0,8},{1,9},{2,10},{3,11},{4,12},{5,13},{6,14},{7,15},{8,0},{9,1},... | collective-permute-start | bytes 1228808 | tf_op jit(solution)/shard_map/ppermute | solution.py:40
  102.8 18.2 %collective-permute-start.7 = (bf16[320,640]{1,0:T(8,128)(2,1)}, bf16[320,640]{1,0:T(8,128)(2,1)}, u32[]{:S(2)}, u32[]{:S(2)}) collective-permute-start(bf16[320,640]{1,0:T(8,128)(2,1)} %collective-permute-done.4.r2), channel_id=1, source_target_pairs={{0,8},{1,9},{2,10},{3,11},{4,12},{5,13},{6,14},{7,15},{8,0},{9,1},... | collective-permute-start | bytes 1228808 | tf_op jit(solution)/shard_map/ppermute | solution.py:40
  106.9 12.1 %collective-permute-start.9 = (bf16[160,640]{1,0:T(8,128)(2,1)}, bf16[160,640]{1,0:T(8,128)(2,1)S(1)}, u32[]{:S(2)}, u32[]{:S(2)}) collective-permute-start(bf16[160,640]{1,0:T(8,128)(2,1)} %slice_select_fusion), channel_id=1, source_target_pairs={{0,32},{1,33},{2,34},{3,35},{4,36},{5,37},{6,38},{7,39},{8,488},{9... | collective-permute-start | bytes 614408 | tf_op jit(solution)/shard_map/ppermute | solution.py:40
  109.8 11.2 %collective-permute-start.8 = (bf16[320,640]{1,0:T(8,128)(2,1)}, bf16[320,640]{1,0:T(8,128)(2,1)}, u32[]{:S(2)}, u32[]{:S(2)}) collective-permute-start(bf16[320,640]{1,0:T(8,128)(2,1)} %collective-permute-done.5.r3), channel_id=1, source_target_pairs={{0,8},{1,9},{2,10},{3,11},{4,12},{5,13},{6,14},{7,15},{8,0},{9,1},... | collective-permute-start | bytes 1228808 | tf_op jit(solution)/shard_map/ppermute | solution.py:40
  116.6 23.4 %collective-permute-start.21 = (f32[2,80,640]{2,1,0:T(8,128)}, f32[2,80,640]{2,1,0:T(8,128)}, u32[]{:S(2)}, u32[]{:S(2)}) collective-permute-start(f32[2,80,640]{2,1,0:T(8,128)} %get-tuple-element.11), channel_id=1, source_target_pairs={{0,8},{1,9},{2,10},{3,11},{4,12},{5,13},{6,14},{7,15},{8,0},{9,1},... | collective-permute-start | bytes 1228808 | tf_op jit(solution)/shard_map/ppermute | solution.py:40
  119.1 3.5 %collective-permute-start.10 = (bf16[160,640]{1,0:T(8,128)(2,1)S(1)}, bf16[160,640]{1,0:T(8,128)(2,1)}, u32[]{:S(2)}, u32[]{:S(2)}) collective-permute-start(bf16[160,640]{1,0:T(8,128)(2,1)S(1)} %collective-permute-done.9.r4), channel_id=1, source_target_pairs={{0,8},{1,9},{2,10},{3,11},{4,12},{5,13},{6,14},{7,15},{8,0},{9,1},... | collective-permute-start | bytes 614408 | tf_op jit(solution)/shard_map/ppermute | solution.py:40
  129.6 18.9 %collective-permute-start.18 = (bf16[192,896]{1,0:T(8,128)(2,1)}, bf16[192,896]{1,0:T(8,128)(2,1)S(1)}, u32[]{:S(2)}, u32[]{:S(2)}) collective-permute-start(bf16[192,896]{1,0:T(8,128)(2,1)} %get-tuple-element.9), channel_id=1, source_target_pairs={{0,16},{1,17},{2,18},{3,19},{4,20},{5,21},{6,22},{7,23},{8,24},{9,... | collective-permute-start | bytes 1032200 | tf_op jit(solution)/shard_map/ppermute | solution.py:40
  141.2 11.8 %collective-permute-start.22 = (f32[80,640]{1,0:T(8,128)S(1)}, f32[80,640]{1,0:T(8,128)S(1)}, u32[]{:S(2)}, u32[]{:S(2)}) collective-permute-start(f32[80,640]{1,0:T(8,128)S(1)} %select_bitcast_fusion), channel_id=1, source_target_pairs={{0,16},{1,17},{2,18},{3,19},{4,20},{5,21},{6,22},{7,23},{8,24},{9,... | collective-permute-start | bytes 614408 | tf_op jit(solution)/shard_map/ppermute | solution.py:40
  (12 other events, 148.3 us)
Sparse Core Ops, SparseCore 0:
  22.8 67.2 all-gather.1

commit v3 on v2

--- a/solution.py
+++ b/solution.py
@@ -16,7 +16,8 @@
 ROWS = 192
 IN_BLOCK = 640
 OUT_BLOCK = 80
-EXTRA = 64
+EXTRA = 112
+SLOT = 224
 
 perturb_scale = 0.5
 
@@ -57,8 +58,8 @@
     return (z, xh, core, y, xl ^ flip)
 
 
-def ring_target(z, xl, core, y, xh):
-    return (z + (1 if core == 0 else -1), xl, core, y, xh)
+def z_target(step, z, xl, core, y, xh):
+    return (z + step, xl, core, y, xh)
 
 
 def core_target(z, xl, core, y, xh):
@@ -86,29 +87,23 @@
     return high.astype(BF16), (value - high).astype(BF16)
 
 
+def slots_of(z):
+    near = [(0, 0, 0), (0, SLOT, -1), (0, 2 * SLOT, 1)]
+    far = [(1, 0, -2), (1, SLOT, 2), (1, 2 * SLOT, -3), (1, 3 * SLOT, 3)]
+    return [(g, row, lax.rem(z + 16 + step, 8)) for g, row, step in near + far + [(2, 0, 4)]]
+
+
 def product_kernel(
-    place, q, r1, r2, r3, s1, s2, s3, r4, s4, t0, t1, t2, t3, mine, mine_proj, give, weights, total, proj
+    place, g0, g1, g2, s0, s1, s2, t0, t1, t2, t3, mine, mine_proj, give, weights, total, proj
 ):
     z, core, own = place[0], place[1], place[2]
-    sign = 2 * core - 1
-
-    def put(near, column, block):
+    for group, row, column in slots_of(z):
         rows = pl.ds(pl.multiple_of(column * OUT_BLOCK, 16), OUT_BLOCK)
-        weights[near, rows, :] = block
-
-    def put_all(offset, ref):
-        column = lax.rem(z + 16 + offset, 8)
-        for near in range(4):
-            put(near, column, ref[near * OUT_BLOCK : (near + 1) * OUT_BLOCK, :])
-
-    put_all(0, q)
-    for step, (ring, swapped) in enumerate(((r1, s1), (r2, s2), (r3, s3)), 1):
-        put_all(sign * step, ring)
-        put_all(-sign * step, swapped)
-    last = lax.rem(z + 4, 8)
-    for i in range(2):
-        put(2 * core + i, last, r4[i * OUT_BLOCK : (i + 1) * OUT_BLOCK, :])
-        put(2 * (1 - core) + i, last, s4[i * OUT_BLOCK : (i + 1) * OUT_BLOCK, :])
+        for half in range(2):
+            start = row + half * (SLOT // 2)
+            block = slice(start, start + OUT_BLOCK)
+            weights[2 * half + core, rows, :] = (g0, g1, g2)[group][block, :]
+            weights[2 * half + 1 - core, rows, :] = (s0, s1, s2)[group][block, :]
 
     for near, rows in enumerate((t0, t1, t2, t3)):
         part = nt_dot(rows[: 2 * ROWS, :], weights[near])
@@ -152,36 +147,43 @@
     )(place, *arrays)
 
 
-def spread_weights(base_weight, z, core):
+def spread_columns(base_weight, left, z):
     piece = base_weight.T.astype(BF16)
     first = move(piece, functools.partial(weight_target, 0))
     second = move(piece, functools.partial(weight_target, 8))
-    pair = jnp.where(z < 8, jnp.stack([first, second]), jnp.stack([second, first]))
-    other = move(pair, core_target)
-    whole = jnp.where(core == 0, jnp.stack([pair, other], 1), jnp.stack([other, pair], 1))
-    return whole.reshape(4 * OUT_BLOCK, IN_BLOCK)
-
-
-def ring(whole, core):
-    held, swapped = [], []
-    block = whole
-    for step in range(4):
-        if step == 3:
-            half = 2 * OUT_BLOCK
-            block = jnp.where(core == 0, block[:half], block[half:])
-        block = move(block, ring_target)
-        held.append(block)
-        swapped.append(move(block, core_target))
-    return held, swapped
-
-
-def spread_right(right_local, z):
+    far = move(left, functools.partial(z_target, 8))
+    slot = jnp.where(
+        z < 8,
+        jnp.concatenate([first, left, second, far]),
+        jnp.concatenate([second, far, first, left]),
+    )
+    ups, downs = [slot], [slot]
+    for _ in range(3):
+        ups.append(move(ups[-1], functools.partial(z_target, 1)))
+        downs.append(move(downs[-1], functools.partial(z_target, -1)))
+    last_up = move(ups[3][: SLOT // 2], functools.partial(z_target, 1))
+    last_down = move(downs[3][SLOT // 2 :], functools.partial(z_target, -1))
+    groups = [
+        jnp.concatenate([slot, ups[1], downs[1]]),
+        jnp.concatenate([ups[2], downs[2], ups[3], downs[3]]),
+        jnp.concatenate([last_up, last_down]),
+    ]
+    return groups, [move(g, core_target) for g in groups]
+
+
+def spread_right(right_local, ranks, z):
     parity = z % 2
-    right = right_local.astype(BF16)
+    levels = jnp.pad(ranks.astype(BF16)[None, :], ((0, 15), (0, 320 - M_DEV)))
+    high, low = split(right_local)
     parts = []
     for flip in range(2):
-        chunk = jnp.where(parity == flip, right[:, :320], right[:, 320:])
-        parts.append(move(chunk, functools.partial(right_target, flip)))
+        chunk = jnp.where(
+            parity == flip,
+            jnp.concatenate([high[:, :320], low[:, :320]]),
+            jnp.concatenate([high[:, 320:], low[:, 320:]]),
+        )
+        sent = jnp.concatenate([chunk, levels])
+        parts.append(move(sent, functools.partial(right_target, flip)))
     return jnp.concatenate(parts, 1)
 
 
@@ -195,54 +197,84 @@
     return near, above, far, below
 
 
-def rank_rows(ranks):
-    own = jnp.pad(ranks.astype(F32)[None, :], ((0, 7), (0, 120)))
-    both = jnp.concatenate([own[:, :M_DEV], move(own, core_target)[:, :M_DEV]], 1)
-    both = jnp.pad(both, ((0, 0), (0, 112)))
-    every = jnp.concatenate([both[:, : 2 * M_DEV], move(both, xl_target)[:, : 2 * M_DEV]], 1)
-    return jnp.pad(every, ((0, 0), (0, IN_BLOCK - 4 * M_DEV)))
-
-
-def update_kernel(members, place, left, t0, t1, t2, t3, keep, give, right, high, low, total):
+def rank_kernel(*refs):
+    out = refs[-1]
+    lane = lax.broadcasted_iota(jnp.int32, (1, 128), 1)
+    for i, ref in enumerate(refs[:-1]):
+        row = ref[:, :384].astype(F32)[:1, :]
+        out[i : i + 1, :128] = jnp.where(lane < M_DEV, row[:, :128], 0.0)
+        second = jnp.logical_and(lane >= 64, lane < 64 + M_DEV)
+        out[i : i + 1, 128:] = jnp.where(second, row[:, 256:384], 0.0)
+
+
+def every_rank(blocks):
+    rows = [(2 * ROWS + m * EXTRA + 96) // 16 for m in range(2)]
+    specs = [pl.BlockSpec((16, IN_BLOCK), lambda i, r=r: (r, 0)) for r in rows]
+    own = pl.pallas_call(
+        rank_kernel,
+        out_shape=jax.ShapeDtypeStruct((8, 256), F32),
+        grid=(1,),
+        in_specs=specs * 4,
+        out_specs=pl.BlockSpec((8, 256), lambda i: (0, 0)),
+        cost_estimate=pl.CostEstimate(flops=10000, bytes_accessed=200000, transcendentals=0),
+    )(*[b for b in blocks for _ in range(2)])
+    both = jnp.concatenate([own, move(own, core_target)])
+    return both, move(both, xl_target)
+
+
+def update_kernel(
+    members, place, own, other, g0, g1, g2, t0, t1, t2, t3, keep, give, lefts, left, high, low, total
+):
     z, core, y, xh = place[0], place[1], place[3], place[4]
-    lanes = lax.broadcasted_iota(jnp.int32, (8, 128), 1)
-    rows = lax.broadcasted_iota(jnp.int32, (8, 128), 0)
-    valid = jnp.logical_and(rows == 0, lanes < 4 * M_DEV)
-    tiles = [left[i * 40 + 32 : i * 40 + 40, :128] for i in range(16)]
-    rank_sum = tiles[0]
-    for tile in tiles[1:]:
-        rank_sum = rank_sum + tile
-    rank_mean = jnp.sum(rank_sum) / members
-    spread = jnp.zeros((8, 128), F32)
-    for tile in tiles:
-        spread = spread + jnp.where(valid, (tile - rank_mean) ** 2, 0.0)
+    for group, row, column in slots_of(z):
+        for half in range(2):
+            start = row + half * (SLOT // 2) + OUT_BLOCK
+            lefts[column + 8 * half] = (g0, g1, g2)[group][start : start + 32, :]
+
+    rank_mean = (jnp.sum(own[...]) + jnp.sum(other[...])) / members
+    lane = lax.broadcasted_iota(jnp.int32, (16, 256), 1)
+    valid = jnp.logical_or(lane < M_DEV, jnp.logical_and(lane >= 192, lane < 192 + M_DEV))
+    spread = jnp.where(valid, (own[...] - rank_mean) ** 2 + (other[...] - rank_mean) ** 2, 0.0)
     variance = jnp.full((8, 128), jnp.sum(spread) / members)
     scale = lax.rsqrt(variance + 1e-05)[:1, :1] * math.sqrt(D / (members * RANK))
 
-    wide_lane = lax.broadcasted_iota(jnp.int32, (32, 128), 1)
-    wide_member = lax.broadcasted_iota(jnp.int32, (32, 128), 0) // RANK
+    lane = lax.broadcasted_iota(jnp.int32, (32, 128), 1)
+    member = lax.broadcasted_iota(jnp.int32, (32, 128), 0) // RANK
+    in_first = lax.broadcasted_iota(jnp.int32, (32, IN_BLOCK), 1) < 320
     for near, extra in enumerate((t0, t1, t2, t3)):
         for m in range(2):
-            slot = (near * 2 + m) * 32
-            right[slot : slot + 32, :] = extra[m * EXTRA + 32 : m * EXTRA + 64, :]
+            index = near * 2 + m
+            rows = slice(index * 32, index * 32 + 32)
+            level = [
+                jnp.sum(
+                    jnp.where(
+                        lane == member + 64 * flip,
+                        own[index : index + 1, flip * 128 : flip * 128 + 128],
+                        0.0,
+                    ),
+                    axis=1,
+                    keepdims=True,
+                )
+                for flip in range(2)
+            ]
+            fitness = (jnp.where(in_first, level[0], level[1]) - rank_mean) * scale
+            base = m * EXTRA
+            scaled = fitness * (
+                extra[base + 32 : base + 64, :].astype(F32)
+                + extra[base + 64 : base + 96, :].astype(F32)
+            )
+            part = scaled.astype(BF16)
+            high[rows, :] = part
+            low[rows, :] = (scaled - part.astype(F32)).astype(BF16)
             pair = (xh ^ m) * 4 + lax.rem(y + near, 4)
             for flip in range(2):
-                start = pl.multiple_of((2 * pair + (lax.rem(z, 2) ^ flip)) * 40, 8)
-                levels = left[pl.ds(start + 32, 8), :128][:1, :]
-                level = jnp.sum(
-                    jnp.where(wide_lane == wide_member, levels, 0.0), axis=1, keepdims=True
-                )
-                scaled = left[pl.ds(start, 32), :] * ((level - rank_mean) * scale)
-                part = scaled.astype(BF16)
-                high[flip, slot : slot + 32, :] = part
-                low[flip, slot : slot + 32, :] = (scaled - part.astype(F32)).astype(BF16)
+                left[flip, rows, :] = lefts[2 * pair + (lax.rem(z, 2) ^ flip)]
 
     def tn_dot(a, b):
         return lax.dot_general(a, b, (((0,), (0,)), ((), ())), preferred_element_type=F32)
 
-    first, second = right[:, :384], right[:, 256:]
-    total[...] = (tn_dot(first, high[0]) + tn_dot(first, low[0]))[:320]
-    total[...] += (tn_dot(second, high[1]) + tn_dot(second, low[1]))[64:]
+    total[...] = (tn_dot(high[:, :384], left[0]) + tn_dot(low[:, :384], left[0]))[:320]
+    total[...] += (tn_dot(high[:, 256:], left[1]) + tn_dot(low[:, 256:], left[1]))[64:]
     for i in range(2):
         here = pl.ds(pl.multiple_of((2 * i + core) * OUT_BLOCK, 8), OUT_BLOCK)
         there = pl.ds(pl.multiple_of((2 * i + 1 - core) * OUT_BLOCK, 8), OUT_BLOCK)
@@ -250,27 +282,27 @@
         give[i] = total[there, :]
 
 
-def update_block(place, left_all, blocks, xl, members):
+def update_block(place, groups, blocks, xl, members):
     vmem = pl.BlockSpec(memory_space=pltpu.VMEM)
-    extra = pl.BlockSpec((2 * EXTRA, IN_BLOCK), lambda i: (2 * ROWS // (2 * EXTRA), 0))
     shape = jax.ShapeDtypeStruct((2, OUT_BLOCK, IN_BLOCK), F32)
+    extras = [b[2 * ROWS :] for b in blocks]
     keep, give = pl.pallas_call(
         functools.partial(update_kernel, members),
         out_shape=(shape, shape),
-        grid=(1,),
-        in_specs=[pl.BlockSpec(memory_space=pltpu.SMEM), vmem] + [extra] * 4,
+        in_specs=[pl.BlockSpec(memory_space=pltpu.SMEM)] + [vmem] * 9,
         out_specs=(vmem, vmem),
         scratch_shapes=[
+            pltpu.VMEM((16, 32, IN_BLOCK), BF16),
+            pltpu.VMEM((2, 256, IN_BLOCK), BF16),
             pltpu.VMEM((256, IN_BLOCK), BF16),
-            pltpu.VMEM((2, 256, IN_BLOCK), BF16),
-            pltpu.VMEM((2, 256, IN_BLOCK), BF16),
+            pltpu.VMEM((256, IN_BLOCK), BF16),
             pltpu.VMEM((320, IN_BLOCK), F32),
         ],
         compiler_params=pltpu.CompilerParams(vmem_limit_bytes=32 * 2**20),
         cost_estimate=pl.CostEstimate(
             flops=8 * 384 * 256 * 640, bytes_accessed=4 * 2**20, transcendentals=0
         ),
-    )(place, left_all, *blocks)
+    )(place, *every_rank(blocks), *groups, *extras)
     keep = keep + move(give, core_target)
     give = jnp.where(xl == 0, keep[1], keep[0])
     keep = jnp.where(xl == 0, keep[0], keep[1])
@@ -305,25 +337,18 @@
 def on_device(tokens, base_weight, left_factors, right_factors, member_of, ranks):
     z, xl, core, y, xh = (lax.axis_index(name) for name in AXES)
     members = M_DEV * 64
-    left = left_factors.reshape(32, IN_BLOCK)
-    left_all = lax.all_gather(
-        jnp.concatenate([left, rank_rows(ranks)]), "z", axis=0, tiled=True
-    )
-
+    left = left_factors.astype(BF16).reshape(32, IN_BLOCK)
     offset = (y * 2 + xh) * IN_BLOCK
     right_local = lax.dynamic_slice_in_dim(right_factors, offset, IN_BLOCK, 2).reshape(32, IN_BLOCK)
-    whole = spread_weights(base_weight, z, core)
-    right = spread_right(right_local, z)
-    held, swapped = ring(whole, core)
-    blocks = spread_rows(jnp.concatenate([tokens, left.astype(BF16), right]), core)
+    right = spread_right(right_local, ranks, z)
+    groups, swapped = spread_columns(base_weight, left, z)
+    blocks = spread_rows(jnp.concatenate([tokens, left, right]), core)
 
     place = jnp.stack([z, core, xl ^ xh, y, xh]).astype(jnp.int32)
-    mine, mine_proj, give = product(
-        place, whole, *held[:3], *swapped[:3], held[3], swapped[3], *blocks
-    )
+    mine, mine_proj, give = product(place, *groups, *swapped, *blocks)
     got = move(give, xl_target)
     outputs = output_block(mine, mine_proj, got, right_local, member_of)
-    update = update_block(place, left_all, blocks, xl, members)
+    update = update_block(place, groups, blocks, xl, members)
     return (outputs, update)
 
 

time: 162 us -> 176 us (1.086)
  starting transfers between devices: 101 us -> 123 us
  between operations: 14.6 us -> 1.34 us
  local copies, waits for them, and re-layouts: 6.66 us -> 11.5 us
  waiting for transfers between devices: 20.4 us -> 16.5 us
  Pallas kernels: 10.5 us -> 13.8 us
    ppermute x23 -> x26, starting transfers between devices: 101 us -> 123 us  [move(): lax.ppermute(value, AXES, [(flat(p), flat(target(*p))) for p in places])]
    ppermute x23 -> x26, waiting for transfers between devices: 20.4 us -> 16.5 us  [move(): lax.ppermute(value, AXES, [(flat(p), flat(target(*p))) for p in places])]
    unnamed x24 -> x48, local copies, waits for them, and re-layouts: 4.74 us -> 8.56 us
    concatenate x4, other arithmetic: 0.89 us -> 2.82 us  [the longest x1 2.02 us: spread_columns(): jnp.concatenate([slot, ups[1], downs[1]])]
  transfers between devices with their start and end apart: 24 -> 26, of which waited for: 9 -> 8; matrix products, arithmetic and copies ran while one was open for 4% -> 8% of each run, Pallas kernels for 7% -> 8%
where the time goes in v3:
time: 176 us; the launch traced here: 174 us
  starting transfers between devices  123 us (70%)
  waiting for transfers between devices  16.5 us (9%)
  Pallas kernels  13.8 us (8%)
  local copies, waits for them, and re-layouts  11.5 us (7%)
  other arithmetic  8.45 us (5%)
    ppermute x26, starting transfers between devices, move(): lax.ppermute(value, AXES, [(flat(p), flat(target(*p))) for p in places])  123 us
    ppermute x26, waiting for transfers between devices, move(): lax.ppermute(value, AXES, [(flat(p), flat(target(*p))) for p in places])  16.5 us
    unnamed x48, local copies, waits for them, and re-layouts  8.56 us
    pallas_call x1, Pallas kernels, product(): pl.pallas_call(product_kernel, out_shape=(jax.ShapeDtypeStruct((ROWS, IN_...  6.05 us
    pallas_call x1, Pallas kernels, update_block(): pl.pallas_call(functools.partial(update_kernel, members), out_shape=(shap...  3.64 us
  transfers between devices with their start and end apart: 26, of which 8 were waited for; matrix products, arithmetic and copies ran while one was open for 8% of the time, Pallas kernels for 8%

profile of v3, /device:TPU:1, one launch (start us, length us, event | category | flops | bytes accessed | tf_op | source)
XLA Modules:
  0.0 174.1 jit_solution(1248250679109044943)
XLA Ops:
  3.3 4.4 %collective-permute-start.15 = (bf16[80,320]{1,0:T(8,128)(2,1)S(1)}, bf16[80,320]{1,0:T(8,128)(2,1)S(1)}, u32[]{:S(2)}, u32[]{:S(2)}) collective-permute-start(bf16[80,320]{1,0:T(8,128)(2,1)S(1)} %get-tuple-element.21), channel_id=1, source_target_pairs={{0,32},{1,96},{2,160},{3,224},{4,288},{5,352},{6,416},{7,480},{8,4... | collective-permute-start | bytes 153608 | tf_op jit(solution)/shard_map/ppermute | solution.py:41
  10.1 19.0 %collective-permute-start.17 = (bf16[304,640]{1,0:T(8,128)(2,1)S(1)}, bf16[304,640]{1,0:T(8,128)(2,1)S(1)}, u32[]{:S(2)}, u32[]{:S(2)}) collective-permute-start(bf16[304,640]{1,0:T(8,128)(2,1)S(1)} %maximum_maximum_fusion), channel_id=1, source_target_pairs={{0,1},{1,17},{2,3},{3,19},{4,5},{5,21},{6,7},{7,23},{8,9},{9,25},{... | collective-permute-start | bytes 1167368 | tf_op jit(solution)/shard_map/ppermute | solution.py:41
  29.0 15.6 %collective-permute-start.2 = (bf16[32,640]{1,0:T(8,128)(2,1)S(1)}, bf16[32,640]{1,0:T(8,128)(2,1)S(1)}, u32[]{:S(2)}, u32[]{:S(2)}) collective-permute-start(bf16[32,640]{1,0:T(8,128)(2,1)S(1)} %reshape.17), channel_id=1, source_target_pairs={{0,256},{1,257},{2,258},{3,259},{4,260},{5,261},{6,262},{7,263},{8... | collective-permute-start | bytes 122888 | tf_op jit(solution)/shard_map/ppermute | solution.py:41
  44.7 4.9 %collective-permute-start = (bf16[80,640]{1,0:T(8,128)(2,1)S(1)}, bf16[80,640]{1,0:T(8,128)(2,1)}, u32[]{:S(2)}, u32[]{:S(2)}) collective-permute-start(bf16[80,640]{1,0:T(8,128)(2,1)S(1)} %convert_bitcast_fusion), channel_id=1, source_target_pairs={{0,0},{1,16},{2,8},{3,24},{4,256},{5,272},{6,264},{7,280},{8,32},{... | collective-permute-start | bytes 307208 | tf_op jit(solution)/shard_map/ppermute | solution.py:41
  49.6 12.9 %collective-permute-start.1 = (bf16[80,640]{1,0:T(8,128)(2,1)S(1)}, bf16[80,640]{1,0:T(8,128)(2,1)}, u32[]{:S(2)}, u32[]{:S(2)}) collective-permute-start(bf16[80,640]{1,0:T(8,128)(2,1)S(1)} %convert_bitcast_fusion), channel_id=1, source_target_pairs={{0,256},{1,272},{2,264},{3,280},{4,0},{5,16},{6,8},{7,24},{8,288},... | collective-permute-start | bytes 307208 | tf_op jit(solution)/shard_map/ppermute | solution.py:41
  64.7 3.4 %collective-permute-start.19 = (bf16[608,640]{1,0:T(8,128)(2,1)S(1)}, bf16[608,640]{1,0:T(8,128)(2,1)S(1)}, u32[]{:S(2)}, u32[]{:S(2)}) collective-permute-start(bf16[608,640]{1,0:T(8,128)(2,1)S(1)} %pad_maximum_fusion.1.t0.refs_0_.refs_1_), channel_id=1, source_target_pairs={{0,2},{1,3},{2,4},{3,5},{4,6},{5,7},{6,0},{7,1},{8,10},{9,11},{10,... | collective-permute-start | bytes 2334728 | tf_op jit(solution)/shard_map/ppermute | solution.py:41
  69.2 3.3 %collective-permute-start.3 = (bf16[224,640]{1,0:T(8,128)(2,1)S(1)}, bf16[224,640]{1,0:T(8,128)(2,1)}, u32[]{:S(2)}, u32[]{:S(2)}) collective-permute-start(bf16[224,640]{1,0:T(8,128)(2,1)S(1)} %maximum_select_fusion), channel_id=1, source_target_pairs={{0,32},{1,33},{2,34},{3,35},{4,36},{5,37},{6,38},{7,39},{8,40},{9,... | collective-permute-start | bytes 860168 | tf_op jit(solution)/shard_map/ppermute | solution.py:41
  72.5 9.0 %collective-permute-start.4 = (bf16[224,640]{1,0:T(8,128)(2,1)S(1)}, bf16[224,640]{1,0:T(8,128)(2,1)}, u32[]{:S(2)}, u32[]{:S(2)}) collective-permute-start(bf16[224,640]{1,0:T(8,128)(2,1)S(1)} %maximum_select_fusion), channel_id=1, source_target_pairs={{0,480},{1,481},{2,482},{3,483},{4,484},{5,485},{6,486},{7,487},{8... | collective-permute-start | bytes 860168 | tf_op jit(solution)/shard_map/ppermute | solution.py:41
  81.5 2.4 %collective-permute-done.3 = bf16[224,640]{1,0:T(8,128)(2,1)} collective-permute-done((bf16[224,640]{1,0:T(8,128)(2,1)S(1)}, bf16[224,640]{1,0:T(8,128)(2,1)}, u32[]{:S(2)}, u32[]{:S(2)}) %collective-permute-start.3) | collective-permute-done | bytes 286752 | tf_op jit(solution)/shard_map/ppermute | solution.py:41
  85.8 4.6 %collective-permute-start.6 = (bf16[224,640]{1,0:T(8,128)(2,1)}, bf16[224,640]{1,0:T(8,128)(2,1)}, u32[]{:S(2)}, u32[]{:S(2)}) collective-permute-start(bf16[224,640]{1,0:T(8,128)(2,1)} %collective-permute-done.4), channel_id=1, source_target_pairs={{0,480},{1,481},{2,482},{3,483},{4,484},{5,485},{6,486},{7,487},{8... | collective-permute-start | bytes 860168 | tf_op jit(solution)/shard_map/ppermute | solution.py:41
  90.4 3.0 %collective-permute-done.5 = bf16[224,640]{1,0:T(8,128)(2,1)} collective-permute-done((bf16[224,640]{1,0:T(8,128)(2,1)}, bf16[224,640]{1,0:T(8,128)(2,1)}, u32[]{:S(2)}, u32[]{:S(2)}) %collective-permute-start.5) | collective-permute-done | bytes 286752 | tf_op jit(solution)/shard_map/ppermute | solution.py:41
  95.4 4.9 %collective-permute-start.8 = (bf16[224,640]{1,0:T(8,128)(2,1)}, bf16[224,640]{1,0:T(8,128)(2,1)S(1)}, u32[]{:S(2)}, u32[]{:S(2)}) collective-permute-start(bf16[224,640]{1,0:T(8,128)(2,1)} %collective-permute-done.6), channel_id=1, source_target_pairs={{0,480},{1,481},{2,482},{3,483},{4,484},{5,485},{6,486},{7,487},{8... | collective-permute-start | bytes 860168 | tf_op jit(solution)/shard_map/ppermute | solution.py:41
  103.4 2.0 %collective-permute-start.20 = (bf16[608,640]{1,0:T(8,128)(2,1)}, bf16[608,640]{1,0:T(8,128)(2,1)}, u32[]{:S(2)}, u32[]{:S(2)}) collective-permute-start(bf16[608,640]{1,0:T(8,128)(2,1)} %broadcast_select_fusion), channel_id=1, source_target_pairs={{0,2},{1,3},{2,4},{3,5},{4,6},{5,7},{6,0},{7,1},{8,14},{9,15},{10,... | collective-permute-start | bytes 2334728 | tf_op jit(solution)/shard_map/ppermute | solution.py:41
  109.4 7.3 %collective-permute-start.12 = (bf16[896,640]{1,0:T(8,128)(2,1)}, bf16[896,640]{1,0:T(8,128)(2,1)}, u32[]{:S(2)}, u32[]{:S(2)}) collective-permute-start(bf16[896,640]{1,0:T(8,128)(2,1)} %constant_dynamic-update-slice_fusion.g1), channel_id=1, source_target_pairs={{0,8},{1,9},{2,10},{3,11},{4,12},{5,13},{6,14},{7,15},{8,0},{9,1},... | collective-permute-start | bytes 3440648 | tf_op jit(solution)/shard_map/ppermute | solution.py:41
  116.7 2.0 %pad_maximum_fusion.g0 = bf16[672,640]{1,0:T(8,128)(2,1)} fusion(bf16[224,640]{1,0:T(8,128)(2,1)} %collective-permute-done.4, bf16[224,640]{1,0:T(8,128)(2,1)} %collective-permute-done.3, bf16[224,640]{1,0:T(8,128)(2,1)S(1)} %copy-done.13), kind=kLoop, calls=%fused_computation | loop fusion | flops 2580480 | bytes 1720320 | tf_op jit(solution)/shard_map/concatenate | solution.py:167
  123.5 4.7 %collective-permute-start.10 = (bf16[112,640]{1,0:T(8,128)(2,1)S(1)}, bf16[112,640]{1,0:T(8,128)(2,1)S(1)}, u32[]{:S(2)}, u32[]{:S(2)}) collective-permute-start(bf16[112,640]{1,0:T(8,128)(2,1)S(1)} %slice.69), channel_id=1, source_target_pairs={{0,480},{1,481},{2,482},{3,483},{4,484},{5,485},{6,486},{7,487},{8... | collective-permute-start | bytes 430088 | tf_op jit(solution)/shard_map/ppermute | solution.py:41
  129.7 3.1 %collective-permute-start.22 = (f32[8,256]{1,0:T(8,128)}, f32[8,256]{1,0:T(8,128)S(1)}, u32[]{:S(2)}, u32[]{:S(2)}) collective-permute-start(f32[8,256]{1,0:T(8,128)} %shard_map.79), channel_id=1, source_target_pairs={{0,8},{1,9},{2,10},{3,11},{4,12},{5,13},{6,14},{7,15},{8,0},{9,1},... | collective-permute-start | bytes 24584 | tf_op jit(solution)/shard_map/ppermute | solution.py:41
  139.0 3.6 %shard_map.80 = (f32[2,80,640]{2,1,0:T(8,128)S(1)}, f32[2,80,640]{2,1,0:T(8,128)}) custom-call(s32[5]{0:T(128)S(1)} %stack.23.place, f32[16,256]{1,0:T(8,128)S(1)} %pad_maximum_fusion.5.own, f32[16,256]{1,0:T(8,128)S(1)} %collective-permute-done.23.other, bf16[672,640]{1,0:T(8,128)(2,1)} %pad_maximum_fusion.g0, ...), custom_call_target="tpu_custom_call" | custom-call | flops 503316480 | bytes 4194304 | tf_op jit(solution)/shard_map/pallas_call | solution.py:289
  143.4 3.4 %collective-permute-start.24 = (f32[2,80,640]{2,1,0:T(8,128)}, f32[2,80,640]{2,1,0:T(8,128)}, u32[]{:S(2)}, u32[]{:S(2)}) collective-permute-start(f32[2,80,640]{2,1,0:T(8,128)} %get-tuple-element.11), channel_id=1, source_target_pairs={{0,8},{1,9},{2,10},{3,11},{4,12},{5,13},{6,14},{7,15},{8,0},{9,1},... | collective-permute-start | bytes 1228808 | tf_op jit(solution)/shard_map/ppermute | solution.py:41
  150.4 6.0 %shard_map.77 = (f32[192,640]{1,0:T(8,128)S(1)}, f32[192,32]{1,0:T(8,128)S(1)}, bf16[192,896]{1,0:T(8,128)(2,1)}) custom-call(s32[5]{0:T(128)S(1)} %stack.23.place, bf16[672,640]{1,0:T(8,128)(2,1)} %pad_maximum_fusion.g0, bf16[896,640]{1,0:T(8,128)(2,1)} %constant_dynamic-update-slice_fusion.g1, bf16[224,640]{1,0:T(8,128)(2,1)S(1)} %constant_dynamic-update-slice_fusion.4.g2, ...), custom_call_target="tpu_custom_call" | custom-call | flops 1258291200 | bytes 8388608 | tf_op jit(solution)/shard_map/pallas_call | solution.py:129
  157.2 2.0 %collective-permute-start.21 = (bf16[192,896]{1,0:T(8,128)(2,1)}, bf16[192,896]{1,0:T(8,128)(2,1)S(1)}, u32[]{:S(2)}, u32[]{:S(2)}) collective-permute-start(bf16[192,896]{1,0:T(8,128)(2,1)} %get-tuple-element.9), channel_id=1, source_target_pairs={{0,16},{1,17},{2,18},{3,19},{4,20},{5,21},{6,22},{7,23},{8,24},{9,... | collective-permute-start | bytes 1032200 | tf_op jit(solution)/shard_map/ppermute | solution.py:41
  160.4 3.4 %collective-permute-start.25 = (f32[80,640]{1,0:T(8,128)S(1)}, f32[80,640]{1,0:T(8,128)S(1)}, u32[]{:S(2)}, u32[]{:S(2)}) collective-permute-start(f32[80,640]{1,0:T(8,128)S(1)} %select_bitcast_fusion), channel_id=1, source_target_pairs={{0,16},{1,17},{2,18},{3,19},{4,20},{5,21},{6,22},{7,23},{8,24},{9,... | collective-permute-start | bytes 614408 | tf_op jit(solution)/shard_map/ppermute | solution.py:41
  164.5 4.4 %collective-permute-done.21.got = bf16[192,896]{1,0:T(8,128)(2,1)S(1)} collective-permute-done((bf16[192,896]{1,0:T(8,128)(2,1)}, bf16[192,896]{1,0:T(8,128)(2,1)S(1)}, u32[]{:S(2)}, u32[]{:S(2)}) %collective-permute-start.21) | collective-permute-done | bytes 344096 | tf_op jit(solution)/shard_map/ppermute | solution.py:41
  169.7 2.6 %shard_map.78 = f32[192,640]{1,0:T(8,128)} custom-call(f32[192,640]{1,0:T(8,128)} %copy-done.8, f32[192,32]{1,0:T(8,128)} %copy-done.11, bf16[192,896]{1,0:T(8,128)(2,1)} %copy-done.17, f32[32,640]{1,0:T(8,128)} %copy-done.14, s32[192,1]{1,0:T(8,128)} %copy.8.member), custom_call_target="tpu_custom_call" | custom-call | flops 47185920 | bytes 2097152 | tf_op jit(solution)/shard_map/pallas_call | solution.py:326
  (113 shorter events, 40.8 us)
Async XLA Ops:
  2.6 5.1 %collective-permute-start.14 = (bf16[80,320]{1,0:T(8,128)(2,1)S(1)}, bf16[80,320]{1,0:T(8,128)(2,1)S(1)}, u32[]{:S(2)}, u32[]{:S(2)}) collective-permute-start(bf16[80,320]{1,0:T(8,128)(2,1)S(1)} %get-tuple-element.20), channel_id=1, source_target_pairs={{0,0},{1,64},{2,128},{3,192},{4,256},{5,320},{6,384},{7,448},{8,8}... | collective-permute-start | bytes 153608 | tf_op jit(solution)/shard_map/ppermute | solution.py:41
  3.3 6.0 %collective-permute-start.15 = (bf16[80,320]{1,0:T(8,128)(2,1)S(1)}, bf16[80,320]{1,0:T(8,128)(2,1)S(1)}, u32[]{:S(2)}, u32[]{:S(2)}) collective-permute-start(bf16[80,320]{1,0:T(8,128)(2,1)S(1)} %get-tuple-element.21), channel_id=1, source_target_pairs={{0,32},{1,96},{2,160},{3,224},{4,288},{5,352},{6,416},{7,480},{8,4... | collective-permute-start | bytes 153608 | tf_op jit(solution)/shard_map/ppermute | solution.py:41
  9.4 53.2 %collective-permute-start.16 = (bf16[304,640]{1,0:T(8,128)(2,1)S(1)}, bf16[304,640]{1,0:T(8,128)(2,1)S(1)}, u32[]{:S(2)}, u32[]{:S(2)}) collective-permute-start(bf16[304,640]{1,0:T(8,128)(2,1)S(1)} %maximum_maximum_fusion), channel_id=1, source_target_pairs={{0,0},{1,16},{2,2},{3,18},{4,4},{5,20},{6,6},{7,22},{8,8},{9,24},{... | collective-permute-start | bytes 1167368 | tf_op jit(solution)/shard_map/ppermute | solution.py:41
  10.1 52.5 %collective-permute-start.17 = (bf16[304,640]{1,0:T(8,128)(2,1)S(1)}, bf16[304,640]{1,0:T(8,128)(2,1)S(1)}, u32[]{:S(2)}, u32[]{:S(2)}) collective-permute-start(bf16[304,640]{1,0:T(8,128)(2,1)S(1)} %maximum_maximum_fusion), channel_id=1, source_target_pairs={{0,1},{1,17},{2,3},{3,19},{4,5},{5,21},{6,7},{7,23},{8,9},{9,25},{... | collective-permute-start | bytes 1167368 | tf_op jit(solution)/shard_map/ppermute | solution.py:41
  29.0 39.0 %collective-permute-start.2 = (bf16[32,640]{1,0:T(8,128)(2,1)S(1)}, bf16[32,640]{1,0:T(8,128)(2,1)S(1)}, u32[]{:S(2)}, u32[]{:S(2)}) collective-permute-start(bf16[32,640]{1,0:T(8,128)(2,1)S(1)} %reshape.17), channel_id=1, source_target_pairs={{0,256},{1,257},{2,258},{3,259},{4,260},{5,261},{6,262},{7,263},{8... | collective-permute-start | bytes 122888 | tf_op jit(solution)/shard_map/ppermute | solution.py:41
  44.7 23.4 %collective-permute-start = (bf16[80,640]{1,0:T(8,128)(2,1)S(1)}, bf16[80,640]{1,0:T(8,128)(2,1)}, u32[]{:S(2)}, u32[]{:S(2)}) collective-permute-start(bf16[80,640]{1,0:T(8,128)(2,1)S(1)} %convert_bitcast_fusion), channel_id=1, source_target_pairs={{0,0},{1,16},{2,8},{3,24},{4,256},{5,272},{6,264},{7,280},{8,32},{... | collective-permute-start | bytes 307208 | tf_op jit(solution)/shard_map/ppermute | solution.py:41
  49.6 18.5 %collective-permute-start.1 = (bf16[80,640]{1,0:T(8,128)(2,1)S(1)}, bf16[80,640]{1,0:T(8,128)(2,1)}, u32[]{:S(2)}, u32[]{:S(2)}) collective-permute-start(bf16[80,640]{1,0:T(8,128)(2,1)S(1)} %convert_bitcast_fusion), channel_id=1, source_target_pairs={{0,256},{1,272},{2,264},{3,280},{4,0},{5,16},{6,8},{7,24},{8,288},... | collective-permute-start | bytes 307208 | tf_op jit(solution)/shard_map/ppermute | solution.py:41
  62.8 39.2 %collective-permute-start.18 = (bf16[608,640]{1,0:T(8,128)(2,1)S(1)}, bf16[608,640]{1,0:T(8,128)(2,1)S(1)}, u32[]{:S(2)}, u32[]{:S(2)}) collective-permute-start(bf16[608,640]{1,0:T(8,128)(2,1)S(1)} %pad_maximum_fusion.1.t0.refs_0_.refs_1_), channel_id=1, source_target_pairs={{0,6},{1,7},{2,0},{3,1},{4,2},{5,3},{6,4},{7,5},{8,14},{9,15},{10,... | collective-permute-start | bytes 2334728 | tf_op jit(solution)/shard_map/ppermute | solution.py:41
  64.7 37.3 %collective-permute-start.19 = (bf16[608,640]{1,0:T(8,128)(2,1)S(1)}, bf16[608,640]{1,0:T(8,128)(2,1)S(1)}, u32[]{:S(2)}, u32[]{:S(2)}) collective-permute-start(bf16[608,640]{1,0:T(8,128)(2,1)S(1)} %pad_maximum_fusion.1.t0.refs_0_.refs_1_), channel_id=1, source_target_pairs={{0,2},{1,3},{2,4},{3,5},{4,6},{5,7},{6,0},{7,1},{8,10},{9,11},{10,... | collective-permute-start | bytes 2334728 | tf_op jit(solution)/shard_map/ppermute | solution.py:41
  69.2 14.7 %collective-permute-start.3 = (bf16[224,640]{1,0:T(8,128)(2,1)S(1)}, bf16[224,640]{1,0:T(8,128)(2,1)}, u32[]{:S(2)}, u32[]{:S(2)}) collective-permute-start(bf16[224,640]{1,0:T(8,128)(2,1)S(1)} %maximum_select_fusion), channel_id=1, source_target_pairs={{0,32},{1,33},{2,34},{3,35},{4,36},{5,37},{6,38},{7,39},{8,40},{9,... | collective-permute-start | bytes 860168 | tf_op jit(solution)/shard_map/ppermute | solution.py:41
  72.5 13.3 %collective-permute-start.4 = (bf16[224,640]{1,0:T(8,128)(2,1)S(1)}, bf16[224,640]{1,0:T(8,128)(2,1)}, u32[]{:S(2)}, u32[]{:S(2)}) collective-permute-start(bf16[224,640]{1,0:T(8,128)(2,1)S(1)} %maximum_select_fusion), channel_id=1, source_target_pairs={{0,480},{1,481},{2,482},{3,483},{4,484},{5,485},{6,486},{7,487},{8... | collective-permute-start | bytes 860168 | tf_op jit(solution)/shard_map/ppermute | solution.py:41
  83.9 9.6 %collective-permute-start.5 = (bf16[224,640]{1,0:T(8,128)(2,1)}, bf16[224,640]{1,0:T(8,128)(2,1)}, u32[]{:S(2)}, u32[]{:S(2)}) collective-permute-start(bf16[224,640]{1,0:T(8,128)(2,1)} %collective-permute-done.3), channel_id=1, source_target_pairs={{0,32},{1,33},{2,34},{3,35},{4,36},{5,37},{6,38},{7,39},{8,40},{9,... | collective-permute-start | bytes 860168 | tf_op jit(solution)/shard_map/ppermute | solution.py:41
  85.8 9.6 %collective-permute-start.6 = (bf16[224,640]{1,0:T(8,128)(2,1)}, bf16[224,640]{1,0:T(8,128)(2,1)}, u32[]{:S(2)}, u32[]{:S(2)}) collective-permute-start(bf16[224,640]{1,0:T(8,128)(2,1)} %collective-permute-done.4), channel_id=1, source_target_pairs={{0,480},{1,481},{2,482},{3,483},{4,484},{5,485},{6,486},{7,487},{8... | collective-permute-start | bytes 860168 | tf_op jit(solution)/shard_map/ppermute | solution.py:41
  93.4 13.7 %collective-permute-start.7 = (bf16[224,640]{1,0:T(8,128)(2,1)}, bf16[224,640]{1,0:T(8,128)(2,1)S(1)}, u32[]{:S(2)}, u32[]{:S(2)}) collective-permute-start(bf16[224,640]{1,0:T(8,128)(2,1)} %collective-permute-done.5), channel_id=1, source_target_pairs={{0,32},{1,33},{2,34},{3,35},{4,36},{5,37},{6,38},{7,39},{8,40},{9,... | collective-permute-start | bytes 860168 | tf_op jit(solution)/shard_map/ppermute | solution.py:41
  95.4 12.5 %collective-permute-start.8 = (bf16[224,640]{1,0:T(8,128)(2,1)}, bf16[224,640]{1,0:T(8,128)(2,1)S(1)}, u32[]{:S(2)}, u32[]{:S(2)}) collective-permute-start(bf16[224,640]{1,0:T(8,128)(2,1)} %collective-permute-done.6), channel_id=1, source_target_pairs={{0,480},{1,481},{2,482},{3,483},{4,484},{5,485},{6,486},{7,487},{8... | collective-permute-start | bytes 860168 | tf_op jit(solution)/shard_map/ppermute | solution.py:41
  103.4 24.8 %collective-permute-start.20 = (bf16[608,640]{1,0:T(8,128)(2,1)}, bf16[608,640]{1,0:T(8,128)(2,1)}, u32[]{:S(2)}, u32[]{:S(2)}) collective-permute-start(bf16[608,640]{1,0:T(8,128)(2,1)} %broadcast_select_fusion), channel_id=1, source_target_pairs={{0,2},{1,3},{2,4},{3,5},{4,6},{5,7},{6,0},{7,1},{8,14},{9,15},{10,... | collective-permute-start | bytes 2334728 | tf_op jit(solution)/shard_map/ppermute | solution.py:41
  109.4 41.0 %collective-permute-start.12 = (bf16[896,640]{1,0:T(8,128)(2,1)}, bf16[896,640]{1,0:T(8,128)(2,1)}, u32[]{:S(2)}, u32[]{:S(2)}) collective-permute-start(bf16[896,640]{1,0:T(8,128)(2,1)} %constant_dynamic-update-slice_fusion.g1), channel_id=1, source_target_pairs={{0,8},{1,9},{2,10},{3,11},{4,12},{5,13},{6,14},{7,15},{8,0},{9,1},... | collective-permute-start | bytes 3440648 | tf_op jit(solution)/shard_map/ppermute | solution.py:41
  118.8 30.0 %collective-permute-start.11 = (bf16[672,640]{1,0:T(8,128)(2,1)}, bf16[672,640]{1,0:T(8,128)(2,1)}, u32[]{:S(2)}, u32[]{:S(2)}) collective-permute-start(bf16[672,640]{1,0:T(8,128)(2,1)} %pad_maximum_fusion.g0), channel_id=1, source_target_pairs={{0,8},{1,9},{2,10},{3,11},{4,12},{5,13},{6,14},{7,15},{8,0},{9,1},... | collective-permute-start | bytes 2580488 | tf_op jit(solution)/shard_map/ppermute | solution.py:41
  120.7 12.1 %collective-permute-start.9 = (bf16[112,640]{1,0:T(8,128)(2,1)S(1)}, bf16[112,640]{1,0:T(8,128)(2,1)S(1)}, u32[]{:S(2)}, u32[]{:S(2)}) collective-permute-start(bf16[112,640]{1,0:T(8,128)(2,1)S(1)} %slice.68), channel_id=1, source_target_pairs={{0,32},{1,33},{2,34},{3,35},{4,36},{5,37},{6,38},{7,39},{8,40},{9,... | collective-permute-start | bytes 430088 | tf_op jit(solution)/shard_map/ppermute | solution.py:41
  123.5 12.9 %collective-permute-start.10 = (bf16[112,640]{1,0:T(8,128)(2,1)S(1)}, bf16[112,640]{1,0:T(8,128)(2,1)S(1)}, u32[]{:S(2)}, u32[]{:S(2)}) collective-permute-start(bf16[112,640]{1,0:T(8,128)(2,1)S(1)} %slice.69), channel_id=1, source_target_pairs={{0,480},{1,481},{2,482},{3,483},{4,484},{5,485},{6,486},{7,487},{8... | collective-permute-start | bytes 430088 | tf_op jit(solution)/shard_map/ppermute | solution.py:41
  134.5 4.5 %collective-permute-start.23 = (f32[16,256]{1,0:T(8,128)S(1)}, f32[16,256]{1,0:T(8,128)S(1)}, u32[]{:S(2)}, u32[]{:S(2)}) collective-permute-start(f32[16,256]{1,0:T(8,128)S(1)} %pad_maximum_fusion.5.own), channel_id=1, source_target_pairs={{0,16},{1,17},{2,18},{3,19},{4,20},{5,21},{6,22},{7,23},{8,24},{9,... | collective-permute-start | bytes 49160 | tf_op jit(solution)/shard_map/ppermute | solution.py:41
  143.4 15.9 %collective-permute-start.24 = (f32[2,80,640]{2,1,0:T(8,128)}, f32[2,80,640]{2,1,0:T(8,128)}, u32[]{:S(2)}, u32[]{:S(2)}) collective-permute-start(f32[2,80,640]{2,1,0:T(8,128)} %get-tuple-element.11), channel_id=1, source_target_pairs={{0,8},{1,9},{2,10},{3,11},{4,12},{5,13},{6,14},{7,15},{8,0},{9,1},... | collective-permute-start | bytes 1228808 | tf_op jit(solution)/shard_map/ppermute | solution.py:41
  157.2 11.7 %collective-permute-start.21 = (bf16[192,896]{1,0:T(8,128)(2,1)}, bf16[192,896]{1,0:T(8,128)(2,1)S(1)}, u32[]{:S(2)}, u32[]{:S(2)}) collective-permute-start(bf16[192,896]{1,0:T(8,128)(2,1)} %get-tuple-element.9), channel_id=1, source_target_pairs={{0,16},{1,17},{2,18},{3,19},{4,20},{5,21},{6,22},{7,23},{8,24},{9,... | collective-permute-start | bytes 1032200 | tf_op jit(solution)/shard_map/ppermute | solution.py:41
  160.4 13.0 %collective-permute-start.25 = (f32[80,640]{1,0:T(8,128)S(1)}, f32[80,640]{1,0:T(8,128)S(1)}, u32[]{:S(2)}, u32[]{:S(2)}) collective-permute-start(f32[80,640]{1,0:T(8,128)S(1)} %select_bitcast_fusion), channel_id=1, source_target_pairs={{0,16},{1,17},{2,18},{3,19},{4,20},{5,21},{6,22},{7,23},{8,24},{9,... | collective-permute-start | bytes 614408 | tf_op jit(solution)/shard_map/ppermute | solution.py:41
  (24 other events, 268.2 us)

commit v4 on v3

v4 whole, which is shorter than its diff:
```python
import functools
import itertools
import math

import jax
import jax.numpy as jnp
from jax import lax
from jax.experimental import pallas as pl
from jax.experimental.pallas import tpu as pltpu
from jax.sharding import Mesh
from jax.sharding import PartitionSpec as P

D = 5120
RANK = 4
M_DEV = 8
ROWS = 192
IN_BLOCK = 640
OUT_BLOCK = 80
SLOT = 224
EXTRA = 80
LEFT_AT = 2 * EXTRA
ROWS_AT = LEFT_AT + 64
SEND = IN_BLOCK + 128

perturb_scale = 0.5

SIZES = {"z": 16, "xl": 2, "core": 2, "y": 4, "xh": 2}
AXES = tuple(SIZES)
POP = ("z", "xl", "core")
TENSOR = ("y", "xh")
BF16 = jnp.bfloat16
F32 = jnp.float32


def flat(place):
    index = 0
    for value, size in zip(place, SIZES.values()):
        index = index * size + value % size
    return index


def move(value, target):
    places = itertools.product(*(range(n) for n in SIZES.values()))
    return lax.ppermute(value, AXES, [(flat(p), flat(target(*p))) for p in places])


def weight_target(z, xl, core, y, xh):
    owner = z // 2
    to_y, to_xh = owner // 2, owner % 2
    column = (z % 2) * 4 + xl * 2 + core
    near = (y - to_y) % 4
    return ((near // 2) * 8 + column, xh, near % 2, to_y, to_xh)


def right_target(z, xl, core, y, xh):
    return (2 * (2 * y + xh) + z % 2, xl, core, z // 4, z // 2 % 2)


def rows_target(flip, z, xl, core, y, xh):
    return (z, xh, core, y, xl ^ flip)


def z_target(step, z, xl, core, y, xh):
    return (z + step, xl, core, y, xh)


def core_target(z, xl, core, y, xh):
    return (z, xl, 1 - core, y, xh)


def z_pair_target(z, xl, core, y, xh):
    return (z ^ 1, xl, core, y, xh)


def xh_target(z, xl, core, y, xh):
    return (z, xl, core, y, 1 - xh)


def xl_target(z, xl, core, y, xh):
    return (z, 1 - xl, core, y, xh)


def y_target(step, z, xl, core, y, xh):
    return (z, xl, core, y + step, xh)


def y_far_target(z, xl, core, y, xh):
    return (z, xl, core, y + (1 if core == 0 else -1), xh)


def nt_dot(a, b):
    return lax.dot_general(a, b, (((1,), (1,)), ((), ())), preferred_element_type=F32)


def split(value):
    high = lax.reduce_precision(value, 8, 7)
    return high.astype(BF16), (value - high).astype(BF16)


SLOT_STEPS = (0, -1, 1, -2, 2, -3, 3)


def slot_halves(z, refs):
    for ref, step in zip(refs, SLOT_STEPS):
        for half in range(2):
            yield lax.rem(z + 16 + step, 8), half, ref, half * (SLOT // 2)
    for half in range(2):
        yield lax.rem(z + 4, 8), half, refs[len(SLOT_STEPS) + half], 0


def paired(proj):
    lane = lax.broadcasted_iota(jnp.int32, proj.shape, 1)
    first = jnp.where(lane < 32, proj, 0.0)
    high = first.astype(BF16).astype(F32)
    return (high + pltpu.roll(first - high, 32, 1)).astype(BF16)


def unpaired(value):
    value = value.astype(F32)
    return value + pltpu.roll(value, 96, 1)


def product_kernel(place, *refs):
    slots, (t0, t1, t2, t3, p0, p1) = refs[:9], refs[9:15]
    mine, mine_proj, give, weights, rows = refs[15:]
    z, core = place[0], place[1]
    for column, half, ref, start in slot_halves(z, slots):
        at = pl.ds(pl.multiple_of(column * OUT_BLOCK, 16), OUT_BLOCK)
        weights[half, at, :] = ref[start : start + OUT_BLOCK, :]

    @pl.when(core == 0)
    def _():
        rows[0] = t0[LEFT_AT:, :]
        rows[1] = t2[LEFT_AT:, :]

    @pl.when(core == 1)
    def _():
        rows[0] = t1[LEFT_AT:, :]
        rows[1] = t3[LEFT_AT:, :]

    def sums(a, b):
        total = nt_dot(a[64:], weights[0]) + nt_dot(b[64:], weights[1])
        proj = []
        for m in range(2):
            part = 0.0
            for block in (a, b):
                left = block[m * 32 : m * 32 + 32]
                left = jnp.concatenate([left] * 4)
                part = part + nt_dot(block[64 + m * ROWS : 64 + (m + 1) * ROWS], left)
            proj.append(part)
        return total, jnp.concatenate(proj)

    total, proj = sums(p0[...], p1[...])
    give[:, :IN_BLOCK] = total.astype(BF16)
    give[:, IN_BLOCK:] = paired(proj)
    total, proj = sums(rows[0], rows[1])
    mine[...] = total
    mine_proj[...] = proj


def product(place, *arrays):
    vmem = pl.BlockSpec(memory_space=pltpu.VMEM)
    return pl.pallas_call(
        product_kernel,
        out_shape=(
            jax.ShapeDtypeStruct((2 * ROWS, IN_BLOCK), F32),
            jax.ShapeDtypeStruct((2 * ROWS, 128), F32),
            jax.ShapeDtypeStruct((2 * ROWS, SEND), BF16),
        ),
        in_specs=[pl.BlockSpec(memory_space=pltpu.SMEM)] + [vmem] * len(arrays),
        out_specs=(vmem, vmem, vmem),
        scratch_shapes=[
            pltpu.VMEM((2, IN_BLOCK, IN_BLOCK), BF16),
            pltpu.VMEM((2, 64 + 2 * ROWS, IN_BLOCK), BF16),
        ],
        compiler_params=pltpu.CompilerParams(vmem_limit_bytes=40 * 2**20),
        cost_estimate=pl.CostEstimate(
            flops=2 * 768 * 640 * 1280, bytes_accessed=8 * 2**20, transcendentals=0
        ),
    )(place, *arrays)


def join_kernel(place, total, proj, got, mine, mine_proj, give):
    own = place[2]
    for block, to_give in ((own, False), (1 - own, True)):
        at = pl.ds(pl.multiple_of(block * ROWS, ROWS), ROWS)
        value = total[at, :] + got[at, :IN_BLOCK].astype(F32)
        sums = proj[at, :] + unpaired(got[at, IN_BLOCK:])
        if to_give:
            give[:, :IN_BLOCK] = value.astype(BF16)
            give[:, IN_BLOCK:] = paired(sums)
        else:
            mine[...] = value
            mine_proj[...] = sums


def join(place, total, proj, got):
    vmem = pl.BlockSpec(memory_space=pltpu.VMEM)
    return pl.pallas_call(
        join_kernel,
        out_shape=(
            jax.ShapeDtypeStruct((ROWS, IN_BLOCK), F32),
            jax.ShapeDtypeStruct((ROWS, 128), F32),
            jax.ShapeDtypeStruct((ROWS, SEND), BF16),
        ),
        in_specs=[pl.BlockSpec(memory_space=pltpu.SMEM)] + [vmem] * 3,
        out_specs=(vmem, vmem, vmem),
        cost_estimate=pl.CostEstimate(flops=10**6, bytes_accessed=3 * 2**20, transcendentals=0),
    )(place, total, proj, got)


def spread_columns(base_weight, left, z):
    piece = move(base_weight.T.astype(BF16), weight_target)
    half = jnp.concatenate([piece, left])
    far = move(half, functools.partial(z_target, 8))
    slot = jnp.where(z < 8, jnp.concatenate([half, far]), jnp.concatenate([far, half]))
    up = down = slot
    slots = [slot]
    for _ in range(3):
        up = move(up, functools.partial(z_target, 1))
        down = move(down, functools.partial(z_target, -1))
        slots += [up, down]
    last_up = move(up[: SLOT // 2], functools.partial(z_target, 1))
    last_down = move(down[SLOT // 2 :], functools.partial(z_target, -1))
    return slots + [last_up, last_down]


def rank_row(ranks):
    own = jnp.pad(ranks.astype(BF16)[None, :], ((0, 15), (0, 120)))
    both = jnp.concatenate([own[:, :M_DEV], move(own, core_target)[:, :M_DEV]], 1)
    both = jnp.pad(both, ((0, 0), (0, 112)))
    every = jnp.concatenate([both[:, : 2 * M_DEV], move(both, xl_target)[:, : 2 * M_DEV]], 1)
    return jnp.pad(every, ((0, 0), (0, IN_BLOCK - 4 * M_DEV)))


def spread_right(right_local, ranks, z):
    sent = jnp.concatenate([*split(right_local), rank_row(ranks)])
    got = move(sent, right_target)
    odd = z % 2 == 1
    levels = got[64:, :320]
    own = jnp.where(odd, got[:64, 320:], got[:64, :320])
    other = jnp.where(odd, got[:64, :320], got[:64, 320:])
    pair = move(jnp.concatenate([other, levels]), z_pair_target)
    both = jnp.concatenate([jnp.concatenate([own, levels]), pair], 1)
    return jnp.concatenate([both, move(both, xh_target)])


def spread_rows(tokens, left, right, core):
    payload = jnp.concatenate([left, tokens])
    a = move(payload, functools.partial(rows_target, 0))
    b = move(payload, functools.partial(rows_target, 1))
    near = jnp.concatenate([right, a[:32], b[:32], a[32:], b[32:]])
    above = move(near, functools.partial(y_target, -1))
    below = move(near, functools.partial(y_target, 1))
    far = move(jnp.where(core == 0, below, above), y_far_target)
    first = move(jnp.where(core == 0, above[LEFT_AT:], near[LEFT_AT:]), core_target)
    second = move(jnp.where(core == 0, below[LEFT_AT:], far[LEFT_AT:]), core_target)
    return (near, above, far, below), (first, second)


def update_kernel(members, place, *refs):
    slots, extras = refs[:9], refs[9:13]
    keep, give, lefts, left, high, low, total = refs[13:]
    z, core, y, xh = place[0], place[1], place[3], place[4]
    for column, half, ref, start in slot_halves(z, slots):
        lefts[column + 8 * half] = ref[start + OUT_BLOCK : start + SLOT // 2, :]

    lane = lax.broadcasted_iota(jnp.int32, (1, 128), 1)
    levels, spread, rank_sum = [], 0.0, 0.0
    for extra in extras:
        for h in range(2):
            row = extra[h * EXTRA + 64 : h * EXTRA + EXTRA, :384].astype(F32)[:1, :]
            pair = [
                (row[:, 256 * f : 256 * f + 128], jnp.logical_and(lane >= 64 * f, lane < 64 * f + 32))
                for f in range(2)
            ]
            levels.append(pair)
    for value, valid in sum(levels, []):
        rank_sum = rank_sum + jnp.where(valid, value, 0.0)
    rank_mean = jnp.sum(rank_sum) / members
    for value, valid in sum(levels, []):
        spread = spread + jnp.where(valid, (value - rank_mean) ** 2, 0.0)
    variance = jnp.full((8, 128), jnp.sum(spread) / members)
    scale = lax.rsqrt(variance + 1e-05)[:1, :1] * math.sqrt(D / (members * RANK))

    lane = lax.broadcasted_iota(jnp.int32, (32, 128), 1)
    member = lax.broadcasted_iota(jnp.int32, (32, 128), 0) // RANK
    in_first = lax.broadcasted_iota(jnp.int32, (32, IN_BLOCK), 1) < 320
    for near, extra in enumerate(extras):
        for h in range(2):
            index = near * 2 + h
            rows = slice(index * 32, index * 32 + 32)
            level = [
                jnp.sum(jnp.where(lane == member + 64 * f, value, 0.0), axis=1, keepdims=True)
                for f, (value, _) in enumerate(levels[index])
            ]
            fitness = (jnp.where(in_first, level[0], level[1]) - rank_mean) * scale
            base = h * EXTRA
            scaled = fitness * (
                extra[base : base + 32, :].astype(F32) + extra[base + 32 : base + 64, :].astype(F32)
            )
            part = scaled.astype(BF16)
            high[rows, :] = part
            low[rows, :] = (scaled - part.astype(F32)).astype(BF16)
            pair = 2 * lax.rem(y + near, 4) + (xh ^ h)
            for flip in range(2):
                left[flip, rows, :] = lefts[2 * pair + (lax.rem(z, 2) ^ flip)]

    def tn_dot(a, b):
        return lax.dot_general(a, b, (((0,), (0,)), ((), ())), preferred_element_type=F32)

    total[...] = (tn_dot(high[:, :384], left[0]) + tn_dot(low[:, :384], left[0]))[:320]
    total[...] += (tn_dot(high[:, 256:], left[1]) + tn_dot(low[:, 256:], left[1]))[64:]
    for i in range(2):
        here = pl.ds(pl.multiple_of((2 * i + core) * OUT_BLOCK, 8), OUT_BLOCK)
        there = pl.ds(pl.multiple_of((2 * i + 1 - core) * OUT_BLOCK, 8), OUT_BLOCK)
        keep[i] = total[here, :]
        give[i] = total[there, :]


def update_block(place, slots, blocks, xl, members):
    vmem = pl.BlockSpec(memory_space=pltpu.VMEM)
    extra = pl.BlockSpec((LEFT_AT, IN_BLOCK), lambda i: (0, 0))
    shape = jax.ShapeDtypeStruct((2, OUT_BLOCK, IN_BLOCK), F32)
    keep, give = pl.pallas_call(
        functools.partial(update_kernel, members),
        out_shape=(shape, shape),
        grid=(1,),
        in_specs=[pl.BlockSpec(memory_space=pltpu.SMEM)] + [vmem] * 9 + [extra] * 4,
        out_specs=(vmem, vmem),
        scratch_shapes=[
            pltpu.VMEM((16, 32, IN_BLOCK), BF16),
            pltpu.VMEM((2, 256, IN_BLOCK), BF16),
            pltpu.VMEM((256, IN_BLOCK), BF16),
            pltpu.VMEM((256, IN_BLOCK), BF16),
            pltpu.VMEM((320, IN_BLOCK), F32),
        ],
        compiler_params=pltpu.CompilerParams(vmem_limit_bytes=32 * 2**20),
        cost_estimate=pl.CostEstimate(
            flops=8 * 384 * 256 * 640, bytes_accessed=4 * 2**20, transcendentals=0
        ),
    )(place, *slots, *blocks)
    keep = keep + move(give, core_target)
    give = jnp.where(xl == 0, keep[1], keep[0])
    keep = jnp.where(xl == 0, keep[0], keep[1])
    return (keep + move(give, xl_target)).T


def output_kernel(scale, mine, mine_proj, got, right, member, out):
    proj = mine_proj[...] + unpaired(got[:, IN_BLOCK:])
    factor = lax.broadcasted_iota(jnp.int32, (ROWS, 128), 1) // RANK
    coefficient = jnp.where(member[...] == factor, proj, 0.0)[:, :32] * scale
    low_rank = jnp.dot(
        coefficient, right[...], precision=lax.Precision.HIGHEST, preferred_element_type=F32
    )
    out[...] = mine[...] + got[:, :IN_BLOCK].astype(F32) + low_rank


def output_block(mine, mine_proj, got, right_local, member_of):
    vmem = pl.BlockSpec(memory_space=pltpu.VMEM)
    return pl.pallas_call(
        functools.partial(output_kernel, perturb_scale / math.sqrt(RANK)),
        out_shape=jax.ShapeDtypeStruct((ROWS, IN_BLOCK), F32),
        in_specs=[vmem] * 5,
        out_specs=vmem,
        cost_estimate=pl.CostEstimate(
            flops=12 * ROWS * 32 * IN_BLOCK, bytes_accessed=2 * 2**20, transcendentals=0
        ),
    )(mine, mine_proj, got, right_local, member_of.reshape(ROWS, 1))


def on_device(tokens, base_weight, left_factors, right_factors, member_of, ranks):
    z, xl, core, y, xh = (lax.axis_index(name) for name in AXES)
    members = M_DEV * 64
    left = left_factors.astype(BF16).reshape(32, IN_BLOCK)
    offset = (y * 2 + xh) * IN_BLOCK
    right_local = lax.dynamic_slice_in_dim(right_factors, offset, IN_BLOCK, 2).reshape(32, IN_BLOCK)
    slots = spread_columns(base_weight, left, z)
    right = spread_right(right_local, ranks, z)
    blocks, others = spread_rows(tokens, left, right, core)

    place = jnp.stack([z, core, xl ^ xh, y, xh]).astype(jnp.int32)
    total, proj, give = product(place, *slots, *blocks, *others)
    mine, mine_proj, give = join(place, total, proj, move(give, core_target))
    got = move(give, xl_target)
    outputs = output_block(mine, mine_proj, got, right_local, member_of)
    update = update_block(place, slots, blocks, xl, members)
    return (outputs, update)


def solution(mesh):
    fine = Mesh(mesh.devices.reshape(tuple(SIZES.values())), AXES)
    return jax.shard_map(
        on_device,
        mesh=fine,
        in_specs=(
            P(POP, TENSOR),
            P(TENSOR, POP),
            P(POP, None, TENSOR),
            P(POP, None, None),
            P(POP, None),
            P(POP),
        ),
        out_specs=(P(POP, TENSOR), P(TENSOR, POP)),
        check_vma=False,
    )
```

time: 176 us -> 214 us (1.22)
  the two profiles are of different devices: /device:TPU:1 before, /device:TPU:14 now
where the time goes in v4:
time: 214 us; the launch traced here: 213 us
  starting transfers between devices  121 us (57%)
  waiting for transfers between devices  50.3 us (24%)
  local copies, waits for them, and re-layouts  18.3 us (9%)
  Pallas kernels  12.4 us (6%)
  other arithmetic  9.57 us (4%)
    ppermute x26, starting transfers between devices, move(): lax.ppermute(value, AXES, [(flat(p), flat(target(*p))) for p in places])  121 us
    ppermute x26, waiting for transfers between devices, move(): lax.ppermute(value, AXES, [(flat(p), flat(target(*p))) for p in places])  50.3 us
    unnamed x70, local copies, waits for them, and re-layouts  14 us
  transfers between devices with their start and end apart: 26, of which 11 were waited for; matrix products, arithmetic and copies ran while one was open for 5% of the time, Pallas kernels for 5%

profile of v4, /device:TPU:14, one launch (start us, length us, event | category | flops | bytes accessed | tf_op | source)
XLA Modules:
  0.0 213.2 jit_solution(3431355661014621673)
XLA Ops:
  4.5 2.7 %collective-permute-start.11 = (bf16[16,128]{1,0:T(8,128)(2,1)S(1)}, bf16[16,128]{1,0:T(8,128)(2,1)S(1)}, u32[]{:S(2)}, u32[]{:S(2)}) collective-permute-start(bf16[16,128]{1,0:T(8,128)(2,1)S(1)} %fusion.10), channel_id=1, source_target_pairs={{0,16},{1,17},{2,18},{3,19},{4,20},{5,21},{6,22},{7,23},{8,24},{9,... | collective-permute-start | bytes 12296 | tf_op jit(solution)/shard_map/ppermute | solution.py:44
  10.1 12.5 %collective-permute-start.12 = (bf16[80,640]{1,0:T(8,128)(2,1)S(1)}, bf16[80,640]{1,0:T(8,128)(2,1)S(1)}, u32[]{:S(2)}, u32[]{:S(2)}) collective-permute-start(bf16[80,640]{1,0:T(8,128)(2,1)S(1)} %pad_maximum_fusion.3), channel_id=1, source_target_pairs={{0,0},{1,64},{2,128},{3,192},{4,256},{5,320},{6,384},{7,448},{8,8}... | collective-permute-start | bytes 307208 | tf_op jit(solution)/shard_map/ppermute | solution.py:44
  22.7 5.9 %collective-permute-done.12 = bf16[80,640]{1,0:T(8,128)(2,1)S(1)} collective-permute-done((bf16[80,640]{1,0:T(8,128)(2,1)S(1)}, bf16[80,640]{1,0:T(8,128)(2,1)S(1)}, u32[]{:S(2)}, u32[]{:S(2)}) %collective-permute-start.12) | collective-permute-done | bytes 102432 | tf_op jit(solution)/shard_map/ppermute | solution.py:44
  31.6 3.3 %collective-permute-done.13 = bf16[80,320]{1,0:T(8,128)(2,1)S(1)} collective-permute-done((bf16[80,320]{1,0:T(8,128)(2,1)S(1)}, bf16[80,320]{1,0:T(8,128)(2,1)S(1)}, u32[]{:S(2)}, u32[]{:S(2)}) %collective-permute-start.13) | collective-permute-done | bytes 51232 | tf_op jit(solution)/shard_map/ppermute | solution.py:44
  35.0 5.1 %collective-permute-start.14 = (bf16[80,640]{1,0:T(8,128)(2,1)S(1)}, bf16[80,640]{1,0:T(8,128)(2,1)S(1)}, u32[]{:S(2)}, u32[]{:S(2)}) collective-permute-start(bf16[80,640]{1,0:T(8,128)(2,1)S(1)} %get-tuple-element.30), channel_id=1, source_target_pairs={{0,1},{1,0},{2,3},{3,2},{4,5},{5,4},{6,7},{7,6},{8,9},{9,8},{10,11... | collective-permute-start | bytes 307208 | tf_op jit(solution)/shard_map/ppermute | solution.py:44
  43.8 4.8 %collective-permute-done.16 = bf16[224,640]{1,0:T(8,128)(2,1)S(1)} collective-permute-done((bf16[224,640]{1,0:T(8,128)(2,1)S(1)}, bf16[224,640]{1,0:T(8,128)(2,1)S(1)}, u32[]{:S(2)}, u32[]{:S(2)}) %collective-permute-start.16) | collective-permute-done | bytes 286752 | tf_op jit(solution)/shard_map/ppermute | solution.py:44
  50.0 4.8 %collective-permute-start.17 = (bf16[608,640]{1,0:T(8,128)(2,1)S(1)}, bf16[608,640]{1,0:T(8,128)(2,1)S(1)}, u32[]{:S(2)}, u32[]{:S(2)}) collective-permute-start(bf16[608,640]{1,0:T(8,128)(2,1)S(1)} %get-tuple-element.25.refs_9_), channel_id=1, source_target_pairs={{0,6},{1,7},{2,0},{3,1},{4,2},{5,3},{6,4},{7,5},{8,14},{9,15},{10,... | collective-permute-start | bytes 2334728 | tf_op jit(solution)/shard_map/ppermute | solution.py:44
  54.8 4.8 %collective-permute-start.18 = (bf16[608,640]{1,0:T(8,128)(2,1)S(1)}, bf16[608,640]{1,0:T(8,128)(2,1)S(1)}, u32[]{:S(2)}, u32[]{:S(2)}) collective-permute-start(bf16[608,640]{1,0:T(8,128)(2,1)S(1)} %get-tuple-element.25.refs_9_), channel_id=1, source_target_pairs={{0,2},{1,3},{2,4},{3,5},{4,6},{5,7},{6,0},{7,1},{8,10},{9,11},{10,... | collective-permute-start | bytes 2334728 | tf_op jit(solution)/shard_map/ppermute | solution.py:44
  61.2 4.6 %collective-permute-start = (bf16[80,640]{1,0:T(8,128)(2,1)}, bf16[80,640]{1,0:T(8,128)(2,1)S(1)}, u32[]{:S(2)}, u32[]{:S(2)}) collective-permute-start(bf16[80,640]{1,0:T(8,128)(2,1)} %convert_bitcast_fusion), channel_id=1, source_target_pairs={{0,0},{1,16},{2,8},{3,24},{4,256},{5,272},{6,264},{7,280},{8,32},{... | collective-permute-start | bytes 307208 | tf_op jit(solution)/shard_map/ppermute | solution.py:44
  65.8 13.1 %collective-permute-done = bf16[80,640]{1,0:T(8,128)(2,1)S(1)} collective-permute-done((bf16[80,640]{1,0:T(8,128)(2,1)}, bf16[80,640]{1,0:T(8,128)(2,1)S(1)}, u32[]{:S(2)}, u32[]{:S(2)}) %collective-permute-start) | collective-permute-done | bytes 102432 | tf_op jit(solution)/shard_map/ppermute | solution.py:44
  78.9 18.4 %collective-permute-start.1 = (bf16[112,640]{1,0:T(8,128)(2,1)S(1)}, bf16[112,640]{1,0:T(8,128)(2,1)}, u32[]{:S(2)}, u32[]{:S(2)}) collective-permute-start(bf16[112,640]{1,0:T(8,128)(2,1)S(1)} %pad_maximum_fusion), channel_id=1, source_target_pairs={{0,256},{1,257},{2,258},{3,259},{4,260},{5,261},{6,262},{7,263},{8... | collective-permute-start | bytes 430088 | tf_op jit(solution)/shard_map/ppermute | solution.py:44
  98.3 6.5 %collective-permute-start.19 = (bf16[608,640]{1,0:T(8,128)(2,1)}, bf16[608,640]{1,0:T(8,128)(2,1)S(1)}, u32[]{:S(2)}, u32[]{:S(2)}) collective-permute-start(bf16[608,640]{1,0:T(8,128)(2,1)} %broadcast_select_fusion), channel_id=1, source_target_pairs={{0,2},{1,3},{2,4},{3,5},{4,6},{5,7},{6,0},{7,1},{8,14},{9,15},{10,... | collective-permute-start | bytes 2334728 | tf_op jit(solution)/shard_map/ppermute | solution.py:44
  108.0 5.1 %collective-permute-start.3 = (bf16[224,640]{1,0:T(8,128)(2,1)S(1)}, bf16[224,640]{1,0:T(8,128)(2,1)S(1)}, u32[]{:S(2)}, u32[]{:S(2)}) collective-permute-start(bf16[224,640]{1,0:T(8,128)(2,1)S(1)} %maximum_select_fusion.refs_0_), channel_id=1, source_target_pairs={{0,480},{1,481},{2,482},{3,483},{4,484},{5,485},{6,486},{7,487},{8... | collective-permute-start | bytes 860168 | tf_op jit(solution)/shard_map/ppermute | solution.py:44
  113.1 5.2 %collective-permute-done.2.refs_1_ = bf16[224,640]{1,0:T(8,128)(2,1)S(1)} collective-permute-done((bf16[224,640]{1,0:T(8,128)(2,1)S(1)}, bf16[224,640]{1,0:T(8,128)(2,1)S(1)}, u32[]{:S(2)}, u32[]{:S(2)}) %collective-permute-start.2) | collective-permute-done | bytes 286752 | tf_op jit(solution)/shard_map/ppermute | solution.py:44
  120.2 5.4 %collective-permute-start.5 = (bf16[224,640]{1,0:T(8,128)(2,1)S(1)}, bf16[224,640]{1,0:T(8,128)(2,1)S(1)}, u32[]{:S(2)}, u32[]{:S(2)}) collective-permute-start(bf16[224,640]{1,0:T(8,128)(2,1)S(1)} %collective-permute-done.3.refs_2_), channel_id=1, source_target_pairs={{0,480},{1,481},{2,482},{3,483},{4,484},{5,485},{6,486},{7,487},{8... | collective-permute-start | bytes 860168 | tf_op jit(solution)/shard_map/ppermute | solution.py:44
  134.7 5.4 %collective-permute-start.7 = (bf16[224,640]{1,0:T(8,128)(2,1)S(1)}, bf16[224,640]{1,0:T(8,128)(2,1)S(1)}, u32[]{:S(2)}, u32[]{:S(2)}) collective-permute-start(bf16[224,640]{1,0:T(8,128)(2,1)S(1)} %collective-permute-done.5.refs_4_), channel_id=1, source_target_pairs={{0,480},{1,481},{2,482},{3,483},{4,484},{5,485},{6,486},{7,487},{8... | collective-permute-start | bytes 860168 | tf_op jit(solution)/shard_map/ppermute | solution.py:44
  140.9 4.3 %collective-permute-done.6.refs_5_ = bf16[224,640]{1,0:T(8,128)(2,1)S(1)} collective-permute-done((bf16[224,640]{1,0:T(8,128)(2,1)S(1)}, bf16[224,640]{1,0:T(8,128)(2,1)S(1)}, u32[]{:S(2)}, u32[]{:S(2)}) %collective-permute-start.6) | collective-permute-done | bytes 286752 | tf_op jit(solution)/shard_map/ppermute | solution.py:44
  149.9 5.1 %collective-permute-start.9 = (bf16[112,640]{1,0:T(8,128)(2,1)}, bf16[112,640]{1,0:T(8,128)(2,1)}, u32[]{:S(2)}, u32[]{:S(2)}) collective-permute-start(bf16[112,640]{1,0:T(8,128)(2,1)} %slice.76), channel_id=1, source_target_pairs={{0,480},{1,481},{2,482},{3,483},{4,484},{5,485},{6,486},{7,487},{8... | collective-permute-start | bytes 430088 | tf_op jit(solution)/shard_map/ppermute | solution.py:44
  155.2 2.8 %collective-permute-done.9.refs_8_ = bf16[112,640]{1,0:T(8,128)(2,1)} collective-permute-done((bf16[112,640]{1,0:T(8,128)(2,1)}, bf16[112,640]{1,0:T(8,128)(2,1)}, u32[]{:S(2)}, u32[]{:S(2)}) %collective-permute-start.9) | collective-permute-done | bytes 143392 | tf_op jit(solution)/shard_map/ppermute | solution.py:44
  164.9 3.2 %shard_map.80 = (f32[2,80,640]{2,1,0:T(8,128)S(1)}, f32[2,80,640]{2,1,0:T(8,128)}) custom-call(s32[5]{0:T(128)S(1)} %stack.23.place, bf16[224,640]{1,0:T(8,128)(2,1)S(1)} %maximum_select_fusion.refs_0_, bf16[224,640]{1,0:T(8,128)(2,1)S(1)} %copy-done.11, bf16[224,640]{1,0:T(8,128)(2,1)S(1)} %copy-done.14, bf16[224,640]{1,0:T(8,128)(2,1)S(1)} %copy-done.17, ...), custom_call_target="tpu_custom_call" | custom-call | flops 503316480 | bytes 4194304 | tf_op jit(solution)/shard_map/pallas_call | solution.py:325
  170.9 4.1 %shard_map.77 = (f32[384,640]{1,0:T(8,128)S(1)}, f32[384,128]{1,0:T(8,128)S(1)}, bf16[384,768]{1,0:T(8,128)(2,1)}) custom-call(s32[5]{0:T(128)S(1)} %stack.23.place, bf16[224,640]{1,0:T(8,128)(2,1)S(1)} %maximum_select_fusion.refs_0_, bf16[224,640]{1,0:T(8,128)(2,1)S(1)} %copy-done.12, bf16[224,640]{1,0:T(8,128)(2,1)S(1)} %copy-done.15, ...), custom_call_target="tpu_custom_call" | custom-call | flops 1258291200 | bytes 8388608 | tf_op jit(solution)/shard_map/pallas_call | solution.py:163
  180.3 15.5 %collective-permute-start.25 = (f32[80,640]{1,0:T(8,128)S(1)}, f32[80,640]{1,0:T(8,128)S(1)}, u32[]{:S(2)}, u32[]{:S(2)}) collective-permute-start(f32[80,640]{1,0:T(8,128)S(1)} %select_bitcast_fusion), channel_id=1, source_target_pairs={{0,16},{1,17},{2,18},{3,19},{4,20},{5,21},{6,22},{7,23},{8,24},{9,... | collective-permute-start | bytes 614408 | tf_op jit(solution)/shard_map/ppermute | solution.py:44
  202.6 7.3 %collective-permute-done.23.got = bf16[192,768]{1,0:T(8,128)(2,1)S(1)} collective-permute-done((bf16[192,768]{1,0:T(8,128)(2,1)}, bf16[192,768]{1,0:T(8,128)(2,1)S(1)}, u32[]{:S(2)}, u32[]{:S(2)}) %collective-permute-start.23) | collective-permute-done | bytes 294944 | tf_op jit(solution)/shard_map/ppermute | solution.py:44
  210.6 2.6 %shard_map.79 = f32[192,640]{1,0:T(8,128)} custom-call(f32[192,640]{1,0:T(8,128)} %get-tuple-element.13.mine, f32[192,128]{1,0:T(8,128)} %get-tuple-element.14.mine_proj, bf16[192,768]{1,0:T(8,128)(2,1)} %copy-done.30, f32[32,640]{1,0:T(8,128)} %copy-done.26, s32[192,1]{1,0:T(8,128)} %copy.8.member), custom_call_target="tpu_custom_call" | custom-call | flops 47185920 | bytes 2097152 | tf_op jit(solution)/shard_map/pallas_call | solution.py:361
  (135 shorter events, 59.3 us)
Async XLA Ops:
  10.1 18.5 %collective-permute-start.12 = (bf16[80,640]{1,0:T(8,128)(2,1)S(1)}, bf16[80,640]{1,0:T(8,128)(2,1)S(1)}, u32[]{:S(2)}, u32[]{:S(2)}) collective-permute-start(bf16[80,640]{1,0:T(8,128)(2,1)S(1)} %pad_maximum_fusion.3), channel_id=1, source_target_pairs={{0,0},{1,64},{2,128},{3,192},{4,256},{5,320},{6,384},{7,448},{8,8}... | collective-permute-start | bytes 307208 | tf_op jit(solution)/shard_map/ppermute | solution.py:44
  28.7 6.1 %collective-permute-start.13 = (bf16[80,320]{1,0:T(8,128)(2,1)S(1)}, bf16[80,320]{1,0:T(8,128)(2,1)S(1)}, u32[]{:S(2)}, u32[]{:S(2)}) collective-permute-start(bf16[80,320]{1,0:T(8,128)(2,1)S(1)} %get-tuple-element.33), channel_id=1, source_target_pairs={{0,32},{1,33},{2,34},{3,35},{4,36},{5,37},{6,38},{7,39},{8,40},{9,... | collective-permute-start | bytes 153608 | tf_op jit(solution)/shard_map/ppermute | solution.py:44
  30.9 12.3 %collective-permute-start.15 = (bf16[224,640]{1,0:T(8,128)(2,1)S(1)}, bf16[224,640]{1,0:T(8,128)(2,1)S(1)}, u32[]{:S(2)}, u32[]{:S(2)}) collective-permute-start(bf16[224,640]{1,0:T(8,128)(2,1)S(1)} %constant_dynamic-update-slice_fusion), channel_id=1, source_target_pairs={{0,0},{1,16},{2,2},{3,18},{4,4},{5,20},{6,6},{7,22},{8,8},{9,24},{... | collective-permute-start | bytes 860168 | tf_op jit(solution)/shard_map/ppermute | solution.py:44
  35.0 8.2 %collective-permute-start.14 = (bf16[80,640]{1,0:T(8,128)(2,1)S(1)}, bf16[80,640]{1,0:T(8,128)(2,1)S(1)}, u32[]{:S(2)}, u32[]{:S(2)}) collective-permute-start(bf16[80,640]{1,0:T(8,128)(2,1)S(1)} %get-tuple-element.30), channel_id=1, source_target_pairs={{0,1},{1,0},{2,3},{3,2},{4,5},{5,4},{6,7},{7,6},{8,9},{9,8},{10,11... | collective-permute-start | bytes 307208 | tf_op jit(solution)/shard_map/ppermute | solution.py:44
  40.1 8.5 %collective-permute-start.16 = (bf16[224,640]{1,0:T(8,128)(2,1)S(1)}, bf16[224,640]{1,0:T(8,128)(2,1)S(1)}, u32[]{:S(2)}, u32[]{:S(2)}) collective-permute-start(bf16[224,640]{1,0:T(8,128)(2,1)S(1)} %constant_dynamic-update-slice_fusion), channel_id=1, source_target_pairs={{0,1},{1,17},{2,3},{3,19},{4,5},{5,21},{6,7},{7,23},{8,9},{9,25},{... | collective-permute-start | bytes 860168 | tf_op jit(solution)/shard_map/ppermute | solution.py:44
  50.0 47.3 %collective-permute-start.17 = (bf16[608,640]{1,0:T(8,128)(2,1)S(1)}, bf16[608,640]{1,0:T(8,128)(2,1)S(1)}, u32[]{:S(2)}, u32[]{:S(2)}) collective-permute-start(bf16[608,640]{1,0:T(8,128)(2,1)S(1)} %get-tuple-element.25.refs_9_), channel_id=1, source_target_pairs={{0,6},{1,7},{2,0},{3,1},{4,2},{5,3},{6,4},{7,5},{8,14},{9,15},{10,... | collective-permute-start | bytes 2334728 | tf_op jit(solution)/shard_map/ppermute | solution.py:44
  54.8 42.5 %collective-permute-start.18 = (bf16[608,640]{1,0:T(8,128)(2,1)S(1)}, bf16[608,640]{1,0:T(8,128)(2,1)S(1)}, u32[]{:S(2)}, u32[]{:S(2)}) collective-permute-start(bf16[608,640]{1,0:T(8,128)(2,1)S(1)} %get-tuple-element.25.refs_9_), channel_id=1, source_target_pairs={{0,2},{1,3},{2,4},{3,5},{4,6},{5,7},{6,0},{7,1},{8,10},{9,11},{10,... | collective-permute-start | bytes 2334728 | tf_op jit(solution)/shard_map/ppermute | solution.py:44
  61.2 17.7 %collective-permute-start = (bf16[80,640]{1,0:T(8,128)(2,1)}, bf16[80,640]{1,0:T(8,128)(2,1)S(1)}, u32[]{:S(2)}, u32[]{:S(2)}) collective-permute-start(bf16[80,640]{1,0:T(8,128)(2,1)} %convert_bitcast_fusion), channel_id=1, source_target_pairs={{0,0},{1,16},{2,8},{3,24},{4,256},{5,272},{6,264},{7,280},{8,32},{... | collective-permute-start | bytes 307208 | tf_op jit(solution)/shard_map/ppermute | solution.py:44
  78.9 25.9 %collective-permute-start.1 = (bf16[112,640]{1,0:T(8,128)(2,1)S(1)}, bf16[112,640]{1,0:T(8,128)(2,1)}, u32[]{:S(2)}, u32[]{:S(2)}) collective-permute-start(bf16[112,640]{1,0:T(8,128)(2,1)S(1)} %pad_maximum_fusion), channel_id=1, source_target_pairs={{0,256},{1,257},{2,258},{3,259},{4,260},{5,261},{6,262},{7,263},{8... | collective-permute-start | bytes 430088 | tf_op jit(solution)/shard_map/ppermute | solution.py:44
  98.3 31.1 %collective-permute-start.19 = (bf16[608,640]{1,0:T(8,128)(2,1)}, bf16[608,640]{1,0:T(8,128)(2,1)S(1)}, u32[]{:S(2)}, u32[]{:S(2)}) collective-permute-start(bf16[608,640]{1,0:T(8,128)(2,1)} %broadcast_select_fusion), channel_id=1, source_target_pairs={{0,2},{1,3},{2,4},{3,5},{4,6},{5,7},{6,0},{7,1},{8,14},{9,15},{10,... | collective-permute-start | bytes 2334728 | tf_op jit(solution)/shard_map/ppermute | solution.py:44
  106.0 12.2 %collective-permute-start.2 = (bf16[224,640]{1,0:T(8,128)(2,1)S(1)}, bf16[224,640]{1,0:T(8,128)(2,1)S(1)}, u32[]{:S(2)}, u32[]{:S(2)}) collective-permute-start(bf16[224,640]{1,0:T(8,128)(2,1)S(1)} %maximum_select_fusion.refs_0_), channel_id=1, source_target_pairs={{0,32},{1,33},{2,34},{3,35},{4,36},{5,37},{6,38},{7,39},{8,40},{9,... | collective-permute-start | bytes 860168 | tf_op jit(solution)/shard_map/ppermute | solution.py:44
  108.0 12.2 %collective-permute-start.3 = (bf16[224,640]{1,0:T(8,128)(2,1)S(1)}, bf16[224,640]{1,0:T(8,128)(2,1)S(1)}, u32[]{:S(2)}, u32[]{:S(2)}) collective-permute-start(bf16[224,640]{1,0:T(8,128)(2,1)S(1)} %maximum_select_fusion.refs_0_), channel_id=1, source_target_pairs={{0,480},{1,481},{2,482},{3,483},{4,484},{5,485},{6,486},{7,487},{8... | collective-permute-start | bytes 860168 | tf_op jit(solution)/shard_map/ppermute | solution.py:44
  118.3 14.5 %collective-permute-start.4 = (bf16[224,640]{1,0:T(8,128)(2,1)S(1)}, bf16[224,640]{1,0:T(8,128)(2,1)S(1)}, u32[]{:S(2)}, u32[]{:S(2)}) collective-permute-start(bf16[224,640]{1,0:T(8,128)(2,1)S(1)} %collective-permute-done.2.refs_1_), channel_id=1, source_target_pairs={{0,32},{1,33},{2,34},{3,35},{4,36},{5,37},{6,38},{7,39},{8,40},{9,... | collective-permute-start | bytes 860168 | tf_op jit(solution)/shard_map/ppermute | solution.py:44
  120.2 14.5 %collective-permute-start.5 = (bf16[224,640]{1,0:T(8,128)(2,1)S(1)}, bf16[224,640]{1,0:T(8,128)(2,1)S(1)}, u32[]{:S(2)}, u32[]{:S(2)}) collective-permute-start(bf16[224,640]{1,0:T(8,128)(2,1)S(1)} %collective-permute-done.3.refs_2_), channel_id=1, source_target_pairs={{0,480},{1,481},{2,482},{3,483},{4,484},{5,485},{6,486},{7,487},{8... | collective-permute-start | bytes 860168 | tf_op jit(solution)/shard_map/ppermute | solution.py:44
  127.5 43.3 %collective-permute-start.20 = (bf16[448,640]{1,0:T(8,128)(2,1)}, bf16[448,640]{1,0:T(8,128)(2,1)}, u32[]{:S(2)}, u32[]{:S(2)}) collective-permute-start(bf16[448,640]{1,0:T(8,128)(2,1)} %slice_select_fusion.1), channel_id=1, source_target_pairs={{0,8},{1,9},{2,10},{3,11},{4,12},{5,13},{6,14},{7,15},{8,0},{9,1},... | collective-permute-start | bytes 1720328 | tf_op jit(solution)/shard_map/ppermute | solution.py:44
  130.4 40.5 %collective-permute-start.21 = (bf16[448,640]{1,0:T(8,128)(2,1)}, bf16[448,640]{1,0:T(8,128)(2,1)}, u32[]{:S(2)}, u32[]{:S(2)}) collective-permute-start(bf16[448,640]{1,0:T(8,128)(2,1)} %slice_select_fusion), channel_id=1, source_target_pairs={{0,8},{1,9},{2,10},{3,11},{4,12},{5,13},{6,14},{7,15},{8,0},{9,1},... | collective-permute-start | bytes 1720328 | tf_op jit(solution)/shard_map/ppermute | solution.py:44
  132.8 12.4 %collective-permute-start.6 = (bf16[224,640]{1,0:T(8,128)(2,1)S(1)}, bf16[224,640]{1,0:T(8,128)(2,1)S(1)}, u32[]{:S(2)}, u32[]{:S(2)}) collective-permute-start(bf16[224,640]{1,0:T(8,128)(2,1)S(1)} %collective-permute-done.4.refs_3_), channel_id=1, source_target_pairs={{0,32},{1,33},{2,34},{3,35},{4,36},{5,37},{6,38},{7,39},{8,40},{9,... | collective-permute-start | bytes 860168 | tf_op jit(solution)/shard_map/ppermute | solution.py:44
  134.7 13.8 %collective-permute-start.7 = (bf16[224,640]{1,0:T(8,128)(2,1)S(1)}, bf16[224,640]{1,0:T(8,128)(2,1)S(1)}, u32[]{:S(2)}, u32[]{:S(2)}) collective-permute-start(bf16[224,640]{1,0:T(8,128)(2,1)S(1)} %collective-permute-done.5.refs_4_), channel_id=1, source_target_pairs={{0,480},{1,481},{2,482},{3,483},{4,484},{5,485},{6,486},{7,487},{8... | collective-permute-start | bytes 860168 | tf_op jit(solution)/shard_map/ppermute | solution.py:44
  146.6 8.6 %collective-permute-start.8 = (bf16[112,640]{1,0:T(8,128)(2,1)}, bf16[112,640]{1,0:T(8,128)(2,1)S(1)}, u32[]{:S(2)}, u32[]{:S(2)}) collective-permute-start(bf16[112,640]{1,0:T(8,128)(2,1)} %slice.75), channel_id=1, source_target_pairs={{0,32},{1,33},{2,34},{3,35},{4,36},{5,37},{6,38},{7,39},{8,40},{9,... | collective-permute-start | bytes 430088 | tf_op jit(solution)/shard_map/ppermute | solution.py:44
  149.9 8.1 %collective-permute-start.9 = (bf16[112,640]{1,0:T(8,128)(2,1)}, bf16[112,640]{1,0:T(8,128)(2,1)}, u32[]{:S(2)}, u32[]{:S(2)}) collective-permute-start(bf16[112,640]{1,0:T(8,128)(2,1)} %slice.76), channel_id=1, source_target_pairs={{0,480},{1,481},{2,482},{3,483},{4,484},{5,485},{6,486},{7,487},{8... | collective-permute-start | bytes 430088 | tf_op jit(solution)/shard_map/ppermute | solution.py:44
  168.9 10.2 %collective-permute-start.24 = (f32[2,80,640]{2,1,0:T(8,128)}, f32[2,80,640]{2,1,0:T(8,128)}, u32[]{:S(2)}, u32[]{:S(2)}) collective-permute-start(f32[2,80,640]{2,1,0:T(8,128)} %get-tuple-element.17), channel_id=1, source_target_pairs={{0,8},{1,9},{2,10},{3,11},{4,12},{5,13},{6,14},{7,15},{8,0},{9,1},... | collective-permute-start | bytes 1228808 | tf_op jit(solution)/shard_map/ppermute | solution.py:44
  176.7 19.1 %collective-permute-start.22 = (bf16[384,768]{1,0:T(8,128)(2,1)}, bf16[384,768]{1,0:T(8,128)(2,1)S(1)}, u32[]{:S(2)}, u32[]{:S(2)}) collective-permute-start(bf16[384,768]{1,0:T(8,128)(2,1)} %get-tuple-element.12), channel_id=1, source_target_pairs={{0,8},{1,9},{2,10},{3,11},{4,12},{5,13},{6,14},{7,15},{8,0},{9,1},... | collective-permute-start | bytes 1769480 | tf_op jit(solution)/shard_map/ppermute | solution.py:44
  180.3 21.5 %collective-permute-start.25 = (f32[80,640]{1,0:T(8,128)S(1)}, f32[80,640]{1,0:T(8,128)S(1)}, u32[]{:S(2)}, u32[]{:S(2)}) collective-permute-start(f32[80,640]{1,0:T(8,128)S(1)} %select_bitcast_fusion), channel_id=1, source_target_pairs={{0,16},{1,17},{2,18},{3,19},{4,20},{5,21},{6,22},{7,23},{8,24},{9,... | collective-permute-start | bytes 614408 | tf_op jit(solution)/shard_map/ppermute | solution.py:44
  199.2 10.7 %collective-permute-start.23 = (bf16[192,768]{1,0:T(8,128)(2,1)}, bf16[192,768]{1,0:T(8,128)(2,1)S(1)}, u32[]{:S(2)}, u32[]{:S(2)}) collective-permute-start(bf16[192,768]{1,0:T(8,128)(2,1)} %get-tuple-element.15), channel_id=1, source_target_pairs={{0,16},{1,17},{2,18},{3,19},{4,20},{5,21},{6,22},{7,23},{8,24},{9,... | collective-permute-start | bytes 884744 | tf_op jit(solution)/shard_map/ppermute | solution.py:44
  (36 other events, 319.5 us)

commit v5 on v4

v5 whole, which is shorter than its diff:
```python
import functools
import itertools
import math

import jax
import jax.numpy as jnp
from jax import lax
from jax.experimental import pallas as pl
from jax.experimental.pallas import tpu as pltpu
from jax.sharding import Mesh
from jax.sharding import PartitionSpec as P

D = 5120
RANK = 4
M_DEV = 8
ROWS = 192
IN_BLOCK = 640
OUT_BLOCK = 80
SLOT = 112
EXTRA = 80
SEND = IN_BLOCK + 128

perturb_scale = 0.5

SIZES = {"z": 16, "xl": 2, "core": 2, "y": 4, "xh": 2}
AXES = tuple(SIZES)
POP = ("z", "xl", "core")
TENSOR = ("y", "xh")
BF16 = jnp.bfloat16
F32 = jnp.float32


def flat(place):
    index = 0
    for value, size in zip(place, SIZES.values()):
        index = index * size + value % size
    return index


def move(value, target):
    places = itertools.product(*(range(n) for n in SIZES.values()))
    return lax.ppermute(value, AXES, [(flat(p), flat(target(*p))) for p in places])


def weight_target(z, xl, core, y, xh):
    owner = z // 2
    to_y, to_xh = owner // 2, owner % 2
    column = (z % 2) * 4 + xl * 2 + core
    near = (y - to_y) % 4
    return ((near % 2) * 8 + column, xh, near // 2, to_y, to_xh)


def right_target(z, xl, core, y, xh):
    return (2 * (2 * y + xh) + z % 2, xl, core, z // 4, z // 2 % 2)


def rows_target(flip, z, xl, core, y, xh):
    return (z, xh, core, y, xl ^ flip)


def z_target(step, z, xl, core, y, xh):
    return (z + step, xl, core, y, xh)


def core_target(z, xl, core, y, xh):
    return (z, xl, 1 - core, y, xh)


def z_pair_target(z, xl, core, y, xh):
    return (z ^ 1, xl, core, y, xh)


def xh_target(z, xl, core, y, xh):
    return (z, xl, core, y, 1 - xh)


def xl_target(z, xl, core, y, xh):
    return (z, 1 - xl, core, y, xh)


def y_pair_target(z, xl, core, y, xh):
    return (z, xl, core, y ^ 1, xh)


def y_half_target(z, xl, core, y, xh):
    return (z, xl, core, y + 2, xh)


def y_apart_target(z, xl, core, y, xh):
    return (z, xl, core, y + (1 if core else -1), xh)


def y_forward_target(z, xl, core, y, xh):
    return (z, xl, core, y + core, xh)


def nt_dot(a, b):
    return lax.dot_general(a, b, (((1,), (1,)), ((), ())), preferred_element_type=F32)


def split(value):
    high = lax.reduce_precision(value, 8, 7)
    return high.astype(BF16), (value - high).astype(BF16)


def paired(proj):
    lane = lax.broadcasted_iota(jnp.int32, proj.shape, 1)
    first = jnp.where(lane < 32, proj, 0.0)
    high = first.astype(BF16).astype(F32)
    return (high + pltpu.roll(first - high, 32, 1)).astype(BF16)


def unpaired(value):
    value = value.astype(F32)
    return value + pltpu.roll(value, 96, 1)


def main_kernel(members, place, *refs):
    slots, near, step, forward, right = refs[:5]
    mine, mine_proj, keep, give = refs[5:9]
    weights, rows, left, high, low, total = refs[9:]
    core = place[1]
    for half in range(2):
        for column in range(8):
            start = (half * 8 + column) * SLOT
            at = slice(column * OUT_BLOCK, (column + 1) * OUT_BLOCK)
            weights[half, at, :] = slots[start : start + OUT_BLOCK, :]

    @pl.when(core == 0)
    def _():
        rows[...] = near[...]

    @pl.when(core == 1)
    def _():
        rows[...] = forward[...]

    def sums(base):
        x = slice(base + 64, base + 64 + 2 * ROWS)
        block = nt_dot(rows[x, :], weights[0]) + nt_dot(step[x, :], weights[1])
        proj = []
        for m in range(2):
            part = 0.0
            for ref in (rows, step):
                factor = ref[base + m * 32 : base + m * 32 + 32, :]
                x = slice(base + 64 + m * ROWS, base + 64 + (m + 1) * ROWS)
                part = part + nt_dot(ref[x, :], jnp.concatenate([factor] * 4))
            proj.append(part)
        return block, jnp.concatenate(proj)

    block, proj = sums(2 * ROWS + 64)
    give[: 2 * ROWS, :IN_BLOCK] = block.astype(BF16)
    give[: 2 * ROWS, IN_BLOCK:] = paired(proj)
    block, proj = sums(0)
    mine[...] = block
    mine_proj[...] = proj

    update_sums(members, place, slots, right, left, high, low, total)
    for i in range(2):
        here = pl.ds(pl.multiple_of((2 * i + core) * OUT_BLOCK, 8), OUT_BLOCK)
        there = pl.ds(pl.multiple_of((2 * i + 1 - core) * OUT_BLOCK, 8), OUT_BLOCK)
        keep[i * OUT_BLOCK : (i + 1) * OUT_BLOCK, :] = total[here, :]
        put_pair(give, 2 * ROWS + 2 * i * OUT_BLOCK, total[there, :])


def put_pair(ref, start, value):
    part = value.astype(BF16)
    ref[start : start + OUT_BLOCK, :IN_BLOCK] = part
    ref[start + OUT_BLOCK : start + 2 * OUT_BLOCK, :IN_BLOCK] = (value - part.astype(F32)).astype(BF16)
    ref[start : start + 2 * OUT_BLOCK, IN_BLOCK:] = jnp.zeros((2 * OUT_BLOCK, SEND - IN_BLOCK), BF16)


def take_pair(ref, start):
    block = ref[start : start + 2 * OUT_BLOCK, :IN_BLOCK].astype(F32)
    return block[:OUT_BLOCK] + block[OUT_BLOCK:]


def main(place, members, *arrays):
    vmem = pl.BlockSpec(memory_space=pltpu.VMEM)
    return pl.pallas_call(
        functools.partial(main_kernel, members),
        out_shape=(
            jax.ShapeDtypeStruct((2 * ROWS, IN_BLOCK), F32),
            jax.ShapeDtypeStruct((2 * ROWS, 128), F32),
            jax.ShapeDtypeStruct((2 * OUT_BLOCK, IN_BLOCK), F32),
            jax.ShapeDtypeStruct((2 * ROWS + 4 * OUT_BLOCK, SEND), BF16),
        ),
        in_specs=[pl.BlockSpec(memory_space=pltpu.SMEM)] + [vmem] * len(arrays),
        out_specs=(vmem,) * 4,
        scratch_shapes=[
            pltpu.VMEM((2, IN_BLOCK, IN_BLOCK), BF16),
            pltpu.VMEM((2 * (64 + 2 * ROWS), IN_BLOCK), BF16),
            pltpu.VMEM((2, 256, IN_BLOCK), BF16),
            pltpu.VMEM((256, IN_BLOCK), BF16),
            pltpu.VMEM((256, IN_BLOCK), BF16),
            pltpu.VMEM((320, IN_BLOCK), F32),
        ],
        compiler_params=pltpu.CompilerParams(vmem_limit_bytes=56 * 2**20),
        cost_estimate=pl.CostEstimate(
            flops=2 * 768 * 640 * 1280, bytes_accessed=10 * 2**20, transcendentals=0
        ),
    )(place, *arrays)


def join_kernel(place, total, proj, keep, got, mine, mine_proj, mine_update, give):
    own, xl = place[2], place[5]
    for block, to_give in ((own, False), (1 - own, True)):
        at = pl.ds(pl.multiple_of(block * ROWS, ROWS), ROWS)
        value = total[at, :] + got[at, :IN_BLOCK].astype(F32)
        sums = proj[at, :] + unpaired(got[at, IN_BLOCK:])
        if to_give:
            give[:ROWS, :IN_BLOCK] = value.astype(BF16)
            give[:ROWS, IN_BLOCK:] = paired(sums)
        else:
            mine[...] = value
            mine_proj[...] = sums
    update = [
        keep[i * OUT_BLOCK : (i + 1) * OUT_BLOCK, :] + take_pair(got, 2 * ROWS + 2 * i * OUT_BLOCK)
        for i in range(2)
    ]
    mine_update[...] = jnp.where(xl == 0, update[0], update[1])
    put_pair(give, ROWS, jnp.where(xl == 0, update[1], update[0]))


def join(place, total, proj, keep, got):
    vmem = pl.BlockSpec(memory_space=pltpu.VMEM)
    return pl.pallas_call(
        join_kernel,
        out_shape=(
            jax.ShapeDtypeStruct((ROWS, IN_BLOCK), F32),
            jax.ShapeDtypeStruct((ROWS, 128), F32),
            jax.ShapeDtypeStruct((OUT_BLOCK, IN_BLOCK), F32),
            jax.ShapeDtypeStruct((ROWS + 2 * OUT_BLOCK, SEND), BF16),
        ),
        in_specs=[pl.BlockSpec(memory_space=pltpu.SMEM)] + [vmem] * 4,
        out_specs=(vmem,) * 4,
        compiler_params=pltpu.CompilerParams(vmem_limit_bytes=56 * 2**20),
        cost_estimate=pl.CostEstimate(flops=10**6, bytes_accessed=4 * 2**20, transcendentals=0),
    )(place, total, proj, keep, got)


def after(value, other):
    there = other[0, 0] == other[0, 0]
    return jnp.where(there, value, jnp.zeros_like(value))


def rank_row(ranks):
    own = jnp.pad(ranks.astype(BF16)[None, :], ((0, 15), (0, 120)))
    every = lax.all_gather(own, ("xl", "core"), axis=1, tiled=True)
    every = jnp.concatenate([every[:, g * 128 : g * 128 + M_DEV] for g in range(4)], 1)
    return jnp.pad(every, ((0, 0), (0, IN_BLOCK - 4 * M_DEV)))


def spread_right(right_local, ranks, slot, z):
    sent = jnp.concatenate([*split(right_local), rank_row(ranks)])
    got = move(sent, right_target)
    odd = z % 2 == 1
    levels = got[64:, :320]
    own = jnp.where(odd, got[:64, 320:], got[:64, :320])
    other = jnp.where(odd, got[:64, :320], got[:64, 320:])
    pair = move(after(jnp.concatenate([other, levels]), slot), z_pair_target)
    held = jnp.concatenate([jnp.concatenate([own, levels]), pair], 1)
    for target in (xh_target, y_pair_target, y_half_target):
        held = jnp.concatenate([held, move(held, target)])
    return held


def spread_rows(tokens, left, slot):
    payload = after(jnp.concatenate([left, tokens]), slot)
    a = move(payload, functools.partial(rows_target, 0))
    b = move(payload, functools.partial(rows_target, 1))
    near = jnp.concatenate([a[:32], b[:32], a[32:], b[32:]])
    near = jnp.concatenate([near, move(near, core_target)])
    step = move(near, y_apart_target)
    return near, step, move(step, y_forward_target)


def update_sums(members, place, slots, right, left, high, low, total):
    z, core, y, xh, xl = place[0], place[1], place[3], place[4], place[5]
    blocks = [(far, pair, h) for far in range(2) for pair in range(2) for h in range(2)]
    lane = lax.broadcasted_iota(jnp.int32, (1, 128), 1)
    levels, spread, rank_sum = [], 0.0, 0.0
    for index in range(8):
        row = right[index * EXTRA + 64 : index * EXTRA + EXTRA, :384].astype(F32)[:1, :]
        pair = [
            (row[:, 256 * f : 256 * f + 128], jnp.logical_and(lane >= 64 * f, lane < 64 * f + 32))
            for f in range(2)
        ]
        levels.append(pair)
    for value, valid in sum(levels, []):
        rank_sum = rank_sum + jnp.where(valid, value, 0.0)
    rank_mean = jnp.sum(rank_sum) / members
    for value, valid in sum(levels, []):
        spread = spread + jnp.where(valid, (value - rank_mean) ** 2, 0.0)
    variance = jnp.full((8, 128), jnp.sum(spread) / members)
    scale = lax.rsqrt(variance + 1e-05)[:1, :1] * math.sqrt(D / (members * RANK))

    lane = lax.broadcasted_iota(jnp.int32, (32, 128), 1)
    member = lax.broadcasted_iota(jnp.int32, (32, 128), 0) // RANK
    in_first = lax.broadcasted_iota(jnp.int32, (32, IN_BLOCK), 1) < 320
    for index, (far, pair, h) in enumerate(blocks):
        rows = slice(index * 32, index * 32 + 32)
        own = member + 8 * (2 * xl + core)
        level = [
            jnp.sum(jnp.where(lane == own + 64 * f, value, 0.0), axis=1, keepdims=True)
            for f, (value, _) in enumerate(levels[index])
        ]
        fitness = (jnp.where(in_first, level[0], level[1]) - rank_mean) * scale
        base = index * EXTRA
        scaled = fitness * (
            right[base : base + 32, :].astype(F32) + right[base + 32 : base + 64, :].astype(F32)
        )
        part = scaled.astype(BF16)
        high[rows, :] = part
        low[rows, :] = (scaled - part.astype(F32)).astype(BF16)
        source = 2 * lax.rem((y ^ pair) + 2 * far, 4) + (xh ^ h)
        for flip in range(2):
            start = (2 * source + (lax.rem(z, 2) ^ flip)) * SLOT + OUT_BLOCK
            left[flip, rows, :] = slots[pl.ds(pl.multiple_of(start, 16), 32), :]

    def tn_dot(a, b):
        return lax.dot_general(a, b, (((0,), (0,)), ((), ())), preferred_element_type=F32)

    total[...] = (tn_dot(high[:, :384], left[0]) + tn_dot(low[:, :384], left[0]))[:320]
    total[...] += (tn_dot(high[:, 256:], left[1]) + tn_dot(low[:, 256:], left[1]))[64:]

def output_kernel(scale, mine, mine_proj, mine_update, got, right, member, out, update):
    proj = mine_proj[...] + unpaired(got[:ROWS, IN_BLOCK:])
    factor = lax.broadcasted_iota(jnp.int32, (ROWS, 128), 1) // RANK
    coefficient = jnp.where(member[...] == factor, proj, 0.0)[:, :32] * scale
    low_rank = jnp.dot(
        coefficient, right[...], precision=lax.Precision.HIGHEST, preferred_element_type=F32
    )
    out[...] = mine[...] + got[:ROWS, :IN_BLOCK].astype(F32) + low_rank
    update[...] = mine_update[...] + take_pair(got, ROWS)


def finish(mine, mine_proj, mine_update, got, right_local, member_of):
    vmem = pl.BlockSpec(memory_space=pltpu.VMEM)
    return pl.pallas_call(
        functools.partial(output_kernel, perturb_scale / math.sqrt(RANK)),
        out_shape=(
            jax.ShapeDtypeStruct((ROWS, IN_BLOCK), F32),
            jax.ShapeDtypeStruct((OUT_BLOCK, IN_BLOCK), F32),
        ),
        in_specs=[vmem] * 6,
        out_specs=(vmem, vmem),
        compiler_params=pltpu.CompilerParams(vmem_limit_bytes=56 * 2**20),
        cost_estimate=pl.CostEstimate(
            flops=12 * ROWS * 32 * IN_BLOCK, bytes_accessed=3 * 2**20, transcendentals=0
        ),
    )(mine, mine_proj, mine_update, got, right_local, member_of.reshape(ROWS, 1))


def on_device(tokens, base_weight, left_factors, right_factors, member_of, ranks):
    z, xl, core, y, xh = (lax.axis_index(name) for name in AXES)
    members = M_DEV * 64
    left = left_factors.astype(BF16).reshape(32, IN_BLOCK)
    offset = (y * 2 + xh) * IN_BLOCK
    right_local = lax.dynamic_slice_in_dim(right_factors, offset, IN_BLOCK, 2).reshape(32, IN_BLOCK)
    slot = jnp.concatenate([move(base_weight.T.astype(BF16), weight_target), left])
    slots = lax.all_gather(slot, "z", axis=0, tiled=True)
    rows = spread_rows(tokens, left, slot)
    right = spread_right(right_local, ranks, slot, z)

    place = jnp.stack([z, core, xl ^ xh, y, xh, xl]).astype(jnp.int32)
    total, proj, keep, give = main(place, members, slots, *rows, right)
    mine, mine_proj, mine_update, give = join(place, total, proj, keep, move(give, core_target))
    got = move(give, xl_target)
    outputs, update = finish(mine, mine_proj, mine_update, got, right_local, member_of)
    return (outputs, update.T)


def solution(mesh):
    fine = Mesh(mesh.devices.reshape(tuple(SIZES.values())), AXES)
    return jax.shard_map(
        on_device,
        mesh=fine,
        in_specs=(
            P(POP, TENSOR),
            P(TENSOR, POP),
            P(POP, None, TENSOR),
            P(POP, None, None),
            P(POP, None),
            P(POP),
        ),
        out_specs=(P(POP, TENSOR), P(TENSOR, POP)),
        check_vma=False,
    )
```

time: 214 us -> 173 us (0.81)
  the two profiles are of different devices: /device:TPU:14 before, /device:TPU:30 now
where the time goes in v5:
time: 173 us; the launch traced here: 172 us
  waiting for transfers between devices  71.4 us (41%)
  starting transfers between devices  53.1 us (31%)
  between operations  15.7 us (9%)
  Pallas kernels  13.2 us (8%)
  blocking collectives  7.57 us (4%)
  other arithmetic  6.91 us (4%)
  local copies, waits for them, and re-layouts  4 us (2%)
    ppermute x13, waiting for transfers between devices, move(): lax.ppermute(value, AXES, [(flat(p), flat(target(*p))) for p in places])  71.4 us
    ppermute x13, starting transfers between devices, move(): lax.ppermute(value, AXES, [(flat(p), flat(target(*p))) for p in places])  53.1 us
    all_gather x1, blocking collectives, rank_row(): every = lax.all_gather(own, ('xl', 'core'), axis=1, tiled=True)  7.57 us
    pallas_call x1, Pallas kernels, main(): pl.pallas_call(functools.partial(main_kernel, members), out_shape=(jax.Sh...  7.47 us
  transfers between devices with their start and end apart: 14, of which 9 were waited for; matrix products, arithmetic and copies ran while one was open for 4% of the time, Pallas kernels for 0%

profile of v5, /device:TPU:30, one launch (start us, length us, event | category | flops | bytes accessed | tf_op | source)
XLA Modules:
  0.0 172.0 jit_solution(10612060843864728305)
XLA Ops:
  8.2 14.8 %collective-permute-start = (bf16[80,640]{1,0:T(8,128)(2,1)S(1)}, bf16[80,640]{1,0:T(8,128)(2,1)S(1)}, u32[]{:S(2)}, u32[]{:S(2)}) collective-permute-start(bf16[80,640]{1,0:T(8,128)(2,1)S(1)} %convert_bitcast_fusion), channel_id=1, source_target_pairs={{0,0},{1,16},{2,256},{3,272},{4,8},{5,24},{6,264},{7,280},{8,32},{... | collective-permute-start | bytes 307208 | tf_op jit(solution)/shard_map/ppermute | solution.py:42
  23.9 4.7 %collective-permute-done = bf16[80,640]{1,0:T(8,128)(2,1)S(1)} collective-permute-done((bf16[80,640]{1,0:T(8,128)(2,1)S(1)}, bf16[80,640]{1,0:T(8,128)(2,1)S(1)}, u32[]{:S(2)}, u32[]{:S(2)}) %collective-permute-start) | collective-permute-done | bytes 102432 | tf_op jit(solution)/shard_map/ppermute | solution.py:42
  32.8 3.7 %collective-permute-start.2 = (bf16[224,640]{1,0:T(8,128)(2,1)S(1)}, bf16[224,640]{1,0:T(8,128)(2,1)S(1)}, u32[]{:S(2)}, u32[]{:S(2)}) collective-permute-start(bf16[224,640]{1,0:T(8,128)(2,1)S(1)} %maximum_select_fusion), channel_id=1, source_target_pairs={{0,1},{1,17},{2,3},{3,19},{4,5},{5,21},{6,7},{7,23},{8,9},{9,25},{... | collective-permute-start | bytes 860168 | tf_op jit(solution)/shard_map/ppermute | solution.py:42
  36.6 7.1 %collective-permute-done.2 = bf16[224,640]{1,0:T(8,128)(2,1)S(1)} collective-permute-done((bf16[224,640]{1,0:T(8,128)(2,1)S(1)}, bf16[224,640]{1,0:T(8,128)(2,1)S(1)}, u32[]{:S(2)}, u32[]{:S(2)}) %collective-permute-start.2) | collective-permute-done | bytes 286752 | tf_op jit(solution)/shard_map/ppermute | solution.py:42
  43.8 1.9 %collective-permute-start.3 = (bf16[448,640]{1,0:T(8,128)(2,1)S(1)}, bf16[448,640]{1,0:T(8,128)(2,1)S(1)}, u32[]{:S(2)}, u32[]{:S(2)}) collective-permute-start(bf16[448,640]{1,0:T(8,128)(2,1)S(1)} %pad_maximum_fusion.1), channel_id=1, source_target_pairs={{0,8},{1,9},{2,10},{3,11},{4,12},{5,13},{6,14},{7,15},{8,0},{9,1},... | collective-permute-start | bytes 1720328 | tf_op jit(solution)/shard_map/ppermute | solution.py:42
  45.9 7.6 %all_gather.7 = bf16[16,512]{1,0:T(8,128)(2,1)S(1)} all-gather(bf16[16,128]{1,0:T(8,128)(2,1)S(1)} %pad.8), channel_id=1, replica_groups=mesh['z'=16,'xl'=2,'core'=2,'y'=4,'xh'=2] {'xl','core'}, dimensions={1}, use_global_device_ids=true | all-gather | bytes 20480 | tf_op jit(solution)/shard_map/all_gather | solution.py:248
  53.6 3.0 %collective-permute-start.4 = (bf16[896,640]{1,0:T(8,128)(2,1)S(1)}, bf16[896,640]{1,0:T(8,128)(2,1)S(1)}, u32[]{:S(2)}, u32[]{:S(2)}) collective-permute-start(bf16[896,640]{1,0:T(8,128)(2,1)S(1)} %constant_dynamic-update-slice_fusion.refs_1_), channel_id=1, source_target_pairs={{0,6},{1,7},{2,0},{3,1},{4,2},{5,3},{6,4},{7,5},{8,10},{9,11},{10,... | collective-permute-start | bytes 3440648 | tf_op jit(solution)/shard_map/ppermute | solution.py:42
  56.7 10.0 %collective-permute-start.6 = (bf16[80,640]{1,0:T(8,128)(2,1)S(1)}, bf16[80,640]{1,0:T(8,128)(2,1)S(1)}, u32[]{:S(2)}, u32[]{:S(2)}) collective-permute-start(bf16[80,640]{1,0:T(8,128)(2,1)S(1)} %pad_maximum_fusion.5), channel_id=1, source_target_pairs={{0,0},{1,64},{2,128},{3,192},{4,256},{5,320},{6,384},{7,448},{8,8}... | collective-permute-start | bytes 307208 | tf_op jit(solution)/shard_map/ppermute | solution.py:42
  66.8 15.9 %collective-permute-done.6 = bf16[80,640]{1,0:T(8,128)(2,1)S(1)} collective-permute-done((bf16[80,640]{1,0:T(8,128)(2,1)S(1)}, bf16[80,640]{1,0:T(8,128)(2,1)S(1)}, u32[]{:S(2)}, u32[]{:S(2)}) %collective-permute-start.6) | collective-permute-done | bytes 102432 | tf_op jit(solution)/shard_map/ppermute | solution.py:42
  82.8 7.1 %collective-permute-start.7 = (bf16[80,320]{1,0:T(8,128)(2,1)S(1)}, bf16[80,320]{1,0:T(8,128)(2,1)S(1)}, u32[]{:S(2)}, u32[]{:S(2)}) collective-permute-start(bf16[80,320]{1,0:T(8,128)(2,1)S(1)} %maximum_select_fusion.1), channel_id=1, source_target_pairs={{0,32},{1,33},{2,34},{3,35},{4,36},{5,37},{6,38},{7,39},{8,40},{9,... | collective-permute-start | bytes 153608 | tf_op jit(solution)/shard_map/ppermute | solution.py:42
  92.4 1.9 %collective-permute-start.8 = (bf16[80,640]{1,0:T(8,128)(2,1)S(1)}, bf16[80,640]{1,0:T(8,128)(2,1)S(1)}, u32[]{:S(2)}, u32[]{:S(2)}) collective-permute-start(bf16[80,640]{1,0:T(8,128)(2,1)S(1)} %pad_maximum_fusion.6), channel_id=1, source_target_pairs={{0,1},{1,0},{2,3},{3,2},{4,5},{5,4},{6,7},{7,6},{8,9},{9,8},{10,11... | collective-permute-start | bytes 307208 | tf_op jit(solution)/shard_map/ppermute | solution.py:42
  94.3 6.1 %collective-permute-done.8 = bf16[80,640]{1,0:T(8,128)(2,1)S(1)} collective-permute-done((bf16[80,640]{1,0:T(8,128)(2,1)S(1)}, bf16[80,640]{1,0:T(8,128)(2,1)S(1)}, u32[]{:S(2)}, u32[]{:S(2)}) %collective-permute-start.8) | collective-permute-done | bytes 102432 | tf_op jit(solution)/shard_map/ppermute | solution.py:42
  100.6 1.9 %collective-permute-start.9 = (bf16[160,640]{1,0:T(8,128)(2,1)S(1)}, bf16[160,640]{1,0:T(8,128)(2,1)S(1)}, u32[]{:S(2)}, u32[]{:S(2)}) collective-permute-start(bf16[160,640]{1,0:T(8,128)(2,1)S(1)} %pad_maximum_fusion.3), channel_id=1, source_target_pairs={{0,2},{1,3},{2,0},{3,1},{4,6},{5,7},{6,4},{7,5},{8,10},{9,11},{10,... | collective-permute-start | bytes 614408 | tf_op jit(solution)/shard_map/ppermute | solution.py:42
  102.5 8.0 %collective-permute-done.9 = bf16[160,640]{1,0:T(8,128)(2,1)S(1)} collective-permute-done((bf16[160,640]{1,0:T(8,128)(2,1)S(1)}, bf16[160,640]{1,0:T(8,128)(2,1)S(1)}, u32[]{:S(2)}, u32[]{:S(2)}) %collective-permute-start.9) | collective-permute-done | bytes 204832 | tf_op jit(solution)/shard_map/ppermute | solution.py:42
  111.3 1.9 %collective-permute-start.10 = (bf16[320,640]{1,0:T(8,128)(2,1)}, bf16[320,640]{1,0:T(8,128)(2,1)}, u32[]{:S(2)}, u32[]{:S(2)}) collective-permute-start(bf16[320,640]{1,0:T(8,128)(2,1)} %pad_maximum_fusion.2), channel_id=1, source_target_pairs={{0,4},{1,5},{2,6},{3,7},{4,0},{5,1},{6,2},{7,3},{8,12},{9,13},{10,... | collective-permute-start | bytes 1228808 | tf_op jit(solution)/shard_map/ppermute | solution.py:42
  113.9 13.0 %collective-permute-done.10 = bf16[320,640]{1,0:T(8,128)(2,1)} collective-permute-done((bf16[320,640]{1,0:T(8,128)(2,1)}, bf16[320,640]{1,0:T(8,128)(2,1)}, u32[]{:S(2)}, u32[]{:S(2)}) %collective-permute-start.10) | collective-permute-done | bytes 409632 | tf_op jit(solution)/shard_map/ppermute | solution.py:42
  126.8 2.0 %pad_maximum_fusion.refs_4_ = bf16[640,640]{1,0:T(8,128)(2,1)} fusion(bf16[320,640]{1,0:T(8,128)(2,1)} %collective-permute-done.10, bf16[160,640]{1,0:T(8,128)(2,1)S(1)} %collective-permute-done.9, bf16[80,640]{1,0:T(8,128)(2,1)S(1)} %collective-permute-done.8, bf16[80,320]{1,0:T(8,128)(2,1)S(1)} %collective-permute-done.7, bf16[16,320]{1,0:T(8,128)(2,1)S(1)} %slice.64, ...), kind=kLoop, calls=%fused_computation | loop fusion | flops 4915200 | bytes 1638400 | tf_op jit(solution)/shard_map/concatenate | solution.py:263
  128.9 7.5 %shard_map.77 = (f32[384,640]{1,0:T(8,128)}, f32[384,128]{1,0:T(8,128)}, f32[160,640]{1,0:T(8,128)}, bf16[704,768]{1,0:T(8,128)(2,1)}) custom-call(s32[6]{0:T(128)} %stack.27.place, bf16[1792,640]{1,0:T(8,128)(2,1)} %all-gather.2.cloned.1.call-done.refs_0_, bf16[896,640]{1,0:T(8,128)(2,1)} %copy-done.1, bf16[896,640]{1,0:T(8,128)(2,1)} %copy-done.2, ...), custom_call_target="tpu_custom_call" | custom-call | flops 1258291200 | bytes 10485760 | tf_op jit(solution)/shard_map/pallas_call | solution.py:179
  136.4 1.9 %collective-permute-start.11 = (bf16[704,768]{1,0:T(8,128)(2,1)}, bf16[704,768]{1,0:T(8,128)(2,1)S(1)}, u32[]{:S(2)}, u32[]{:S(2)}) collective-permute-start(bf16[704,768]{1,0:T(8,128)(2,1)} %get-tuple-element.15), channel_id=1, source_target_pairs={{0,8},{1,9},{2,10},{3,11},{4,12},{5,13},{6,14},{7,15},{8,0},{9,1},... | collective-permute-start | bytes 3244040 | tf_op jit(solution)/shard_map/ppermute | solution.py:42
  138.3 2.9 %collective-permute-done.11.got = bf16[704,768]{1,0:T(8,128)(2,1)S(1)} collective-permute-done((bf16[704,768]{1,0:T(8,128)(2,1)}, bf16[704,768]{1,0:T(8,128)(2,1)S(1)}, u32[]{:S(2)}, u32[]{:S(2)}) %collective-permute-start.11) | collective-permute-done | bytes 1081376 | tf_op jit(solution)/shard_map/ppermute | solution.py:42
  142.2 3.0 %shard_map.78 = (f32[192,640]{1,0:T(8,128)}, f32[192,128]{1,0:T(8,128)}, f32[80,640]{1,0:T(8,128)}, bf16[352,768]{1,0:T(8,128)(2,1)}) custom-call(s32[6]{0:T(128)} %stack.27.place, f32[384,640]{1,0:T(8,128)} %get-tuple-element.12.total, f32[384,128]{1,0:T(8,128)} %get-tuple-element.13.proj, f32[160,640]{1,0:T(8,128)} %get-tuple-element.14.keep, ...), custom_call_target="tpu_custom_call" | custom-call | flops 1000000 | bytes 4194304 | tf_op jit(solution)/shard_map/pallas_call | solution.py:226
  145.1 2.5 %collective-permute-start.12 = (bf16[352,768]{1,0:T(8,128)(2,1)}, bf16[352,768]{1,0:T(8,128)(2,1)S(1)}, u32[]{:S(2)}, u32[]{:S(2)}) collective-permute-start(bf16[352,768]{1,0:T(8,128)(2,1)} %get-tuple-element.19), channel_id=1, source_target_pairs={{0,16},{1,17},{2,18},{3,19},{4,20},{5,21},{6,22},{7,23},{8,24},{9,... | collective-permute-start | bytes 1622024 | tf_op jit(solution)/shard_map/ppermute | solution.py:42
  148.5 13.1 %collective-permute-done.12.got = bf16[352,768]{1,0:T(8,128)(2,1)S(1)} collective-permute-done((bf16[352,768]{1,0:T(8,128)(2,1)}, bf16[352,768]{1,0:T(8,128)(2,1)S(1)}, u32[]{:S(2)}, u32[]{:S(2)}) %collective-permute-start.12) | collective-permute-done | bytes 540704 | tf_op jit(solution)/shard_map/ppermute | solution.py:42
  162.3 2.8 %shard_map.79 = (f32[192,640]{1,0:T(8,128)}, f32[80,640]{1,0:T(8,128)}) custom-call(f32[192,640]{1,0:T(8,128)} %get-tuple-element.16.mine, f32[192,128]{1,0:T(8,128)} %get-tuple-element.17.mine_proj, f32[80,640]{1,0:T(8,128)} %get-tuple-element.18.mine_update, bf16[352,768]{1,0:T(8,128)(2,1)} %copy-done.5, f32[32,640]{1,0:T(8,128)} %copy-done.4, ...), custom_call_target="tpu_custom_call" | custom-call | flops 47185920 | bytes 3145728 | tf_op jit(solution)/shard_map/pallas_call | solution.py:339
  (54 shorter events, 12.0 us)
Async XLA Ops:
  7.2 38.6 %copy-start = (f32[8,4,5120]{2,1,0:T(4,128)S(1)}, f32[8,4,5120]{2,1,0:T(4,128)}, u32[]{:S(2)}) copy-start(f32[8,4,5120]{2,1,0:T(4,128)} %param.9) | copy-start | bytes 1966084
  7.2 121.7 %all-gather.2.cloned.1.call-start = ((), (), s32[]{:S(2)}) async-start(), calls=%async_computation | async-start | bytes 2437120 | tf_op jit(solution)/shard_map/all_gather | solution.py:361
  8.2 20.4 %collective-permute-start = (bf16[80,640]{1,0:T(8,128)(2,1)S(1)}, bf16[80,640]{1,0:T(8,128)(2,1)S(1)}, u32[]{:S(2)}, u32[]{:S(2)}) collective-permute-start(bf16[80,640]{1,0:T(8,128)(2,1)S(1)} %convert_bitcast_fusion), channel_id=1, source_target_pairs={{0,0},{1,16},{2,256},{3,272},{4,8},{5,24},{6,264},{7,280},{8,32},{... | collective-permute-start | bytes 307208 | tf_op jit(solution)/shard_map/ppermute | solution.py:42
  31.5 5.1 %collective-permute-start.1 = (bf16[224,640]{1,0:T(8,128)(2,1)S(1)}, bf16[224,640]{1,0:T(8,128)(2,1)S(1)}, u32[]{:S(2)}, u32[]{:S(2)}) collective-permute-start(bf16[224,640]{1,0:T(8,128)(2,1)S(1)} %maximum_select_fusion), channel_id=1, source_target_pairs={{0,0},{1,16},{2,2},{3,18},{4,4},{5,20},{6,6},{7,22},{8,8},{9,24},{... | collective-permute-start | bytes 860168 | tf_op jit(solution)/shard_map/ppermute | solution.py:42
  32.8 10.8 %collective-permute-start.2 = (bf16[224,640]{1,0:T(8,128)(2,1)S(1)}, bf16[224,640]{1,0:T(8,128)(2,1)S(1)}, u32[]{:S(2)}, u32[]{:S(2)}) collective-permute-start(bf16[224,640]{1,0:T(8,128)(2,1)S(1)} %maximum_select_fusion), channel_id=1, source_target_pairs={{0,1},{1,17},{2,3},{3,19},{4,5},{5,21},{6,7},{7,23},{8,9},{9,25},{... | collective-permute-start | bytes 860168 | tf_op jit(solution)/shard_map/ppermute | solution.py:42
  43.7 2.1 %copy-start.7 = (s32[8]{0:T(128)S(1)}, s32[8]{0:T(128)}, u32[]{:S(2)}) copy-start(s32[8]{0:T(128)} %param.11) | copy-start | bytes 100
  43.8 9.6 %collective-permute-start.3 = (bf16[448,640]{1,0:T(8,128)(2,1)S(1)}, bf16[448,640]{1,0:T(8,128)(2,1)S(1)}, u32[]{:S(2)}, u32[]{:S(2)}) collective-permute-start(bf16[448,640]{1,0:T(8,128)(2,1)S(1)} %pad_maximum_fusion.1), channel_id=1, source_target_pairs={{0,8},{1,9},{2,10},{3,11},{4,12},{5,13},{6,14},{7,15},{8,0},{9,1},... | collective-permute-start | bytes 1720328 | tf_op jit(solution)/shard_map/ppermute | solution.py:42
  45.8 54.7 %copy-start.4 = (f32[32,640]{1,0:T(8,128)}, f32[32,640]{1,0:T(8,128)S(1)}, u32[]{:S(2)}) copy-start(f32[32,640]{1,0:T(8,128)S(1)} %reshape.15.right) | copy-start | bytes 245764
  53.5 57.8 %copy-start.1 = (bf16[896,640]{1,0:T(8,128)(2,1)}, bf16[896,640]{1,0:T(8,128)(2,1)S(1)}, u32[]{:S(2)}) copy-start(bf16[896,640]{1,0:T(8,128)(2,1)S(1)} %constant_dynamic-update-slice_fusion.refs_1_) | copy-start | bytes 3440644
  53.6 36.3 %collective-permute-start.4 = (bf16[896,640]{1,0:T(8,128)(2,1)S(1)}, bf16[896,640]{1,0:T(8,128)(2,1)S(1)}, u32[]{:S(2)}, u32[]{:S(2)}) collective-permute-start(bf16[896,640]{1,0:T(8,128)(2,1)S(1)} %constant_dynamic-update-slice_fusion.refs_1_), channel_id=1, source_target_pairs={{0,6},{1,7},{2,0},{3,1},{4,2},{5,3},{6,4},{7,5},{8,10},{9,11},{10,... | collective-permute-start | bytes 3440648 | tf_op jit(solution)/shard_map/ppermute | solution.py:42
  56.7 25.9 %collective-permute-start.6 = (bf16[80,640]{1,0:T(8,128)(2,1)S(1)}, bf16[80,640]{1,0:T(8,128)(2,1)S(1)}, u32[]{:S(2)}, u32[]{:S(2)}) collective-permute-start(bf16[80,640]{1,0:T(8,128)(2,1)S(1)} %pad_maximum_fusion.5), channel_id=1, source_target_pairs={{0,0},{1,64},{2,128},{3,192},{4,256},{5,320},{6,384},{7,448},{8,8}... | collective-permute-start | bytes 307208 | tf_op jit(solution)/shard_map/ppermute | solution.py:42
  82.8 9.5 %collective-permute-start.7 = (bf16[80,320]{1,0:T(8,128)(2,1)S(1)}, bf16[80,320]{1,0:T(8,128)(2,1)S(1)}, u32[]{:S(2)}, u32[]{:S(2)}) collective-permute-start(bf16[80,320]{1,0:T(8,128)(2,1)S(1)} %maximum_select_fusion.1), channel_id=1, source_target_pairs={{0,32},{1,33},{2,34},{3,35},{4,36},{5,37},{6,38},{7,39},{8,40},{9,... | collective-permute-start | bytes 153608 | tf_op jit(solution)/shard_map/ppermute | solution.py:42
  89.9 39.0 %copy-start.2 = (bf16[896,640]{1,0:T(8,128)(2,1)}, bf16[896,640]{1,0:T(8,128)(2,1)S(1)}, u32[]{:S(2)}) copy-start(bf16[896,640]{1,0:T(8,128)(2,1)S(1)} %collective-permute-done.4.refs_2_) | copy-start | bytes 3440644
  89.9 39.0 %collective-permute-start.5 = (bf16[896,640]{1,0:T(8,128)(2,1)S(1)}, bf16[896,640]{1,0:T(8,128)(2,1)}, u32[]{:S(2)}, u32[]{:S(2)}) collective-permute-start(bf16[896,640]{1,0:T(8,128)(2,1)S(1)} %collective-permute-done.4.refs_2_), channel_id=1, source_target_pairs={{0,0},{1,1},{2,2},{3,3},{4,4},{5,5},{6,6},{7,7},{8,10},{9,11},{10,... | collective-permute-start | bytes 3440648 | tf_op jit(solution)/shard_map/ppermute | solution.py:42
  92.4 8.1 %collective-permute-start.8 = (bf16[80,640]{1,0:T(8,128)(2,1)S(1)}, bf16[80,640]{1,0:T(8,128)(2,1)S(1)}, u32[]{:S(2)}, u32[]{:S(2)}) collective-permute-start(bf16[80,640]{1,0:T(8,128)(2,1)S(1)} %pad_maximum_fusion.6), channel_id=1, source_target_pairs={{0,1},{1,0},{2,3},{3,2},{4,5},{5,4},{6,7},{7,6},{8,9},{9,8},{10,11... | collective-permute-start | bytes 307208 | tf_op jit(solution)/shard_map/ppermute | solution.py:42
  100.6 9.9 %collective-permute-start.9 = (bf16[160,640]{1,0:T(8,128)(2,1)S(1)}, bf16[160,640]{1,0:T(8,128)(2,1)S(1)}, u32[]{:S(2)}, u32[]{:S(2)}) collective-permute-start(bf16[160,640]{1,0:T(8,128)(2,1)S(1)} %pad_maximum_fusion.3), channel_id=1, source_target_pairs={{0,2},{1,3},{2,0},{3,1},{4,6},{5,7},{6,4},{7,5},{8,10},{9,11},{10,... | collective-permute-start | bytes 614408 | tf_op jit(solution)/shard_map/ppermute | solution.py:42
  111.3 15.5 %collective-permute-start.10 = (bf16[320,640]{1,0:T(8,128)(2,1)}, bf16[320,640]{1,0:T(8,128)(2,1)}, u32[]{:S(2)}, u32[]{:S(2)}) collective-permute-start(bf16[320,640]{1,0:T(8,128)(2,1)} %pad_maximum_fusion.2), channel_id=1, source_target_pairs={{0,4},{1,5},{2,6},{3,7},{4,0},{5,1},{6,2},{7,3},{8,12},{9,13},{10,... | collective-permute-start | bytes 1228808 | tf_op jit(solution)/shard_map/ppermute | solution.py:42
  136.4 4.8 %collective-permute-start.11 = (bf16[704,768]{1,0:T(8,128)(2,1)}, bf16[704,768]{1,0:T(8,128)(2,1)S(1)}, u32[]{:S(2)}, u32[]{:S(2)}) collective-permute-start(bf16[704,768]{1,0:T(8,128)(2,1)} %get-tuple-element.15), channel_id=1, source_target_pairs={{0,8},{1,9},{2,10},{3,11},{4,12},{5,13},{6,14},{7,15},{8,0},{9,1},... | collective-permute-start | bytes 3244040 | tf_op jit(solution)/shard_map/ppermute | solution.py:42
  141.2 1.0 copy-start.3
  142.2 5.5 %copy-start.6 = (s32[1,192]{1,0:T(1,128)S(1)}, s32[1,192]{1,0:T(1,128)}, u32[]{:S(2)}) copy-start(s32[1,192]{1,0:T(1,128)} %param.10) | copy-start | bytes 2308
  145.1 16.4 %collective-permute-start.12 = (bf16[352,768]{1,0:T(8,128)(2,1)}, bf16[352,768]{1,0:T(8,128)(2,1)S(1)}, u32[]{:S(2)}, u32[]{:S(2)}) collective-permute-start(bf16[352,768]{1,0:T(8,128)(2,1)} %get-tuple-element.19), channel_id=1, source_target_pairs={{0,16},{1,17},{2,18},{3,19},{4,20},{5,21},{6,22},{7,23},{8,24},{9,... | collective-permute-start | bytes 1622024 | tf_op jit(solution)/shard_map/ppermute | solution.py:42
  161.5 0.8 copy-start.5
Sparse Core Ops, SparseCore 0:
  33.0 89.4 all-gather.1

commit v6 on v0

v6 whole, which is shorter than its diff:
```python
import functools
import itertools
import math

import jax
import jax.numpy as jnp
from jax import lax
from jax.experimental import pallas as pl
from jax.experimental.pallas import tpu as pltpu
from jax.sharding import Mesh
from jax.sharding import PartitionSpec as P

D = 5120
RANK = 4
M_DEV = 8
ROWS = 192
IN_BLOCK = 640
OUT_BLOCK = 80
EXTRA = 80
SLOT = OUT_BLOCK + 32
GROUP_ROWS = 768
GIVE = 176

perturb_scale = 0.5

SIZES = {"z": 16, "xl": 2, "core": 2, "y": 4, "xh": 2}
AXES = tuple(SIZES)
POP = ("z", "xl", "core")
TENSOR = ("y", "xh")
BF16 = jnp.bfloat16
F32 = jnp.float32


def flat(place):
    index = 0
    for value, size in zip(place, SIZES.values()):
        index = index * size + value % size
    return index


def move(value, target):
    places = itertools.product(*(range(n) for n in SIZES.values()))
    return lax.ppermute(value, AXES, [(flat(p), flat(target(*p))) for p in places])


def right_target(near, z, xl, core, y, xh):
    return (z + 2 * (2 * y + xh) + near, xl, core, y, xh)


def core_target(z, xl, core, y, xh):
    return (z, xl, 1 - core, y, xh)


def xl_target(z, xl, core, y, xh):
    return (z, 1 - xl, core, y, xh)


def xh_target(z, xl, core, y, xh):
    return (z, xl, core, y, 1 - xh)


def y_pair_target(z, xl, core, y, xh):
    return (z, xl, core, y ^ 1, xh)


def y_half_target(z, xl, core, y, xh):
    return (z, xl, core, y + 2, xh)


def diagonal_target(z, xl, core, y, xh):
    return (z, 1 - xl, 1 - core, y, xh)


def nt_dot(a, b):
    return lax.dot_general(a, b, (((1,), (1,)), ((), ())), preferred_element_type=F32)


def split(value):
    high = lax.reduce_precision(value, 8, 7)
    return high.astype(BF16), (value - high).astype(BF16)


def product_kernel(place, slots, rows, left, member, give, weights):
    for source in range(16):
        block = slots[source * SLOT : source * SLOT + OUT_BLOCK, :]
        weights[source * OUT_BLOCK : (source + 1) * OUT_BLOCK, :] = block
    proj = nt_dot(left[...], rows[:ROWS, :])
    owner = lax.broadcasted_iota(jnp.int32, (32, ROWS), 0) // RANK
    proj = jnp.where(owner == member[...], proj, 0.0)
    folded = proj[:8] + proj[8:16] + proj[16:24] + proj[24:]
    high = folded.astype(BF16).astype(F32)
    pair = jnp.concatenate([high, folded - high]).astype(BF16)
    for part in range(2):
        block = nt_dot(weights[part * 640 : part * 640 + 640, :], rows[...])
        for i in range(4):
            at = part * 4 + i
            give[at, :160, :] = block[i * 160 : (i + 1) * 160].astype(BF16)
            give[at, 160:, :] = jnp.zeros((16, GROUP_ROWS), BF16)
            give[at, 160:, :ROWS] = pair


VMEM = pl.BlockSpec(memory_space=pltpu.VMEM)
SMEM = pl.BlockSpec(memory_space=pltpu.SMEM)
LIMIT = pltpu.CompilerParams(vmem_limit_bytes=50 * 2**20)


def shape(*dims, dtype=F32):
    return jax.ShapeDtypeStruct(dims, dtype)


def call(kernel, outs, place, arrays, scratch=(), flops=10**6, moved=4 * 2**20):
    return pl.pallas_call(
        kernel,
        out_shape=outs,
        in_specs=[SMEM] + [VMEM] * len(arrays),
        out_specs=(VMEM,) * len(outs),
        scratch_shapes=list(scratch),
        compiler_params=LIMIT,
        cost_estimate=pl.CostEstimate(flops=flops, bytes_accessed=moved, transcendentals=0),
    )(place, *arrays)


def update_kernel(members, place, slots, right, keep, give, total, *scratch):
    core = place[1]
    update_sums(members, place, slots, right, total, *scratch)
    for i in range(2):
        at = slice(i * OUT_BLOCK, (i + 1) * OUT_BLOCK)
        here = pl.ds(pl.multiple_of((2 * i + core) * OUT_BLOCK, 8), OUT_BLOCK)
        there = pl.ds(pl.multiple_of((2 * i + 1 - core) * OUT_BLOCK, 8), OUT_BLOCK)
        keep[at, :] = total[here, :]
        give[at, :] = total[there, :]


def join_kernel(place, keep, got, mine, give):
    xl = place[5]
    first = keep[:OUT_BLOCK, :] + got[:OUT_BLOCK, :]
    second = keep[OUT_BLOCK:, :] + got[OUT_BLOCK:, :]
    mine[...] = jnp.where(xl == 0, first, second)
    give[...] = jnp.where(xl == 0, second, first)


def sum_kernel(place, got, mine, coefficient, to_core, to_xl, to_diagonal):
    total, folded = 0.0, 0.0
    for index in range(8):
        total = total + got[index, :160, :].astype(F32)
        pair = got[index, 160:, :256].astype(F32)[:, :ROWS]
        folded = folded + pair[:8] + pair[8:]
    coefficient[...] = folded
    mine[...] = total[:, :256]
    to_core[...] = total[:, 384:640]
    to_xl[...] = pltpu.roll(total[:, :384], 192, 1)[:, :256].astype(BF16)
    to_diagonal[...] = pltpu.roll(total[:, 384:], 192, 1)[:, :256].astype(BF16)


def finish_kernel(
    scale, place, mine, from_core, from_xl, from_diagonal, coefficient, right, member, out, full
):
    core, xl = place[1], place[5]
    sources = (
        (mine, xl, core),
        (from_core, xl, 1 - core),
        (from_xl, 1 - xl, core),
        (from_diagonal, 1 - xl, 1 - core),
    )
    for ref, side, half in sources:
        for j in range(2):
            start = (4 * j + 2 * side + half) * OUT_BLOCK
            block = ref[j * OUT_BLOCK : (j + 1) * OUT_BLOCK, :].astype(F32)
            full[pl.ds(pl.multiple_of(start, 8), OUT_BLOCK), :] = block
    owner = lax.broadcasted_iota(jnp.int32, (32, ROWS), 0) // RANK
    factor = jnp.where(owner == member[...], jnp.concatenate([coefficient[...]] * 4), 0.0) * scale
    low_rank = lax.dot_general(
        factor,
        right[...],
        (((0,), (0,)), ((), ())),
        precision=lax.Precision.HIGHEST,
        preferred_element_type=F32,
    )
    out[...] = full[...].T[:ROWS] + low_rank


def zero_after(value):
    return jnp.where(value[-1, -1] == value[-1, -1], 0, 1).astype(jnp.int32)


def rank_row(ranks):
    own = jnp.pad(ranks.astype(BF16)[None, :], ((0, 15), (0, 120)))
    every = lax.all_gather(own, ("xl", "core"), axis=1, tiled=True)
    every = jnp.concatenate([every[:, g * 128 : g * 128 + M_DEV] for g in range(4)], 1)
    return jnp.pad(every, ((0, 0), (0, 320 - 4 * M_DEV)))


def spread_right(right_factors, ranks, z, tensor):
    levels = rank_row(ranks)
    parts = []
    for near in range(2):
        start = lax.rem(z + 2 * tensor + near, 16) * 320
        chunk = lax.dynamic_slice_in_dim(right_factors, start, 320, 2).reshape(32, 320)
        sent = jnp.concatenate([*split(chunk), levels])
        parts.append(jnp.pad(move(sent, functools.partial(right_target, near)), ((0, 0), (0, 64))))
    return jnp.concatenate(parts, 1)


def gather_right(held):
    for target in (xh_target, y_pair_target, y_half_target):
        held = jnp.concatenate([held, move(held, target)])
    return held


def update_sums(members, place, slots, right, total, left, high, low):
    z, core, y, xh, xl = place[0], place[1], place[3], place[4], place[5]
    blocks = [(far, pair, h) for far in range(2) for pair in range(2) for h in range(2)]
    lane = lax.broadcasted_iota(jnp.int32, (1, 128), 1)
    levels, spread, rank_sum = [], 0.0, 0.0
    for index in range(8):
        row = right[index * EXTRA + 64 : (index + 1) * EXTRA, :].astype(F32)[:1, :]
        levels.append([row[:, :128], row[:, 384:512]])
    for value in sum(levels, []):
        rank_sum = rank_sum + jnp.where(lane < 4 * M_DEV, value, 0.0)
    rank_mean = jnp.sum(rank_sum) / members
    for value in sum(levels, []):
        spread = spread + jnp.where(lane < 4 * M_DEV, (value - rank_mean) ** 2, 0.0)
    variance = jnp.full((8, 128), jnp.sum(spread) / members)
    scale = lax.rsqrt(variance + 1e-05)[:1, :1] * math.sqrt(D / (members * RANK))

    lane = lax.broadcasted_iota(jnp.int32, (32, 128), 1)
    member = lax.broadcasted_iota(jnp.int32, (32, 128), 0) // RANK + M_DEV * (2 * xl + core)
    in_first = lax.broadcasted_iota(jnp.int32, (32, GROUP_ROWS), 1) < 384
    for index, (far, pair, h) in enumerate(blocks):
        base = index * EXTRA
        rows = slice(index * 32, index * 32 + 32)
        level = [
            jnp.sum(jnp.where(lane == member, value, 0.0), axis=1, keepdims=True)
            for value in levels[index]
        ]
        fitness = (jnp.where(in_first, level[0], level[1]) - rank_mean) * scale
        scaled = fitness * (
            right[base : base + 32, :].astype(F32) + right[base + 32 : base + 64, :].astype(F32)
        )
        part = scaled.astype(BF16)
        high[rows, :] = part
        low[rows, :] = (scaled - part.astype(F32)).astype(BF16)
        owner = 2 * lax.rem((y ^ pair) + 2 * far, 4) + (xh ^ h)
        for near in range(2):
            start = lax.rem(z + 32 - 2 * owner - near, 16) * SLOT + OUT_BLOCK
            left[near, rows, :] = slots[pl.ds(pl.multiple_of(start, 16), 32), :]

    def tn_dot(a, b):
        return lax.dot_general(a, b, (((0,), (0,)), ((), ())), preferred_element_type=F32)

    for near in range(2):
        lanes = slice(near * 384, near * 384 + 384)
        part = (tn_dot(high[:, lanes], left[near]) + tn_dot(low[:, lanes], left[near]))[:320]
        total[...] = part if near == 0 else total[...] + part


def on_device(tokens, base_weight, left_factors, right_factors, member_of, ranks):
    z, xl, core, y, xh = (lax.axis_index(name) for name in AXES)
    members = M_DEV * 64
    left = left_factors.astype(BF16).reshape(32, IN_BLOCK)
    tensor = y * 2 + xh
    place = jnp.stack([z, core, xl ^ xh, y, xh, xl, tensor]).astype(jnp.int32)
    slot = jnp.concatenate([base_weight.T.astype(BF16), left])
    slots = lax.all_gather(slot, "z", axis=0, tiled=True)

    rows = jnp.concatenate([tokens, move(tokens, xl_target)])
    rows = jnp.concatenate([rows, move(rows, core_target)])
    right = gather_right(spread_right(right_factors, ranks, z, tensor))
    keep, give = call(
        functools.partial(update_kernel, members),
        (shape(160, IN_BLOCK), shape(160, IN_BLOCK)),
        place,
        (slots, right),
        [
            pltpu.VMEM((320, IN_BLOCK), F32),
            pltpu.VMEM((2, 256, IN_BLOCK), BF16),
            pltpu.VMEM((256, GROUP_ROWS), BF16),
            pltpu.VMEM((256, GROUP_ROWS), BF16),
        ],
        flops=8 * 384 * 256 * 640,
    )
    keep, give = call(
        join_kernel,
        (shape(OUT_BLOCK, IN_BLOCK), shape(OUT_BLOCK, IN_BLOCK)),
        place,
        (keep, move(give, core_target)),
    )
    update = keep + move(give, xl_target)

    (give,) = call(
        product_kernel,
        (shape(8, GIVE, GROUP_ROWS, dtype=BF16),),
        place + zero_after(right),
        (slots, rows, left, member_of),
        [pltpu.VMEM((2 * IN_BLOCK, IN_BLOCK), BF16)],
        flops=2 * 768 * 640 * 1280,
        moved=6 * 2**20,
    )
    got = lax.all_to_all(give, TENSOR, split_axis=0, concat_axis=0, tiled=True)
    block = (160, 256)
    mine, coefficient, to_core, to_xl, to_diagonal = call(
        sum_kernel,
        (shape(*block), shape(8, ROWS), shape(*block))
        + (shape(*block, dtype=BF16), shape(*block, dtype=BF16)),
        place,
        (got,),
    )
    right_local = lax.dynamic_slice_in_dim(right_factors, tensor * IN_BLOCK, IN_BLOCK, 2)
    (outputs,) = call(
        functools.partial(finish_kernel, perturb_scale / math.sqrt(RANK)),
        (shape(ROWS, IN_BLOCK),),
        place,
        (
            mine,
            move(to_core, core_target),
            move(to_xl, xl_target),
            move(to_diagonal, diagonal_target),
            coefficient,
            right_local.reshape(32, IN_BLOCK),
            member_of,
        ),
        [pltpu.VMEM((IN_BLOCK, 256), F32)],
        flops=12 * ROWS * 32 * IN_BLOCK,
    )
    return (outputs, update.T)


def solution(mesh):
    fine = Mesh(mesh.devices.reshape(tuple(SIZES.values())), AXES)
    return jax.shard_map(
        on_device,
        mesh=fine,
        in_specs=(
            P(POP, TENSOR),
            P(TENSOR, POP),
            P(POP, None, TENSOR),
            P(POP, None, None),
            P(POP, None),
            P(POP),
        ),
        out_specs=(P(POP, TENSOR), P(TENSOR, POP)),
        check_vma=False,
    )
```

time: 480 us -> 157 us (0.33)
  blocking collectives: 244 us -> 11.8 us
  waiting for transfers between devices: 145 us -> 22.8 us
  starting transfers between devices: 6.69 us -> 84.5 us
  local copies, waits for them, and re-layouts: 42.9 us -> 4.8 us
  matrix products: 16.6 us -> 0 us
  Pallas kernels: 0 us -> 9.81 us
    psum x3 -> x0, blocking collectives: 244 us -> none  [the longest x1 113 us: rank_statistics(): overall = lax.psum(jnp.sum(rank_values), 'pop')]
    reduce_scatter x1 -> x0, waiting for transfers between devices: 91.1 us -> none  [base_product(): lax.psum_scatter(partial_value, 'tensor', scatter_dimension=1, tiled=True)]
    ppermute x0 -> x12, starting transfers between devices: none -> 73.4 us  [move(): lax.ppermute(value, AXES, [(flat(p), flat(target(*p))) for p in places])]
    unnamed x11 -> x8, local copies, waits for them, and re-layouts: 34.8 us -> 1.39 us
    all_gather x2 -> x1, waiting for transfers between devices: 32.4 us -> 0.02 us  [on_device(): slots = lax.all_gather(slot, 'z', axis=0, tiled=True)]
    ppermute x0 -> x12, waiting for transfers between devices: none -> 20.1 us  [move(): lax.ppermute(value, AXES, [(flat(p), flat(target(*p))) for p in places])]
    all_to_all x1, waiting for transfers between devices: 21.6 us -> 2.72 us  [on_device(): got = lax.all_to_all(give, TENSOR, split_axis=0, concat_axis=0, tiled=True)]
    dot_general x4 -> x0, matrix products: 16.6 us -> none  [the longest x1 7.16 us: base_product(): jnp.dot(tokens, lax.all_gather(base_half, 'pop', axis=1, tiled=True), pre...]
  transfers between devices with their start and end apart: 4 -> 14, of which waited for: 3 -> 5; matrix products, arithmetic and copies ran while one was open for 13% -> 5% of each run, Pallas kernels for 0% -> 3%
where the time goes in v6:
time: 157 us; the launch traced here: 156 us
  starting transfers between devices  84.5 us (54%)
  waiting for transfers between devices  22.8 us (15%)
  between operations  15.7 us (10%)
  blocking collectives  11.8 us (8%)
  Pallas kernels  9.81 us (6%)
  other arithmetic  6.41 us (4%)
  local copies, waits for them, and re-layouts  4.8 us (3%)
    ppermute x12, starting transfers between devices, move(): lax.ppermute(value, AXES, [(flat(p), flat(target(*p))) for p in places])  73.4 us
    ppermute x12, waiting for transfers between devices, move(): lax.ppermute(value, AXES, [(flat(p), flat(target(*p))) for p in places])  20.1 us
    all_gather x1, blocking collectives, rank_row(): every = lax.all_gather(own, ('xl', 'core'), axis=1, tiled=True)  11.8 us
    all_to_all x1, starting transfers between devices, on_device(): got = lax.all_to_all(give, TENSOR, split_axis=0, concat_axis=0, tiled=True)  11.1 us
    pallas_call x5, Pallas kernels, call(): pl.pallas_call(kernel, out_shape=outs, in_specs=[SMEM] + [VMEM] * len(arr...  9.81 us
  transfers between devices with their start and end apart: 14, of which 5 were waited for; matrix products, arithmetic and copies ran while one was open for 5% of the time, Pallas kernels for 3%

profile of v6, /device:TPU:1, one launch (start us, length us, event | category | flops | bytes accessed | tf_op | source)
XLA Modules:
  0.0 155.9 jit_solution(315624554197577381)
XLA Ops:
  11.7 11.8 %all_gather.6 = bf16[16,512]{1,0:T(8,128)(2,1)S(1)} all-gather(bf16[16,128]{1,0:T(8,128)(2,1)S(1)} %pad.15), channel_id=1, replica_groups=mesh['z'=16,'xl'=2,'core'=2,'y'=4,'xh'=2] {'xl','core'}, dimensions={1}, use_global_device_ids=true | all-gather | bytes 20480 | tf_op jit(solution)/shard_map/all_gather | solution.py:188
  24.3 1.9 %collective-permute-start.1 = (bf16[80,320]{1,0:T(8,128)(2,1)S(1)}, bf16[80,320]{1,0:T(8,128)(2,1)S(1)}, u32[]{:S(2)}, u32[]{:S(2)}) collective-permute-start(bf16[80,320]{1,0:T(8,128)(2,1)S(1)} %get-tuple-element.31), channel_id=1, source_target_pairs={{0,32},{1,97},{2,162},{3,227},{4,292},{5,357},{6,422},{7,487},{8,4... | collective-permute-start | bytes 153608 | tf_op jit(solution)/shard_map/ppermute | solution.py:43
  26.3 6.0 %collective-permute-done.1 = bf16[80,320]{1,0:T(8,128)(2,1)S(1)} collective-permute-done((bf16[80,320]{1,0:T(8,128)(2,1)S(1)}, bf16[80,320]{1,0:T(8,128)(2,1)S(1)}, u32[]{:S(2)}, u32[]{:S(2)}) %collective-permute-start.1) | collective-permute-done | bytes 51232 | tf_op jit(solution)/shard_map/ppermute | solution.py:43
  32.3 9.7 %collective-permute-start.2 = (bf16[80,768]{1,0:T(8,128)(2,1)S(1)}, bf16[80,768]{1,0:T(8,128)(2,1)S(1)}, u32[]{:S(2)}, u32[]{:S(2)}) collective-permute-start(bf16[80,768]{1,0:T(8,128)(2,1)S(1)} %pad_maximum_fusion.6), channel_id=1, source_target_pairs={{0,1},{1,0},{2,3},{3,2},{4,5},{5,4},{6,7},{7,6},{8,9},{9,8},{10,11... | collective-permute-start | bytes 368648 | tf_op jit(solution)/shard_map/ppermute | solution.py:43
  42.0 2.2 %collective-permute-start.5 = (bf16[192,640]{1,0:T(8,128)(2,1)S(1)}, bf16[192,640]{1,0:T(8,128)(2,1)S(1)}, u32[]{:S(2)}, u32[]{:S(2)}) collective-permute-start(bf16[192,640]{1,0:T(8,128)(2,1)S(1)} %copy-done.3), channel_id=1, source_target_pairs={{0,16},{1,17},{2,18},{3,19},{4,20},{5,21},{6,22},{7,23},{8,24},{9,... | collective-permute-start | bytes 737288 | tf_op jit(solution)/shard_map/ppermute | solution.py:43
  44.3 17.1 %collective-permute-start.3 = (bf16[160,768]{1,0:T(8,128)(2,1)S(1)}, bf16[160,768]{1,0:T(8,128)(2,1)S(1)}, u32[]{:S(2)}, u32[]{:S(2)}) collective-permute-start(bf16[160,768]{1,0:T(8,128)(2,1)S(1)} %pad_maximum_fusion.4), channel_id=1, source_target_pairs={{0,2},{1,3},{2,0},{3,1},{4,6},{5,7},{6,4},{7,5},{8,10},{9,11},{10,... | collective-permute-start | bytes 737288 | tf_op jit(solution)/shard_map/ppermute | solution.py:43
  61.5 7.9 %collective-permute-start.6 = (bf16[384,640]{1,0:T(8,128)(2,1)S(1)}, bf16[384,640]{1,0:T(8,128)(2,1)}, u32[]{:S(2)}, u32[]{:S(2)}) collective-permute-start(bf16[384,640]{1,0:T(8,128)(2,1)S(1)} %pad_maximum_fusion.3), channel_id=1, source_target_pairs={{0,8},{1,9},{2,10},{3,11},{4,12},{5,13},{6,14},{7,15},{8,0},{9,1},... | collective-permute-start | bytes 1474568 | tf_op jit(solution)/shard_map/ppermute | solution.py:43
  69.5 2.7 %collective-permute-start.4 = (bf16[320,768]{1,0:T(8,128)(2,1)S(1)}, bf16[320,768]{1,0:T(8,128)(2,1)}, u32[]{:S(2)}, u32[]{:S(2)}) collective-permute-start(bf16[320,768]{1,0:T(8,128)(2,1)S(1)} %pad_maximum_fusion.2), channel_id=1, source_target_pairs={{0,4},{1,5},{2,6},{3,7},{4,0},{5,1},{6,2},{7,3},{8,12},{9,13},{10,... | collective-permute-start | bytes 1474568 | tf_op jit(solution)/shard_map/ppermute | solution.py:43
  73.4 10.1 %collective-permute-done.4 = bf16[320,768]{1,0:T(8,128)(2,1)} collective-permute-done((bf16[320,768]{1,0:T(8,128)(2,1)S(1)}, bf16[320,768]{1,0:T(8,128)(2,1)}, u32[]{:S(2)}, u32[]{:S(2)}) %collective-permute-start.4) | collective-permute-done | bytes 491552 | tf_op jit(solution)/shard_map/ppermute | solution.py:43
  83.5 1.3 slice.25
  86.2 3.4 %shard_map.77 = bf16[8,176,768]{2,1,0:T(8,128)(2,1)S(1)} custom-call(s32[7]{0:T(128)S(1)} %broadcast_add_fusion.place, bf16[1792,640]{1,0:T(8,128)(2,1)} %all-gather.2.cloned.1.call-done.slots, bf16[768,640]{1,0:T(8,128)(2,1)S(1)} %pad_maximum_fusion.rows, bf16[32,640]{1,0:T(8,128)(2,1)S(1)} %reshape.22.left, s32[1,192]{1,0:T(1,128)S(1)} %copy-done.2), custom_call_target="tpu_custom_call" | custom-call | flops 1258291200 | bytes 6291456 | tf_op jit(solution)/shard_map/pallas_call | solution.py:112
  89.6 1.4 copy-done.1
  91.0 11.1 %all-to-all-start = ((bf16[8,176,768]{2,1,0:T(8,128)(2,1)}), bf16[8,176,768]{2,1,0:T(8,128)(2,1)}, u32[]{:S(2)}, u32[]{:S(2)}) async-start(bf16[8,176,768]{2,1,0:T(8,128)(2,1)} %copy-done.1), calls=%async_computation | async-start | bytes 4325376 | tf_op jit(solution)/shard_map/all_to_all | solution.py:299
  103.2 1.9 %shard_map.80 = (f32[160,640]{1,0:T(8,128)S(1)}, f32[160,640]{1,0:T(8,128)S(1)}) custom-call(s32[7]{0:T(128)S(1)} %stack.31.place, bf16[1792,640]{1,0:T(8,128)(2,1)S(1)} %copy-done, bf16[640,768]{1,0:T(8,128)(2,1)S(1)} %pad_maximum_fusion.1.right), custom_call_target="tpu_custom_call" | custom-call | flops 503316480 | bytes 4194304 | tf_op jit(solution)/shard_map/pallas_call | solution.py:112
  105.1 10.1 %collective-permute-start.10 = (f32[160,640]{1,0:T(8,128)S(1)}, f32[160,640]{1,0:T(8,128)S(1)}, u32[]{:S(2)}, u32[]{:S(2)}) collective-permute-start(f32[160,640]{1,0:T(8,128)S(1)} %get-tuple-element.17), channel_id=1, source_target_pairs={{0,8},{1,9},{2,10},{3,11},{4,12},{5,13},{6,14},{7,15},{8,0},{9,1},... | collective-permute-start | bytes 1228808 | tf_op jit(solution)/shard_map/ppermute | solution.py:43
  115.2 1.4 collective-permute-done.10.got
  117.2 2.2 %collective-permute-start.11 = (f32[80,640]{1,0:T(8,128)S(1)}, f32[80,640]{1,0:T(8,128)S(1)}, u32[]{:S(2)}, u32[]{:S(2)}) collective-permute-start(f32[80,640]{1,0:T(8,128)S(1)} %get-tuple-element.19), channel_id=1, source_target_pairs={{0,16},{1,17},{2,18},{3,19},{4,20},{5,21},{6,22},{7,23},{8,24},{9,... | collective-permute-start | bytes 614408 | tf_op jit(solution)/shard_map/ppermute | solution.py:43
  120.3 2.7 %all-to-all-done.got = bf16[8,176,768]{2,1,0:T(8,128)(2,1)} async-done(((bf16[8,176,768]{2,1,0:T(8,128)(2,1)}), bf16[8,176,768]{2,1,0:T(8,128)(2,1)}, u32[]{:S(2)}, u32[]{:S(2)}) %all-to-all-start) | async-done | bytes 2162720 | tf_op jit(solution)/shard_map/all_to_all | solution.py:299
  123.0 1.9 %shard_map.78 = (f32[160,256]{1,0:T(8,128)S(1)}, f32[8,192]{1,0:T(8,128)S(1)}, f32[160,256]{1,0:T(8,128)S(1)}, bf16[160,256]{1,0:T(8,128)(2,1)S(1)}, bf16[160,256]{1,0:T(8,128)(2,1)S(1)}) custom-call(s32[7]{0:T(128)S(1)} %stack.31.place, bf16[8,176,768]{2,1,0:T(8,128)(2,1)} %all-to-all-done.got), custom_call_target="tpu_custom_call" | custom-call | flops 1000000 | bytes 4194304 | tf_op jit(solution)/shard_map/pallas_call | solution.py:112
  125.0 13.4 %collective-permute-start.7 = (f32[160,256]{1,0:T(8,128)S(1)}, f32[160,256]{1,0:T(8,128)S(1)}, u32[]{:S(2)}, u32[]{:S(2)}) collective-permute-start(f32[160,256]{1,0:T(8,128)S(1)} %get-tuple-element.12), channel_id=1, source_target_pairs={{0,8},{1,9},{2,10},{3,11},{4,12},{5,13},{6,14},{7,15},{8,0},{9,1},... | collective-permute-start | bytes 491528 | tf_op jit(solution)/shard_map/ppermute | solution.py:43
  138.4 2.5 %collective-permute-start.8 = (bf16[160,256]{1,0:T(8,128)(2,1)S(1)}, bf16[160,256]{1,0:T(8,128)(2,1)S(1)}, u32[]{:S(2)}, u32[]{:S(2)}) collective-permute-start(bf16[160,256]{1,0:T(8,128)(2,1)S(1)} %get-tuple-element.13), channel_id=1, source_target_pairs={{0,16},{1,17},{2,18},{3,19},{4,20},{5,21},{6,22},{7,23},{8,24},{9,... | collective-permute-start | bytes 245768 | tf_op jit(solution)/shard_map/ppermute | solution.py:43
  140.9 3.0 %collective-permute-start.9 = (bf16[160,256]{1,0:T(8,128)(2,1)S(1)}, bf16[160,256]{1,0:T(8,128)(2,1)S(1)}, u32[]{:S(2)}, u32[]{:S(2)}) collective-permute-start(bf16[160,256]{1,0:T(8,128)(2,1)S(1)} %get-tuple-element.14), channel_id=1, source_target_pairs={{0,24},{1,25},{2,26},{3,27},{4,28},{5,29},{6,30},{7,31},{8,16},{9,... | collective-permute-start | bytes 245768 | tf_op jit(solution)/shard_map/ppermute | solution.py:43
  144.6 2.5 %collective-permute-done.9.from_diagonal = bf16[160,256]{1,0:T(8,128)(2,1)S(1)} collective-permute-done((bf16[160,256]{1,0:T(8,128)(2,1)S(1)}, bf16[160,256]{1,0:T(8,128)(2,1)S(1)}, u32[]{:S(2)}, u32[]{:S(2)}) %collective-permute-start.9) | collective-permute-done | bytes 81952 | tf_op jit(solution)/shard_map/ppermute | solution.py:43
  147.1 1.9 %shard_map.79 = f32[192,640]{1,0:T(8,128)} custom-call(s32[7]{0:T(128)S(1)} %stack.31.place, f32[160,256]{1,0:T(8,128)S(1)} %get-tuple-element.11.mine, f32[160,256]{1,0:T(8,128)S(1)} %collective-permute-done.7.from_core, bf16[160,256]{1,0:T(8,128)(2,1)S(1)} %collective-permute-done.8.from_xl, bf16[160,256]{1,0:T(8,128)(2,1)S(1)} %collective-permute-done.9.from_diagonal, ...), custom_call_target="tpu_custom_call" | custom-call | flops 47185920 | bytes 4194304 | tf_op jit(solution)/shard_map/pallas_call | solution.py:112
  (46 shorter events, 9.9 us)
Async XLA Ops:
  7.2 34.9 %copy-start.3 = (bf16[192,640]{1,0:T(8,128)(2,1)S(1)}, bf16[192,640]{1,0:T(8,128)(2,1)}, u32[]{:S(2)}) copy-start(bf16[192,640]{1,0:T(8,128)(2,1)} %param.6) | copy-start | bytes 737284
  7.2 79.0 %all-gather.2.cloned.1.call-start = ((), (), s32[]{:S(2)}) async-start(), calls=%async_computation.1 | async-start | bytes 2437120 | tf_op jit(solution)/shard_map/all_gather | solution.py:264
  23.6 2.6 %collective-permute-start = (bf16[80,320]{1,0:T(8,128)(2,1)S(1)}, bf16[80,320]{1,0:T(8,128)(2,1)S(1)}, u32[]{:S(2)}, u32[]{:S(2)}) collective-permute-start(bf16[80,320]{1,0:T(8,128)(2,1)S(1)} %get-tuple-element.30), channel_id=1, source_target_pairs={{0,0},{1,65},{2,130},{3,195},{4,260},{5,325},{6,390},{7,455},{8,8}... | collective-permute-start | bytes 153608 | tf_op jit(solution)/shard_map/ppermute | solution.py:43
  24.3 8.0 %collective-permute-start.1 = (bf16[80,320]{1,0:T(8,128)(2,1)S(1)}, bf16[80,320]{1,0:T(8,128)(2,1)S(1)}, u32[]{:S(2)}, u32[]{:S(2)}) collective-permute-start(bf16[80,320]{1,0:T(8,128)(2,1)S(1)} %get-tuple-element.31), channel_id=1, source_target_pairs={{0,32},{1,97},{2,162},{3,227},{4,292},{5,357},{6,422},{7,487},{8,4... | collective-permute-start | bytes 153608 | tf_op jit(solution)/shard_map/ppermute | solution.py:43
  32.3 12.0 %collective-permute-start.2 = (bf16[80,768]{1,0:T(8,128)(2,1)S(1)}, bf16[80,768]{1,0:T(8,128)(2,1)S(1)}, u32[]{:S(2)}, u32[]{:S(2)}) collective-permute-start(bf16[80,768]{1,0:T(8,128)(2,1)S(1)} %pad_maximum_fusion.6), channel_id=1, source_target_pairs={{0,1},{1,0},{2,3},{3,2},{4,5},{5,4},{6,7},{7,6},{8,9},{9,8},{10,11... | collective-permute-start | bytes 368648 | tf_op jit(solution)/shard_map/ppermute | solution.py:43
  42.0 19.4 %collective-permute-start.5 = (bf16[192,640]{1,0:T(8,128)(2,1)S(1)}, bf16[192,640]{1,0:T(8,128)(2,1)S(1)}, u32[]{:S(2)}, u32[]{:S(2)}) collective-permute-start(bf16[192,640]{1,0:T(8,128)(2,1)S(1)} %copy-done.3), channel_id=1, source_target_pairs={{0,16},{1,17},{2,18},{3,19},{4,20},{5,21},{6,22},{7,23},{8,24},{9,... | collective-permute-start | bytes 737288 | tf_op jit(solution)/shard_map/ppermute | solution.py:43
  44.3 41.8 %copy-start.2 = (s32[1,192]{1,0:T(1,128)S(1)}, s32[1,192]{1,0:T(1,128)}, u32[]{:S(2)}) copy-start(s32[1,192]{1,0:T(1,128)} %member.3) | copy-start | bytes 2308
  44.3 25.1 %collective-permute-start.3 = (bf16[160,768]{1,0:T(8,128)(2,1)S(1)}, bf16[160,768]{1,0:T(8,128)(2,1)S(1)}, u32[]{:S(2)}, u32[]{:S(2)}) collective-permute-start(bf16[160,768]{1,0:T(8,128)(2,1)S(1)} %pad_maximum_fusion.4), channel_id=1, source_target_pairs={{0,2},{1,3},{2,0},{3,1},{4,6},{5,7},{6,4},{7,5},{8,10},{9,11},{10,... | collective-permute-start | bytes 737288 | tf_op jit(solution)/shard_map/ppermute | solution.py:43
  61.5 10.8 %collective-permute-start.6 = (bf16[384,640]{1,0:T(8,128)(2,1)S(1)}, bf16[384,640]{1,0:T(8,128)(2,1)}, u32[]{:S(2)}, u32[]{:S(2)}) collective-permute-start(bf16[384,640]{1,0:T(8,128)(2,1)S(1)} %pad_maximum_fusion.3), channel_id=1, source_target_pairs={{0,8},{1,9},{2,10},{3,11},{4,12},{5,13},{6,14},{7,15},{8,0},{9,1},... | collective-permute-start | bytes 1474568 | tf_op jit(solution)/shard_map/ppermute | solution.py:43
  69.5 14.1 %collective-permute-start.4 = (bf16[320,768]{1,0:T(8,128)(2,1)S(1)}, bf16[320,768]{1,0:T(8,128)(2,1)}, u32[]{:S(2)}, u32[]{:S(2)}) collective-permute-start(bf16[320,768]{1,0:T(8,128)(2,1)S(1)} %pad_maximum_fusion.2), channel_id=1, source_target_pairs={{0,4},{1,5},{2,6},{3,7},{4,0},{5,1},{6,2},{7,3},{8,12},{9,13},{10,... | collective-permute-start | bytes 1474568 | tf_op jit(solution)/shard_map/ppermute | solution.py:43
  89.6 1.4 copy-start.1
  91.0 12.2 %copy-start = (bf16[1792,640]{1,0:T(8,128)(2,1)S(1)}, bf16[1792,640]{1,0:T(8,128)(2,1)}, u32[]{:S(2)}) copy-start(bf16[1792,640]{1,0:T(8,128)(2,1)} %all-gather.2.cloned.1.call-done.slots) | copy-start | bytes 6881284
  91.0 32.0 %all-to-all-start = ((bf16[8,176,768]{2,1,0:T(8,128)(2,1)}), bf16[8,176,768]{2,1,0:T(8,128)(2,1)}, u32[]{:S(2)}, u32[]{:S(2)}) async-start(bf16[8,176,768]{2,1,0:T(8,128)(2,1)} %copy-done.1), calls=%async_computation | async-start | bytes 4325376 | tf_op jit(solution)/shard_map/all_to_all | solution.py:299
  105.1 11.5 %collective-permute-start.10 = (f32[160,640]{1,0:T(8,128)S(1)}, f32[160,640]{1,0:T(8,128)S(1)}, u32[]{:S(2)}, u32[]{:S(2)}) collective-permute-start(f32[160,640]{1,0:T(8,128)S(1)} %get-tuple-element.17), channel_id=1, source_target_pairs={{0,8},{1,9},{2,10},{3,11},{4,12},{5,13},{6,14},{7,15},{8,0},{9,1},... | collective-permute-start | bytes 1228808 | tf_op jit(solution)/shard_map/ppermute | solution.py:43
  117.2 26.7 %collective-permute-start.11 = (f32[80,640]{1,0:T(8,128)S(1)}, f32[80,640]{1,0:T(8,128)S(1)}, u32[]{:S(2)}, u32[]{:S(2)}) collective-permute-start(f32[80,640]{1,0:T(8,128)S(1)} %get-tuple-element.19), channel_id=1, source_target_pairs={{0,16},{1,17},{2,18},{3,19},{4,20},{5,21},{6,22},{7,23},{8,24},{9,... | collective-permute-start | bytes 614408 | tf_op jit(solution)/shard_map/ppermute | solution.py:43
  125.0 22.1 %collective-permute-start.7 = (f32[160,256]{1,0:T(8,128)S(1)}, f32[160,256]{1,0:T(8,128)S(1)}, u32[]{:S(2)}, u32[]{:S(2)}) collective-permute-start(f32[160,256]{1,0:T(8,128)S(1)} %get-tuple-element.12), channel_id=1, source_target_pairs={{0,8},{1,9},{2,10},{3,11},{4,12},{5,13},{6,14},{7,15},{8,0},{9,1},... | collective-permute-start | bytes 491528 | tf_op jit(solution)/shard_map/ppermute | solution.py:43
  138.4 6.2 %collective-permute-start.8 = (bf16[160,256]{1,0:T(8,128)(2,1)S(1)}, bf16[160,256]{1,0:T(8,128)(2,1)S(1)}, u32[]{:S(2)}, u32[]{:S(2)}) collective-permute-start(bf16[160,256]{1,0:T(8,128)(2,1)S(1)} %get-tuple-element.13), channel_id=1, source_target_pairs={{0,16},{1,17},{2,18},{3,19},{4,20},{5,21},{6,22},{7,23},{8,24},{9,... | collective-permute-start | bytes 245768 | tf_op jit(solution)/shard_map/ppermute | solution.py:43
  140.9 6.2 %collective-permute-start.9 = (bf16[160,256]{1,0:T(8,128)(2,1)S(1)}, bf16[160,256]{1,0:T(8,128)(2,1)S(1)}, u32[]{:S(2)}, u32[]{:S(2)}) collective-permute-start(bf16[160,256]{1,0:T(8,128)(2,1)S(1)} %get-tuple-element.14), channel_id=1, source_target_pairs={{0,24},{1,25},{2,26},{3,27},{4,28},{5,29},{6,30},{7,31},{8,16},{9,... | collective-permute-start | bytes 245768 | tf_op jit(solution)/shard_map/ppermute | solution.py:43
Sparse Core Ops, SparseCore 0:
  10.7 70.9 all-gather.1

commit v7 on v6

--- a/solution.py
+++ b/solution.py
@@ -55,6 +55,11 @@
     return (z, 1 - xl, core, y, xh)
 
 
+def half_target(z, xl, core, y, xh):
+    half = z // 2 % 2
+    return (z, xl, core, y, xh) if xh == half else (z ^ 2, xl, core, y, half)
+
+
 def xh_target(z, xl, core, y, xh):
     return (z, xl, core, y, 1 - xh)
 
@@ -80,23 +85,31 @@
     return high.astype(BF16), (value - high).astype(BF16)
 
 
-def product_kernel(place, slots, rows, left, member, give, weights):
-    for source in range(16):
-        block = slots[source * SLOT : source * SLOT + OUT_BLOCK, :]
-        weights[source * OUT_BLOCK : (source + 1) * OUT_BLOCK, :] = block
-    proj = nt_dot(left[...], rows[:ROWS, :])
+def product_kernel(place, slots, rows, left, other_left, member, give, weights, inputs):
+    xh = place[4]
+    for block in range(8):
+        for other in range(2):
+            source = 4 * (block // 2) + 2 * (xh ^ other) + block % 2
+            start = pl.multiple_of(source * SLOT, 16)
+            at = slice(block * OUT_BLOCK, (block + 1) * OUT_BLOCK)
+            weights[other, at, :] = slots[pl.ds(start, OUT_BLOCK), :]
+    for group in range(4):
+        for other in range(2):
+            at = slice(group * ROWS, (group + 1) * ROWS)
+            start = (2 * group + other) * ROWS
+            inputs[other, at, :] = rows[start : start + ROWS, :]
+
+    proj = nt_dot(left[...], rows[:ROWS, :]) + nt_dot(other_left[...], rows[ROWS : 2 * ROWS, :])
     owner = lax.broadcasted_iota(jnp.int32, (32, ROWS), 0) // RANK
     proj = jnp.where(owner == member[...], proj, 0.0)
     folded = proj[:8] + proj[8:16] + proj[16:24] + proj[24:]
     high = folded.astype(BF16).astype(F32)
     pair = jnp.concatenate([high, folded - high]).astype(BF16)
-    for part in range(2):
-        block = nt_dot(weights[part * 640 : part * 640 + 640, :], rows[...])
-        for i in range(4):
-            at = part * 4 + i
-            give[at, :160, :] = block[i * 160 : (i + 1) * 160].astype(BF16)
-            give[at, 160:, :] = jnp.zeros((16, GROUP_ROWS), BF16)
-            give[at, 160:, :ROWS] = pair
+    block = nt_dot(weights[0], inputs[0]) + nt_dot(weights[1], inputs[1])
+    for at in range(4):
+        give[at, :160, :] = block[at * 160 : (at + 1) * 160].astype(BF16)
+        give[at, 160:, :] = jnp.zeros((16, GROUP_ROWS), BF16)
+        give[at, 160:, :ROWS] = pair
 
 
 VMEM = pl.BlockSpec(memory_space=pltpu.VMEM)
@@ -141,7 +154,7 @@
 
 def sum_kernel(place, got, mine, coefficient, to_core, to_xl, to_diagonal):
     total, folded = 0.0, 0.0
-    for index in range(8):
+    for index in range(4):
         total = total + got[index, :160, :].astype(F32)
         pair = got[index, 160:, :256].astype(F32)[:, :ROWS]
         folded = folded + pair[:8] + pair[8:]
@@ -260,10 +273,12 @@
     left = left_factors.astype(BF16).reshape(32, IN_BLOCK)
     tensor = y * 2 + xh
     place = jnp.stack([z, core, xl ^ xh, y, xh, xl, tensor]).astype(jnp.int32)
-    slot = jnp.concatenate([base_weight.T.astype(BF16), left])
+    slot = jnp.concatenate([move(base_weight.T.astype(BF16), half_target), left])
     slots = lax.all_gather(slot, "z", axis=0, tiled=True)
 
-    rows = jnp.concatenate([tokens, move(tokens, xl_target)])
+    other = move(jnp.concatenate([tokens, left]), xh_target)
+    rows = jnp.concatenate([tokens, other[:ROWS]])
+    rows = jnp.concatenate([rows, move(rows, xl_target)])
     rows = jnp.concatenate([rows, move(rows, core_target)])
     right = gather_right(spread_right(right_factors, ranks, z, tensor))
     keep, give = call(
@@ -289,14 +304,14 @@
 
     (give,) = call(
         product_kernel,
-        (shape(8, GIVE, GROUP_ROWS, dtype=BF16),),
+        (shape(4, GIVE, GROUP_ROWS, dtype=BF16),),
         place + zero_after(right),
-        (slots, rows, left, member_of),
-        [pltpu.VMEM((2 * IN_BLOCK, IN_BLOCK), BF16)],
+        (slots, rows, left, other[ROWS:], member_of),
+        [pltpu.VMEM((2, IN_BLOCK, IN_BLOCK), BF16), pltpu.VMEM((2, GROUP_ROWS, IN_BLOCK), BF16)],
         flops=2 * 768 * 640 * 1280,
         moved=6 * 2**20,
     )
-    got = lax.all_to_all(give, TENSOR, split_axis=0, concat_axis=0, tiled=True)
+    got = lax.all_to_all(give, "y", split_axis=0, concat_axis=0, tiled=True)
     block = (160, 256)
     mine, coefficient, to_core, to_xl, to_diagonal = call(
         sum_kernel,

time: 157 us -> 150 us (0.955)
  starting transfers between devices: 84.5 us -> 80.1 us
  blocking collectives: 11.8 us -> 9.28 us
    all_to_all x1, starting transfers between devices: 11.1 us -> 4.86 us  [on_device(): got = lax.all_to_all(give, 'y', split_axis=0, concat_axis=0, tiled=True)]
    ppermute x12 -> x14, waiting for transfers between devices: 20.1 us -> 23.2 us  [move(): lax.ppermute(value, AXES, [(flat(p), flat(target(*p))) for p in places])]
    all_to_all x1, waiting for transfers between devices: 2.72 us -> 0.01 us  [on_device(): got = lax.all_to_all(give, 'y', split_axis=0, concat_axis=0, tiled=True)]
    all_gather x1, blocking collectives: 11.8 us -> 9.28 us  [rank_row(): every = lax.all_gather(own, ('xl', 'core'), axis=1, tiled=True)]
    ppermute x12 -> x14, starting transfers between devices: 73.4 us -> 75.2 us  [move(): lax.ppermute(value, AXES, [(flat(p), flat(target(*p))) for p in places])]
  transfers between devices with their start and end apart: 14 -> 16, of which waited for: 5 -> 6; matrix products, arithmetic and copies ran while one was open for 5% -> 6% of each run, Pallas kernels for 3% -> 2%
where the time goes in v7:
time: 150 us
  starting transfers between devices  80.1 us (53%)
  waiting for transfers between devices  23.3 us (16%)
  between operations  15.8 us (11%)
  blocking collectives  9.28 us (6%)
  Pallas kernels  8.71 us (6%)
  other arithmetic  7.17 us (5%)
  local copies, waits for them, and re-layouts  5.22 us (3%)
    ppermute x14, starting transfers between devices, move(): lax.ppermute(value, AXES, [(flat(p), flat(target(*p))) for p in places])  75.2 us
    ppermute x14, waiting for transfers between devices, move(): lax.ppermute(value, AXES, [(flat(p), flat(target(*p))) for p in places])  23.2 us
    all_gather x1, blocking collectives, rank_row(): every = lax.all_gather(own, ('xl', 'core'), axis=1, tiled=True)  9.28 us
    pallas_call x5, Pallas kernels, call(): pl.pallas_call(kernel, out_shape=outs, in_specs=[SMEM] + [VMEM] * len(arr...  8.71 us
    all_to_all x1, starting transfers between devices, on_device(): got = lax.all_to_all(give, 'y', split_axis=0, concat_axis=0, tiled=True)  4.86 us
  transfers between devices with their start and end apart: 16, of which 6 were waited for; matrix products, arithmetic and copies ran while one was open for 6% of the time, Pallas kernels for 2%

profile of v7, /device:TPU:1, one launch (start us, length us, event | category | flops | bytes accessed | tf_op | source)
XLA Modules:
  0.0 149.6 jit_solution(16944744030811557158)
XLA Ops:
  11.5 12.6 %collective-permute-start.6 = (bf16[224,640]{1,0:T(8,128)(2,1)S(1)}, bf16[224,640]{1,0:T(8,128)(2,1)S(1)}, u32[]{:S(2)}, u32[]{:S(2)}) collective-permute-start(bf16[224,640]{1,0:T(8,128)(2,1)S(1)} %pad_maximum_fusion.5), channel_id=1, source_target_pairs={{0,1},{1,0},{2,3},{3,2},{4,5},{5,4},{6,7},{7,6},{8,9},{9,8},{10,11... | collective-permute-start | bytes 860168 | tf_op jit(solution)/shard_map/ppermute | solution.py:43
  25.2 9.3 %all_gather.6 = bf16[16,512]{1,0:T(8,128)(2,1)S(1)} all-gather(bf16[16,128]{1,0:T(8,128)(2,1)S(1)} %pad.15), channel_id=1, replica_groups=mesh['z'=16,'xl'=2,'core'=2,'y'=4,'xh'=2] {'xl','core'}, dimensions={1}, use_global_device_ids=true | all-gather | bytes 20480 | tf_op jit(solution)/shard_map/all_gather | solution.py:201
  34.7 2.9 %collective-permute-start.7 = (bf16[384,640]{1,0:T(8,128)(2,1)S(1)}, bf16[384,640]{1,0:T(8,128)(2,1)S(1)}, u32[]{:S(2)}, u32[]{:S(2)}) collective-permute-start(bf16[384,640]{1,0:T(8,128)(2,1)S(1)} %pad_maximum_fusion.4), channel_id=1, source_target_pairs={{0,16},{1,17},{2,18},{3,19},{4,20},{5,21},{6,22},{7,23},{8,24},{9,... | collective-permute-start | bytes 1474568 | tf_op jit(solution)/shard_map/ppermute | solution.py:43
  38.3 2.6 %collective-permute-start.1 = (bf16[80,320]{1,0:T(8,128)(2,1)S(1)}, bf16[80,320]{1,0:T(8,128)(2,1)S(1)}, u32[]{:S(2)}, u32[]{:S(2)}) collective-permute-start(bf16[80,320]{1,0:T(8,128)(2,1)S(1)} %get-tuple-element.31), channel_id=1, source_target_pairs={{0,32},{1,97},{2,162},{3,227},{4,292},{5,357},{6,422},{7,487},{8,4... | collective-permute-start | bytes 153608 | tf_op jit(solution)/shard_map/ppermute | solution.py:43
  41.0 9.1 %collective-permute-done.1 = bf16[80,320]{1,0:T(8,128)(2,1)S(1)} collective-permute-done((bf16[80,320]{1,0:T(8,128)(2,1)S(1)}, bf16[80,320]{1,0:T(8,128)(2,1)S(1)}, u32[]{:S(2)}, u32[]{:S(2)}) %collective-permute-start.1) | collective-permute-done | bytes 51232 | tf_op jit(solution)/shard_map/ppermute | solution.py:43
  50.1 14.1 %collective-permute-start.2 = (bf16[80,768]{1,0:T(8,128)(2,1)S(1)}, bf16[80,768]{1,0:T(8,128)(2,1)S(1)}, u32[]{:S(2)}, u32[]{:S(2)}) collective-permute-start(bf16[80,768]{1,0:T(8,128)(2,1)S(1)} %pad_maximum_fusion.8), channel_id=1, source_target_pairs={{0,1},{1,0},{2,3},{3,2},{4,5},{5,4},{6,7},{7,6},{8,9},{9,8},{10,11... | collective-permute-start | bytes 368648 | tf_op jit(solution)/shard_map/ppermute | solution.py:43
  64.3 2.9 %collective-permute-done.2 = bf16[80,768]{1,0:T(8,128)(2,1)S(1)} collective-permute-done((bf16[80,768]{1,0:T(8,128)(2,1)S(1)}, bf16[80,768]{1,0:T(8,128)(2,1)S(1)}, u32[]{:S(2)}, u32[]{:S(2)}) %collective-permute-start.2) | collective-permute-done | bytes 122912 | tf_op jit(solution)/shard_map/ppermute | solution.py:43
  67.2 15.3 %collective-permute-start.3 = (bf16[160,768]{1,0:T(8,128)(2,1)S(1)}, bf16[160,768]{1,0:T(8,128)(2,1)S(1)}, u32[]{:S(2)}, u32[]{:S(2)}) collective-permute-start(bf16[160,768]{1,0:T(8,128)(2,1)S(1)} %pad_maximum_fusion.6), channel_id=1, source_target_pairs={{0,2},{1,3},{2,0},{3,1},{4,6},{5,7},{6,4},{7,5},{8,10},{9,11},{10,... | collective-permute-start | bytes 737288 | tf_op jit(solution)/shard_map/ppermute | solution.py:43
  82.6 3.5 %collective-permute-start.8 = (bf16[768,640]{1,0:T(8,128)(2,1)S(1)}, bf16[768,640]{1,0:T(8,128)(2,1)}, u32[]{:S(2)}, u32[]{:S(2)}) collective-permute-start(bf16[768,640]{1,0:T(8,128)(2,1)S(1)} %pad_maximum_fusion.1), channel_id=1, source_target_pairs={{0,8},{1,9},{2,10},{3,11},{4,12},{5,13},{6,14},{7,15},{8,0},{9,1},... | collective-permute-start | bytes 2949128 | tf_op jit(solution)/shard_map/ppermute | solution.py:43
  86.1 1.5 collective-permute-done.3
  87.6 4.3 %collective-permute-start.4 = (bf16[320,768]{1,0:T(8,128)(2,1)S(1)}, bf16[320,768]{1,0:T(8,128)(2,1)}, u32[]{:S(2)}, u32[]{:S(2)}) collective-permute-start(bf16[320,768]{1,0:T(8,128)(2,1)S(1)} %pad_maximum_fusion.3), channel_id=1, source_target_pairs={{0,4},{1,5},{2,6},{3,7},{4,0},{5,1},{6,2},{7,3},{8,12},{9,13},{10,... | collective-permute-start | bytes 1474568 | tf_op jit(solution)/shard_map/ppermute | solution.py:43
  92.7 8.1 %collective-permute-done.4 = bf16[320,768]{1,0:T(8,128)(2,1)} collective-permute-done((bf16[320,768]{1,0:T(8,128)(2,1)S(1)}, bf16[320,768]{1,0:T(8,128)(2,1)}, u32[]{:S(2)}, u32[]{:S(2)}) %collective-permute-start.4) | collective-permute-done | bytes 491552 | tf_op jit(solution)/shard_map/ppermute | solution.py:43
  100.8 1.3 slice.33
  103.4 1.4 pad_maximum_fusion.rows
  104.9 3.6 %shard_map.77 = bf16[4,176,768]{2,1,0:T(8,128)(2,1)S(1)} custom-call(s32[7]{0:T(128)S(1)} %broadcast_add_fusion.place, bf16[1792,640]{1,0:T(8,128)(2,1)} %all-gather.2.cloned.1.call-done.slots, bf16[1536,640]{1,0:T(8,128)(2,1)S(1)} %pad_maximum_fusion.rows, bf16[32,640]{1,0:T(8,128)(2,1)S(1)} %reshape.22.left, bf16[32,640]{1,0:T(8,128)(2,1)S(1)} %slice.35.other_left, ...), custom_call_target="tpu_custom_call" | custom-call | flops 1258291200 | bytes 6291456 | tf_op jit(solution)/shard_map/pallas_call | solution.py:125
  109.4 4.9 %all-to-all-start = ((bf16[4,176,768]{2,1,0:T(8,128)(2,1)}), bf16[4,176,768]{2,1,0:T(8,128)(2,1)S(1)}, u32[]{:S(2)}, u32[]{:S(2)}) async-start(bf16[4,176,768]{2,1,0:T(8,128)(2,1)} %copy-done.1), calls=%async_computation | async-start | bytes 2162688 | tf_op jit(solution)/shard_map/all_to_all | solution.py:314
  115.5 1.9 %shard_map.80 = (f32[160,640]{1,0:T(8,128)S(1)}, f32[160,640]{1,0:T(8,128)S(1)}) custom-call(s32[7]{0:T(128)S(1)} %stack.31.place, bf16[1792,640]{1,0:T(8,128)(2,1)S(1)} %copy-done, bf16[640,768]{1,0:T(8,128)(2,1)S(1)} %pad_maximum_fusion.2.right), custom_call_target="tpu_custom_call" | custom-call | flops 503316480 | bytes 4194304 | tf_op jit(solution)/shard_map/pallas_call | solution.py:125
  117.4 7.6 %collective-permute-start.12 = (f32[160,640]{1,0:T(8,128)S(1)}, f32[160,640]{1,0:T(8,128)S(1)}, u32[]{:S(2)}, u32[]{:S(2)}) collective-permute-start(f32[160,640]{1,0:T(8,128)S(1)} %get-tuple-element.17), channel_id=1, source_target_pairs={{0,8},{1,9},{2,10},{3,11},{4,12},{5,13},{6,14},{7,15},{8,0},{9,1},... | collective-permute-start | bytes 1228808 | tf_op jit(solution)/shard_map/ppermute | solution.py:43
  125.0 1.4 collective-permute-done.12.got
  126.9 2.4 %collective-permute-start.13 = (f32[80,640]{1,0:T(8,128)S(1)}, f32[80,640]{1,0:T(8,128)S(1)}, u32[]{:S(2)}, u32[]{:S(2)}) collective-permute-start(f32[80,640]{1,0:T(8,128)S(1)} %get-tuple-element.19), channel_id=1, source_target_pairs={{0,16},{1,17},{2,18},{3,19},{4,20},{5,21},{6,22},{7,23},{8,24},{9,... | collective-permute-start | bytes 614408 | tf_op jit(solution)/shard_map/ppermute | solution.py:43
  131.1 2.8 %collective-permute-start.10 = (bf16[160,256]{1,0:T(8,128)(2,1)S(1)}, bf16[160,256]{1,0:T(8,128)(2,1)S(1)}, u32[]{:S(2)}, u32[]{:S(2)}) collective-permute-start(bf16[160,256]{1,0:T(8,128)(2,1)S(1)} %get-tuple-element.13), channel_id=1, source_target_pairs={{0,16},{1,17},{2,18},{3,19},{4,20},{5,21},{6,22},{7,23},{8,24},{9,... | collective-permute-start | bytes 245768 | tf_op jit(solution)/shard_map/ppermute | solution.py:43
  133.9 3.5 %collective-permute-start.11 = (bf16[160,256]{1,0:T(8,128)(2,1)S(1)}, bf16[160,256]{1,0:T(8,128)(2,1)S(1)}, u32[]{:S(2)}, u32[]{:S(2)}) collective-permute-start(bf16[160,256]{1,0:T(8,128)(2,1)S(1)} %get-tuple-element.14), channel_id=1, source_target_pairs={{0,24},{1,25},{2,26},{3,27},{4,28},{5,29},{6,30},{7,31},{8,16},{9,... | collective-permute-start | bytes 245768 | tf_op jit(solution)/shard_map/ppermute | solution.py:43
  137.5 2.3 %collective-permute-start.9 = (f32[160,256]{1,0:T(8,128)S(1)}, f32[160,256]{1,0:T(8,128)S(1)}, u32[]{:S(2)}, u32[]{:S(2)}) collective-permute-start(f32[160,256]{1,0:T(8,128)S(1)} %get-tuple-element.12), channel_id=1, source_target_pairs={{0,8},{1,9},{2,10},{3,11},{4,12},{5,13},{6,14},{7,15},{8,0},{9,1},... | collective-permute-start | bytes 491528 | tf_op jit(solution)/shard_map/ppermute | solution.py:43
  140.8 1.9 %shard_map.79 = f32[192,640]{1,0:T(8,128)} custom-call(s32[7]{0:T(128)S(1)} %stack.31.place, f32[160,256]{1,0:T(8,128)S(1)} %get-tuple-element.11.mine, f32[160,256]{1,0:T(8,128)S(1)} %collective-permute-done.9.from_core, bf16[160,256]{1,0:T(8,128)(2,1)S(1)} %collective-permute-done.10.from_xl, bf16[160,256]{1,0:T(8,128)(2,1)S(1)} %collective-permute-done.11.from_diagonal, ...), custom_call_target="tpu_custom_call" | custom-call | flops 47185920 | bytes 4194304 | tf_op jit(solution)/shard_map/pallas_call | solution.py:125
  (62 shorter events, 12.8 us)
Async XLA Ops:
  7.2 27.5 %copy-start.3 = (bf16[192,640]{1,0:T(8,128)(2,1)S(1)}, bf16[192,640]{1,0:T(8,128)(2,1)}, u32[]{:S(2)}) copy-start(bf16[192,640]{1,0:T(8,128)(2,1)} %param.6) | copy-start | bytes 737284
  7.2 18.0 %copy-start.7 = (s32[8]{0:T(128)S(1)}, s32[8]{0:T(128)}, u32[]{:S(2)}) copy-start(s32[8]{0:T(128)} %param.11) | copy-start | bytes 100
  7.2 97.6 %all-gather.2.cloned.1.call-start = ((), (), s32[]{:S(2)}) async-start(), calls=%async_computation.1 | async-start | bytes 2437120 | tf_op jit(solution)/shard_map/all_gather | solution.py:277
  8.2 1.6 %collective-permute-start.5 = (bf16[80,640]{1,0:T(8,128)(2,1)S(1)}, bf16[80,640]{1,0:T(8,128)(2,1)S(1)}, u32[]{:S(2)}, u32[]{:S(2)}) collective-permute-start(bf16[80,640]{1,0:T(8,128)(2,1)S(1)} %convert_bitcast_fusion), channel_id=1, source_target_pairs={{0,0},{1,64},{2,2},{3,66},{4,4},{5,68},{6,6},{7,70},{8,8},{9,72},{... | collective-permute-start | bytes 307208 | tf_op jit(solution)/shard_map/ppermute | solution.py:43
  11.5 23.1 %collective-permute-start.6 = (bf16[224,640]{1,0:T(8,128)(2,1)S(1)}, bf16[224,640]{1,0:T(8,128)(2,1)S(1)}, u32[]{:S(2)}, u32[]{:S(2)}) collective-permute-start(bf16[224,640]{1,0:T(8,128)(2,1)S(1)} %pad_maximum_fusion.5), channel_id=1, source_target_pairs={{0,1},{1,0},{2,3},{3,2},{4,5},{5,4},{6,7},{7,6},{8,9},{9,8},{10,11... | collective-permute-start | bytes 860168 | tf_op jit(solution)/shard_map/ppermute | solution.py:43
  34.6 47.8 %copy-start.6 = (bf16[224,640]{1,0:T(8,128)(2,1)}, bf16[224,640]{1,0:T(8,128)(2,1)S(1)}, u32[]{:S(2)}) copy-start(bf16[224,640]{1,0:T(8,128)(2,1)S(1)} %collective-permute-done.6) | copy-start | bytes 860164
  34.7 47.7 %collective-permute-start.7 = (bf16[384,640]{1,0:T(8,128)(2,1)S(1)}, bf16[384,640]{1,0:T(8,128)(2,1)S(1)}, u32[]{:S(2)}, u32[]{:S(2)}) collective-permute-start(bf16[384,640]{1,0:T(8,128)(2,1)S(1)} %pad_maximum_fusion.4), channel_id=1, source_target_pairs={{0,16},{1,17},{2,18},{3,19},{4,20},{5,21},{6,22},{7,23},{8,24},{9,... | collective-permute-start | bytes 1474568 | tf_op jit(solution)/shard_map/ppermute | solution.py:43
  37.7 3.3 %collective-permute-start = (bf16[80,320]{1,0:T(8,128)(2,1)S(1)}, bf16[80,320]{1,0:T(8,128)(2,1)S(1)}, u32[]{:S(2)}, u32[]{:S(2)}) collective-permute-start(bf16[80,320]{1,0:T(8,128)(2,1)S(1)} %get-tuple-element.30), channel_id=1, source_target_pairs={{0,0},{1,65},{2,130},{3,195},{4,260},{5,325},{6,390},{7,455},{8,8}... | collective-permute-start | bytes 153608 | tf_op jit(solution)/shard_map/ppermute | solution.py:43
  38.3 11.8 %collective-permute-start.1 = (bf16[80,320]{1,0:T(8,128)(2,1)S(1)}, bf16[80,320]{1,0:T(8,128)(2,1)S(1)}, u32[]{:S(2)}, u32[]{:S(2)}) collective-permute-start(bf16[80,320]{1,0:T(8,128)(2,1)S(1)} %get-tuple-element.31), channel_id=1, source_target_pairs={{0,32},{1,97},{2,162},{3,227},{4,292},{5,357},{6,422},{7,487},{8,4... | collective-permute-start | bytes 153608 | tf_op jit(solution)/shard_map/ppermute | solution.py:43
  50.1 17.0 %collective-permute-start.2 = (bf16[80,768]{1,0:T(8,128)(2,1)S(1)}, bf16[80,768]{1,0:T(8,128)(2,1)S(1)}, u32[]{:S(2)}, u32[]{:S(2)}) collective-permute-start(bf16[80,768]{1,0:T(8,128)(2,1)S(1)} %pad_maximum_fusion.8), channel_id=1, source_target_pairs={{0,1},{1,0},{2,3},{3,2},{4,5},{5,4},{6,7},{7,6},{8,9},{9,8},{10,11... | collective-permute-start | bytes 368648 | tf_op jit(solution)/shard_map/ppermute | solution.py:43
  67.2 37.7 %copy-start.4 = (bf16[80,768]{1,0:T(8,128)(2,1)}, bf16[80,768]{1,0:T(8,128)(2,1)S(1)}, u32[]{:S(2)}) copy-start(bf16[80,768]{1,0:T(8,128)(2,1)S(1)} %collective-permute-done.2) | copy-start | bytes 368644
  67.2 20.3 %collective-permute-start.3 = (bf16[160,768]{1,0:T(8,128)(2,1)S(1)}, bf16[160,768]{1,0:T(8,128)(2,1)S(1)}, u32[]{:S(2)}, u32[]{:S(2)}) collective-permute-start(bf16[160,768]{1,0:T(8,128)(2,1)S(1)} %pad_maximum_fusion.6), channel_id=1, source_target_pairs={{0,2},{1,3},{2,0},{3,1},{4,6},{5,7},{6,4},{7,5},{8,10},{9,11},{10,... | collective-permute-start | bytes 737288 | tf_op jit(solution)/shard_map/ppermute | solution.py:43
  82.6 20.9 %collective-permute-start.8 = (bf16[768,640]{1,0:T(8,128)(2,1)S(1)}, bf16[768,640]{1,0:T(8,128)(2,1)}, u32[]{:S(2)}, u32[]{:S(2)}) collective-permute-start(bf16[768,640]{1,0:T(8,128)(2,1)S(1)} %pad_maximum_fusion.1), channel_id=1, source_target_pairs={{0,8},{1,9},{2,10},{3,11},{4,12},{5,13},{6,14},{7,15},{8,0},{9,1},... | collective-permute-start | bytes 2949128 | tf_op jit(solution)/shard_map/ppermute | solution.py:43
  87.5 15.9 %copy-start.5 = (bf16[160,768]{1,0:T(8,128)(2,1)}, bf16[160,768]{1,0:T(8,128)(2,1)S(1)}, u32[]{:S(2)}) copy-start(bf16[160,768]{1,0:T(8,128)(2,1)S(1)} %collective-permute-done.3) | copy-start | bytes 737284
  87.6 13.3 %collective-permute-start.4 = (bf16[320,768]{1,0:T(8,128)(2,1)S(1)}, bf16[320,768]{1,0:T(8,128)(2,1)}, u32[]{:S(2)}, u32[]{:S(2)}) collective-permute-start(bf16[320,768]{1,0:T(8,128)(2,1)S(1)} %pad_maximum_fusion.3), channel_id=1, source_target_pairs={{0,4},{1,5},{2,6},{3,7},{4,0},{5,1},{6,2},{7,3},{8,12},{9,13},{10,... | collective-permute-start | bytes 1474568 | tf_op jit(solution)/shard_map/ppermute | solution.py:43
  103.4 1.4 copy-start.2
  108.4 1.0 copy-start.1
  109.4 6.1 %copy-start = (bf16[1792,640]{1,0:T(8,128)(2,1)S(1)}, bf16[1792,640]{1,0:T(8,128)(2,1)}, u32[]{:S(2)}) copy-start(bf16[1792,640]{1,0:T(8,128)(2,1)} %all-gather.2.cloned.1.call-done.slots) | copy-start | bytes 6881284
  109.4 20.9 %all-to-all-start = ((bf16[4,176,768]{2,1,0:T(8,128)(2,1)}), bf16[4,176,768]{2,1,0:T(8,128)(2,1)S(1)}, u32[]{:S(2)}, u32[]{:S(2)}) async-start(bf16[4,176,768]{2,1,0:T(8,128)(2,1)} %copy-done.1), calls=%async_computation | async-start | bytes 2162688 | tf_op jit(solution)/shard_map/all_to_all | solution.py:314
  117.4 8.9 %collective-permute-start.12 = (f32[160,640]{1,0:T(8,128)S(1)}, f32[160,640]{1,0:T(8,128)S(1)}, u32[]{:S(2)}, u32[]{:S(2)}) collective-permute-start(f32[160,640]{1,0:T(8,128)S(1)} %get-tuple-element.17), channel_id=1, source_target_pairs={{0,8},{1,9},{2,10},{3,11},{4,12},{5,13},{6,14},{7,15},{8,0},{9,1},... | collective-permute-start | bytes 1228808 | tf_op jit(solution)/shard_map/ppermute | solution.py:43
  126.9 12.8 %collective-permute-start.13 = (f32[80,640]{1,0:T(8,128)S(1)}, f32[80,640]{1,0:T(8,128)S(1)}, u32[]{:S(2)}, u32[]{:S(2)}) collective-permute-start(f32[80,640]{1,0:T(8,128)S(1)} %get-tuple-element.19), channel_id=1, source_target_pairs={{0,16},{1,17},{2,18},{3,19},{4,20},{5,21},{6,22},{7,23},{8,24},{9,... | collective-permute-start | bytes 614408 | tf_op jit(solution)/shard_map/ppermute | solution.py:43
  131.1 9.4 %collective-permute-start.10 = (bf16[160,256]{1,0:T(8,128)(2,1)S(1)}, bf16[160,256]{1,0:T(8,128)(2,1)S(1)}, u32[]{:S(2)}, u32[]{:S(2)}) collective-permute-start(bf16[160,256]{1,0:T(8,128)(2,1)S(1)} %get-tuple-element.13), channel_id=1, source_target_pairs={{0,16},{1,17},{2,18},{3,19},{4,20},{5,21},{6,22},{7,23},{8,24},{9,... | collective-permute-start | bytes 245768 | tf_op jit(solution)/shard_map/ppermute | solution.py:43
  133.9 6.6 %collective-permute-start.11 = (bf16[160,256]{1,0:T(8,128)(2,1)S(1)}, bf16[160,256]{1,0:T(8,128)(2,1)S(1)}, u32[]{:S(2)}, u32[]{:S(2)}) collective-permute-start(bf16[160,256]{1,0:T(8,128)(2,1)S(1)} %get-tuple-element.14), channel_id=1, source_target_pairs={{0,24},{1,25},{2,26},{3,27},{4,28},{5,29},{6,30},{7,31},{8,16},{9,... | collective-permute-start | bytes 245768 | tf_op jit(solution)/shard_map/ppermute | solution.py:43
  137.5 3.3 %collective-permute-start.9 = (f32[160,256]{1,0:T(8,128)S(1)}, f32[160,256]{1,0:T(8,128)S(1)}, u32[]{:S(2)}, u32[]{:S(2)}) collective-permute-start(f32[160,256]{1,0:T(8,128)S(1)} %get-tuple-element.12), channel_id=1, source_target_pairs={{0,8},{1,9},{2,10},{3,11},{4,12},{5,13},{6,14},{7,15},{8,0},{9,1},... | collective-permute-start | bytes 491528 | tf_op jit(solution)/shard_map/ppermute | solution.py:43
Sparse Core Ops, SparseCore 0:
  10.7 81.7 all-gather.1

commit v8 on v7

--- a/solution.py
+++ b/solution.py
@@ -203,8 +203,11 @@
     return jnp.pad(every, ((0, 0), (0, 320 - 4 * M_DEV)))
 
 
-def spread_right(right_factors, ranks, z, tensor):
-    levels = rank_row(ranks)
+def after(value, other):
+    return jnp.where(other[0, 0] == other[0, 0], value, jnp.zeros_like(value))
+
+
+def spread_right(right_factors, levels, z, tensor):
     parts = []
     for near in range(2):
         start = lax.rem(z + 2 * tensor + near, 16) * 320
@@ -276,11 +279,12 @@
     slot = jnp.concatenate([move(base_weight.T.astype(BF16), half_target), left])
     slots = lax.all_gather(slot, "z", axis=0, tiled=True)
 
-    other = move(jnp.concatenate([tokens, left]), xh_target)
+    levels = rank_row(ranks)
+    other = move(after(jnp.concatenate([tokens, left]), levels), xh_target)
     rows = jnp.concatenate([tokens, other[:ROWS]])
     rows = jnp.concatenate([rows, move(rows, xl_target)])
     rows = jnp.concatenate([rows, move(rows, core_target)])
-    right = gather_right(spread_right(right_factors, ranks, z, tensor))
+    right = gather_right(spread_right(right_factors, levels, z, tensor))
     keep, give = call(
         functools.partial(update_kernel, members),
         (shape(160, IN_BLOCK), shape(160, IN_BLOCK)),

time: 150 us -> 157 us (1.047)
  waiting for transfers between devices: 23.3 us -> 29.8 us
  starting transfers between devices: 80.1 us -> 74.9 us
  blocking collectives: 9.28 us -> 11.8 us
    ppermute x14, waiting for transfers between devices: 23.2 us -> 29.8 us  [move(): lax.ppermute(value, AXES, [(flat(p), flat(target(*p))) for p in places])]
    ppermute x14, starting transfers between devices: 75.2 us -> 70 us  [move(): lax.ppermute(value, AXES, [(flat(p), flat(target(*p))) for p in places])]
    all_gather x1, blocking collectives: 9.28 us -> 11.8 us  [rank_row(): every = lax.all_gather(own, ('xl', 'core'), axis=1, tiled=True)]
  transfers between devices with their start and end apart: 16 -> 16, of which waited for: 6 -> 6; matrix products, arithmetic and copies ran while one was open for 6% -> 7% of each run, Pallas kernels for 2% -> 2%
where the time goes in v8:
time: 157 us; the launch traced here: 156 us
  starting transfers between devices  74.9 us (48%)
  waiting for transfers between devices  29.8 us (19%)
  between operations  17.1 us (11%)
  blocking collectives  11.8 us (8%)
  Pallas kernels  8.72 us (6%)
  other arithmetic  7.88 us (5%)
  local copies, waits for them, and re-layouts  5.75 us (4%)
    ppermute x14, starting transfers between devices, move(): lax.ppermute(value, AXES, [(flat(p), flat(target(*p))) for p in places])  70 us
    ppermute x14, waiting for transfers between devices, move(): lax.ppermute(value, AXES, [(flat(p), flat(target(*p))) for p in places])  29.8 us
    all_gather x1, blocking collectives, rank_row(): every = lax.all_gather(own, ('xl', 'core'), axis=1, tiled=True)  11.8 us
    pallas_call x5, Pallas kernels, call(): pl.pallas_call(kernel, out_shape=outs, in_specs=[SMEM] + [VMEM] * len(arr...  8.72 us
    all_to_all x1, starting transfers between devices, on_device(): got = lax.all_to_all(give, 'y', split_axis=0, concat_axis=0, tiled=True)  4.89 us
  transfers between devices with their start and end apart: 16, of which 6 were waited for; matrix products, arithmetic and copies ran while one was open for 7% of the time, Pallas kernels for 2%

profile of v8, /device:TPU:1, one launch (start us, length us, event | category | flops | bytes accessed | tf_op | source)
XLA Modules:
  0.0 156.0 jit_solution(11483233102738722469)
XLA Ops:
  11.2 11.8 %all_gather.6 = bf16[16,512]{1,0:T(8,128)(2,1)S(1)} all-gather(bf16[16,128]{1,0:T(8,128)(2,1)S(1)} %pad.15), channel_id=1, replica_groups=mesh['z'=16,'xl'=2,'core'=2,'y'=4,'xh'=2] {'xl','core'}, dimensions={1}, use_global_device_ids=true | all-gather | bytes 20480 | tf_op jit(solution)/shard_map/all_gather | solution.py:201
  25.9 9.7 %collective-permute-start.6 = (bf16[224,640]{1,0:T(8,128)(2,1)S(1)}, bf16[224,640]{1,0:T(8,128)(2,1)S(1)}, u32[]{:S(2)}, u32[]{:S(2)}) collective-permute-start(bf16[224,640]{1,0:T(8,128)(2,1)S(1)} %maximum_select_fusion), channel_id=1, source_target_pairs={{0,1},{1,0},{2,3},{3,2},{4,5},{5,4},{6,7},{7,6},{8,9},{9,8},{10,11... | collective-permute-start | bytes 860168 | tf_op jit(solution)/shard_map/ppermute | solution.py:43
  36.8 5.9 %collective-permute-done.6 = bf16[224,640]{1,0:T(8,128)(2,1)S(1)} collective-permute-done((bf16[224,640]{1,0:T(8,128)(2,1)S(1)}, bf16[224,640]{1,0:T(8,128)(2,1)S(1)}, u32[]{:S(2)}, u32[]{:S(2)}) %collective-permute-start.6) | collective-permute-done | bytes 286752 | tf_op jit(solution)/shard_map/ppermute | solution.py:43
  42.8 2.2 %collective-permute-start.7 = (bf16[384,640]{1,0:T(8,128)(2,1)S(1)}, bf16[384,640]{1,0:T(8,128)(2,1)S(1)}, u32[]{:S(2)}, u32[]{:S(2)}) collective-permute-start(bf16[384,640]{1,0:T(8,128)(2,1)S(1)} %pad_maximum_fusion.4), channel_id=1, source_target_pairs={{0,16},{1,17},{2,18},{3,19},{4,20},{5,21},{6,22},{7,23},{8,24},{9,... | collective-permute-start | bytes 1474568 | tf_op jit(solution)/shard_map/ppermute | solution.py:43
  45.7 1.9 %collective-permute-start.1 = (bf16[80,320]{1,0:T(8,128)(2,1)S(1)}, bf16[80,320]{1,0:T(8,128)(2,1)S(1)}, u32[]{:S(2)}, u32[]{:S(2)}) collective-permute-start(bf16[80,320]{1,0:T(8,128)(2,1)S(1)} %get-tuple-element.31), channel_id=1, source_target_pairs={{0,32},{1,97},{2,162},{3,227},{4,292},{5,357},{6,422},{7,487},{8,4... | collective-permute-start | bytes 153608 | tf_op jit(solution)/shard_map/ppermute | solution.py:43
  47.7 12.5 %collective-permute-done.1 = bf16[80,320]{1,0:T(8,128)(2,1)S(1)} collective-permute-done((bf16[80,320]{1,0:T(8,128)(2,1)S(1)}, bf16[80,320]{1,0:T(8,128)(2,1)S(1)}, u32[]{:S(2)}, u32[]{:S(2)}) %collective-permute-start.1) | collective-permute-done | bytes 51232 | tf_op jit(solution)/shard_map/ppermute | solution.py:43
  60.2 8.9 %collective-permute-start.2 = (bf16[80,768]{1,0:T(8,128)(2,1)S(1)}, bf16[80,768]{1,0:T(8,128)(2,1)S(1)}, u32[]{:S(2)}, u32[]{:S(2)}) collective-permute-start(bf16[80,768]{1,0:T(8,128)(2,1)S(1)} %pad_maximum_fusion.7), channel_id=1, source_target_pairs={{0,1},{1,0},{2,3},{3,2},{4,5},{5,4},{6,7},{7,6},{8,9},{9,8},{10,11... | collective-permute-start | bytes 368648 | tf_op jit(solution)/shard_map/ppermute | solution.py:43
  69.1 2.3 %collective-permute-done.2 = bf16[80,768]{1,0:T(8,128)(2,1)S(1)} collective-permute-done((bf16[80,768]{1,0:T(8,128)(2,1)S(1)}, bf16[80,768]{1,0:T(8,128)(2,1)S(1)}, u32[]{:S(2)}, u32[]{:S(2)}) %collective-permute-start.2) | collective-permute-done | bytes 122912 | tf_op jit(solution)/shard_map/ppermute | solution.py:43
  71.4 14.2 %collective-permute-start.3 = (bf16[160,768]{1,0:T(8,128)(2,1)S(1)}, bf16[160,768]{1,0:T(8,128)(2,1)S(1)}, u32[]{:S(2)}, u32[]{:S(2)}) collective-permute-start(bf16[160,768]{1,0:T(8,128)(2,1)S(1)} %pad_maximum_fusion.5), channel_id=1, source_target_pairs={{0,2},{1,3},{2,0},{3,1},{4,6},{5,7},{6,4},{7,5},{8,10},{9,11},{10,... | collective-permute-start | bytes 737288 | tf_op jit(solution)/shard_map/ppermute | solution.py:43
  85.7 7.9 %collective-permute-start.8 = (bf16[768,640]{1,0:T(8,128)(2,1)S(1)}, bf16[768,640]{1,0:T(8,128)(2,1)}, u32[]{:S(2)}, u32[]{:S(2)}) collective-permute-start(bf16[768,640]{1,0:T(8,128)(2,1)S(1)} %pad_maximum_fusion.1), channel_id=1, source_target_pairs={{0,8},{1,9},{2,10},{3,11},{4,12},{5,13},{6,14},{7,15},{8,0},{9,1},... | collective-permute-start | bytes 2949128 | tf_op jit(solution)/shard_map/ppermute | solution.py:43
  93.7 5.2 %collective-permute-start.4 = (bf16[320,768]{1,0:T(8,128)(2,1)S(1)}, bf16[320,768]{1,0:T(8,128)(2,1)}, u32[]{:S(2)}, u32[]{:S(2)}) collective-permute-start(bf16[320,768]{1,0:T(8,128)(2,1)S(1)} %pad_maximum_fusion.3), channel_id=1, source_target_pairs={{0,4},{1,5},{2,6},{3,7},{4,0},{5,1},{6,2},{7,3},{8,12},{9,13},{10,... | collective-permute-start | bytes 1474568 | tf_op jit(solution)/shard_map/ppermute | solution.py:43
  99.8 7.5 %collective-permute-done.4 = bf16[320,768]{1,0:T(8,128)(2,1)} collective-permute-done((bf16[320,768]{1,0:T(8,128)(2,1)S(1)}, bf16[320,768]{1,0:T(8,128)(2,1)}, u32[]{:S(2)}, u32[]{:S(2)}) %collective-permute-start.4) | collective-permute-done | bytes 491552 | tf_op jit(solution)/shard_map/ppermute | solution.py:43
  107.3 1.3 slice.41
  109.9 1.4 pad_maximum_fusion.rows
  111.3 3.6 %shard_map.77 = bf16[4,176,768]{2,1,0:T(8,128)(2,1)S(1)} custom-call(s32[7]{0:T(128)S(1)} %broadcast_add_fusion.place, bf16[1792,640]{1,0:T(8,128)(2,1)} %all-gather.2.cloned.1.call-done.slots, bf16[1536,640]{1,0:T(8,128)(2,1)S(1)} %pad_maximum_fusion.rows, bf16[32,640]{1,0:T(8,128)(2,1)S(1)} %reshape.23.left, bf16[32,640]{1,0:T(8,128)(2,1)S(1)} %slice.44.other_left, ...), custom_call_target="tpu_custom_call" | custom-call | flops 1258291200 | bytes 6291456 | tf_op jit(solution)/shard_map/pallas_call | solution.py:125
  115.9 4.9 %all-to-all-start = ((bf16[4,176,768]{2,1,0:T(8,128)(2,1)}), bf16[4,176,768]{2,1,0:T(8,128)(2,1)S(1)}, u32[]{:S(2)}, u32[]{:S(2)}) async-start(bf16[4,176,768]{2,1,0:T(8,128)(2,1)} %copy-done.1), calls=%async_computation | async-start | bytes 2162688 | tf_op jit(solution)/shard_map/all_to_all | solution.py:318
  122.0 1.9 %shard_map.80 = (f32[160,640]{1,0:T(8,128)S(1)}, f32[160,640]{1,0:T(8,128)S(1)}) custom-call(s32[7]{0:T(128)S(1)} %stack.31.place, bf16[1792,640]{1,0:T(8,128)(2,1)S(1)} %copy-done, bf16[640,768]{1,0:T(8,128)(2,1)S(1)} %pad_maximum_fusion.2.right), custom_call_target="tpu_custom_call" | custom-call | flops 503316480 | bytes 4194304 | tf_op jit(solution)/shard_map/pallas_call | solution.py:125
  123.9 5.5 %collective-permute-start.12 = (f32[160,640]{1,0:T(8,128)S(1)}, f32[160,640]{1,0:T(8,128)S(1)}, u32[]{:S(2)}, u32[]{:S(2)}) collective-permute-start(f32[160,640]{1,0:T(8,128)S(1)} %get-tuple-element.17), channel_id=1, source_target_pairs={{0,8},{1,9},{2,10},{3,11},{4,12},{5,13},{6,14},{7,15},{8,0},{9,1},... | collective-permute-start | bytes 1228808 | tf_op jit(solution)/shard_map/ppermute | solution.py:43
  129.5 1.4 collective-permute-done.12.got
  131.4 3.8 %collective-permute-start.13 = (f32[80,640]{1,0:T(8,128)S(1)}, f32[80,640]{1,0:T(8,128)S(1)}, u32[]{:S(2)}, u32[]{:S(2)}) collective-permute-start(f32[80,640]{1,0:T(8,128)S(1)} %get-tuple-element.19), channel_id=1, source_target_pairs={{0,16},{1,17},{2,18},{3,19},{4,20},{5,21},{6,22},{7,23},{8,24},{9,... | collective-permute-start | bytes 614408 | tf_op jit(solution)/shard_map/ppermute | solution.py:43
  137.0 1.9 %collective-permute-start.10 = (bf16[160,256]{1,0:T(8,128)(2,1)S(1)}, bf16[160,256]{1,0:T(8,128)(2,1)S(1)}, u32[]{:S(2)}, u32[]{:S(2)}) collective-permute-start(bf16[160,256]{1,0:T(8,128)(2,1)S(1)} %get-tuple-element.13), channel_id=1, source_target_pairs={{0,16},{1,17},{2,18},{3,19},{4,20},{5,21},{6,22},{7,23},{8,24},{9,... | collective-permute-start | bytes 245768 | tf_op jit(solution)/shard_map/ppermute | solution.py:43
  138.9 5.0 %collective-permute-start.11 = (bf16[160,256]{1,0:T(8,128)(2,1)S(1)}, bf16[160,256]{1,0:T(8,128)(2,1)S(1)}, u32[]{:S(2)}, u32[]{:S(2)}) collective-permute-start(bf16[160,256]{1,0:T(8,128)(2,1)S(1)} %get-tuple-element.14), channel_id=1, source_target_pairs={{0,24},{1,25},{2,26},{3,27},{4,28},{5,29},{6,30},{7,31},{8,16},{9,... | collective-permute-start | bytes 245768 | tf_op jit(solution)/shard_map/ppermute | solution.py:43
  143.9 2.3 %collective-permute-start.9 = (f32[160,256]{1,0:T(8,128)S(1)}, f32[160,256]{1,0:T(8,128)S(1)}, u32[]{:S(2)}, u32[]{:S(2)}) collective-permute-start(f32[160,256]{1,0:T(8,128)S(1)} %get-tuple-element.12), channel_id=1, source_target_pairs={{0,8},{1,9},{2,10},{3,11},{4,12},{5,13},{6,14},{7,15},{8,0},{9,1},... | collective-permute-start | bytes 491528 | tf_op jit(solution)/shard_map/ppermute | solution.py:43
  147.2 1.9 %shard_map.79 = f32[192,640]{1,0:T(8,128)} custom-call(s32[7]{0:T(128)S(1)} %stack.31.place, f32[160,256]{1,0:T(8,128)S(1)} %get-tuple-element.11.mine, f32[160,256]{1,0:T(8,128)S(1)} %collective-permute-done.9.from_core, bf16[160,256]{1,0:T(8,128)(2,1)S(1)} %collective-permute-done.10.from_xl, bf16[160,256]{1,0:T(8,128)(2,1)S(1)} %collective-permute-done.11.from_diagonal, ...), custom_call_target="tpu_custom_call" | custom-call | flops 47185920 | bytes 4194304 | tf_op jit(solution)/shard_map/pallas_call | solution.py:125
  (61 shorter events, 14.0 us)
Async XLA Ops:
  7.2 35.6 %copy-start.3 = (bf16[192,640]{1,0:T(8,128)(2,1)S(1)}, bf16[192,640]{1,0:T(8,128)(2,1)}, u32[]{:S(2)}) copy-start(bf16[192,640]{1,0:T(8,128)(2,1)} %param.6) | copy-start | bytes 737284
  7.2 104.1 %all-gather.2.cloned.1.call-start = ((), (), s32[]{:S(2)}) async-start(), calls=%async_computation.1 | async-start | bytes 2437120 | tf_op jit(solution)/shard_map/all_gather | solution.py:280
  8.2 1.6 %collective-permute-start.5 = (bf16[80,640]{1,0:T(8,128)(2,1)S(1)}, bf16[80,640]{1,0:T(8,128)(2,1)S(1)}, u32[]{:S(2)}, u32[]{:S(2)}) collective-permute-start(bf16[80,640]{1,0:T(8,128)(2,1)S(1)} %convert_bitcast_fusion), channel_id=1, source_target_pairs={{0,0},{1,64},{2,2},{3,66},{4,4},{5,68},{6,6},{7,70},{8,8},{9,72},{... | collective-permute-start | bytes 307208 | tf_op jit(solution)/shard_map/ppermute | solution.py:43
  25.9 16.8 %collective-permute-start.6 = (bf16[224,640]{1,0:T(8,128)(2,1)S(1)}, bf16[224,640]{1,0:T(8,128)(2,1)S(1)}, u32[]{:S(2)}, u32[]{:S(2)}) collective-permute-start(bf16[224,640]{1,0:T(8,128)(2,1)S(1)} %maximum_select_fusion), channel_id=1, source_target_pairs={{0,1},{1,0},{2,3},{3,2},{4,5},{5,4},{6,7},{7,6},{8,9},{9,8},{10,11... | collective-permute-start | bytes 860168 | tf_op jit(solution)/shard_map/ppermute | solution.py:43
  42.7 42.9 %copy-start.6 = (bf16[224,640]{1,0:T(8,128)(2,1)}, bf16[224,640]{1,0:T(8,128)(2,1)S(1)}, u32[]{:S(2)}) copy-start(bf16[224,640]{1,0:T(8,128)(2,1)S(1)} %collective-permute-done.6) | copy-start | bytes 860164
  42.8 42.9 %collective-permute-start.7 = (bf16[384,640]{1,0:T(8,128)(2,1)S(1)}, bf16[384,640]{1,0:T(8,128)(2,1)S(1)}, u32[]{:S(2)}, u32[]{:S(2)}) collective-permute-start(bf16[384,640]{1,0:T(8,128)(2,1)S(1)} %pad_maximum_fusion.4), channel_id=1, source_target_pairs={{0,16},{1,17},{2,18},{3,19},{4,20},{5,21},{6,22},{7,23},{8,24},{9,... | collective-permute-start | bytes 1474568 | tf_op jit(solution)/shard_map/ppermute | solution.py:43
  45.0 2.6 %collective-permute-start = (bf16[80,320]{1,0:T(8,128)(2,1)S(1)}, bf16[80,320]{1,0:T(8,128)(2,1)S(1)}, u32[]{:S(2)}, u32[]{:S(2)}) collective-permute-start(bf16[80,320]{1,0:T(8,128)(2,1)S(1)} %get-tuple-element.30), channel_id=1, source_target_pairs={{0,0},{1,65},{2,130},{3,195},{4,260},{5,325},{6,390},{7,455},{8,8}... | collective-permute-start | bytes 153608 | tf_op jit(solution)/shard_map/ppermute | solution.py:43
  45.7 14.5 %collective-permute-start.1 = (bf16[80,320]{1,0:T(8,128)(2,1)S(1)}, bf16[80,320]{1,0:T(8,128)(2,1)S(1)}, u32[]{:S(2)}, u32[]{:S(2)}) collective-permute-start(bf16[80,320]{1,0:T(8,128)(2,1)S(1)} %get-tuple-element.31), channel_id=1, source_target_pairs={{0,32},{1,97},{2,162},{3,227},{4,292},{5,357},{6,422},{7,487},{8,4... | collective-permute-start | bytes 153608 | tf_op jit(solution)/shard_map/ppermute | solution.py:43
  60.2 11.1 %collective-permute-start.2 = (bf16[80,768]{1,0:T(8,128)(2,1)S(1)}, bf16[80,768]{1,0:T(8,128)(2,1)S(1)}, u32[]{:S(2)}, u32[]{:S(2)}) collective-permute-start(bf16[80,768]{1,0:T(8,128)(2,1)S(1)} %pad_maximum_fusion.7), channel_id=1, source_target_pairs={{0,1},{1,0},{2,3},{3,2},{4,5},{5,4},{6,7},{7,6},{8,9},{9,8},{10,11... | collective-permute-start | bytes 368648 | tf_op jit(solution)/shard_map/ppermute | solution.py:43
  71.3 40.0 %copy-start.4 = (bf16[80,768]{1,0:T(8,128)(2,1)}, bf16[80,768]{1,0:T(8,128)(2,1)S(1)}, u32[]{:S(2)}) copy-start(bf16[80,768]{1,0:T(8,128)(2,1)S(1)} %collective-permute-done.2) | copy-start | bytes 368644
  71.4 22.3 %collective-permute-start.3 = (bf16[160,768]{1,0:T(8,128)(2,1)S(1)}, bf16[160,768]{1,0:T(8,128)(2,1)S(1)}, u32[]{:S(2)}, u32[]{:S(2)}) collective-permute-start(bf16[160,768]{1,0:T(8,128)(2,1)S(1)} %pad_maximum_fusion.5), channel_id=1, source_target_pairs={{0,2},{1,3},{2,0},{3,1},{4,6},{5,7},{6,4},{7,5},{8,10},{9,11},{10,... | collective-permute-start | bytes 737288 | tf_op jit(solution)/shard_map/ppermute | solution.py:43
  85.7 24.2 %collective-permute-start.8 = (bf16[768,640]{1,0:T(8,128)(2,1)S(1)}, bf16[768,640]{1,0:T(8,128)(2,1)}, u32[]{:S(2)}, u32[]{:S(2)}) collective-permute-start(bf16[768,640]{1,0:T(8,128)(2,1)S(1)} %pad_maximum_fusion.1), channel_id=1, source_target_pairs={{0,8},{1,9},{2,10},{3,11},{4,12},{5,13},{6,14},{7,15},{8,0},{9,1},... | collective-permute-start | bytes 2949128 | tf_op jit(solution)/shard_map/ppermute | solution.py:43
  93.6 16.3 %copy-start.5 = (bf16[160,768]{1,0:T(8,128)(2,1)}, bf16[160,768]{1,0:T(8,128)(2,1)S(1)}, u32[]{:S(2)}) copy-start(bf16[160,768]{1,0:T(8,128)(2,1)S(1)} %collective-permute-done.3) | copy-start | bytes 737284
  93.7 13.6 %collective-permute-start.4 = (bf16[320,768]{1,0:T(8,128)(2,1)S(1)}, bf16[320,768]{1,0:T(8,128)(2,1)}, u32[]{:S(2)}, u32[]{:S(2)}) collective-permute-start(bf16[320,768]{1,0:T(8,128)(2,1)S(1)} %pad_maximum_fusion.3), channel_id=1, source_target_pairs={{0,4},{1,5},{2,6},{3,7},{4,0},{5,1},{6,2},{7,3},{8,12},{9,13},{10,... | collective-permute-start | bytes 1474568 | tf_op jit(solution)/shard_map/ppermute | solution.py:43
  109.9 1.4 copy-start.2
  114.9 1.0 copy-start.1
  115.9 6.1 %copy-start = (bf16[1792,640]{1,0:T(8,128)(2,1)S(1)}, bf16[1792,640]{1,0:T(8,128)(2,1)}, u32[]{:S(2)}) copy-start(bf16[1792,640]{1,0:T(8,128)(2,1)} %all-gather.2.cloned.1.call-done.slots) | copy-start | bytes 6881284
  115.9 20.3 %all-to-all-start = ((bf16[4,176,768]{2,1,0:T(8,128)(2,1)}), bf16[4,176,768]{2,1,0:T(8,128)(2,1)S(1)}, u32[]{:S(2)}, u32[]{:S(2)}) async-start(bf16[4,176,768]{2,1,0:T(8,128)(2,1)} %copy-done.1), calls=%async_computation | async-start | bytes 2162688 | tf_op jit(solution)/shard_map/all_to_all | solution.py:318
  123.9 6.9 %collective-permute-start.12 = (f32[160,640]{1,0:T(8,128)S(1)}, f32[160,640]{1,0:T(8,128)S(1)}, u32[]{:S(2)}, u32[]{:S(2)}) collective-permute-start(f32[160,640]{1,0:T(8,128)S(1)} %get-tuple-element.17), channel_id=1, source_target_pairs={{0,8},{1,9},{2,10},{3,11},{4,12},{5,13},{6,14},{7,15},{8,0},{9,1},... | collective-permute-start | bytes 1228808 | tf_op jit(solution)/shard_map/ppermute | solution.py:43
  131.4 14.8 %collective-permute-start.13 = (f32[80,640]{1,0:T(8,128)S(1)}, f32[80,640]{1,0:T(8,128)S(1)}, u32[]{:S(2)}, u32[]{:S(2)}) collective-permute-start(f32[80,640]{1,0:T(8,128)S(1)} %get-tuple-element.19), channel_id=1, source_target_pairs={{0,16},{1,17},{2,18},{3,19},{4,20},{5,21},{6,22},{7,23},{8,24},{9,... | collective-permute-start | bytes 614408 | tf_op jit(solution)/shard_map/ppermute | solution.py:43
  137.0 10.0 %collective-permute-start.10 = (bf16[160,256]{1,0:T(8,128)(2,1)S(1)}, bf16[160,256]{1,0:T(8,128)(2,1)S(1)}, u32[]{:S(2)}, u32[]{:S(2)}) collective-permute-start(bf16[160,256]{1,0:T(8,128)(2,1)S(1)} %get-tuple-element.13), channel_id=1, source_target_pairs={{0,16},{1,17},{2,18},{3,19},{4,20},{5,21},{6,22},{7,23},{8,24},{9,... | collective-permute-start | bytes 245768 | tf_op jit(solution)/shard_map/ppermute | solution.py:43
  138.9 8.0 %collective-permute-start.11 = (bf16[160,256]{1,0:T(8,128)(2,1)S(1)}, bf16[160,256]{1,0:T(8,128)(2,1)S(1)}, u32[]{:S(2)}, u32[]{:S(2)}) collective-permute-start(bf16[160,256]{1,0:T(8,128)(2,1)S(1)} %get-tuple-element.14), channel_id=1, source_target_pairs={{0,24},{1,25},{2,26},{3,27},{4,28},{5,29},{6,30},{7,31},{8,16},{9,... | collective-permute-start | bytes 245768 | tf_op jit(solution)/shard_map/ppermute | solution.py:43
  143.9 3.3 %collective-permute-start.9 = (f32[160,256]{1,0:T(8,128)S(1)}, f32[160,256]{1,0:T(8,128)S(1)}, u32[]{:S(2)}, u32[]{:S(2)}) collective-permute-start(f32[160,256]{1,0:T(8,128)S(1)} %get-tuple-element.12), channel_id=1, source_target_pairs={{0,8},{1,9},{2,10},{3,11},{4,12},{5,13},{6,14},{7,15},{8,0},{9,1},... | collective-permute-start | bytes 491528 | tf_op jit(solution)/shard_map/ppermute | solution.py:43
Sparse Core Ops, SparseCore 0:
  10.7 80.8 all-gather.1

commit v9 on v8

--- a/solution.py
+++ b/solution.py
@@ -280,11 +280,12 @@
     slots = lax.all_gather(slot, "z", axis=0, tiled=True)
 
     levels = rank_row(ranks)
-    other = move(after(jnp.concatenate([tokens, left]), levels), xh_target)
+    chunk = spread_right(right_factors, levels, z, tensor)
+    other = move(after(jnp.concatenate([tokens, left]), chunk), xh_target)
     rows = jnp.concatenate([tokens, other[:ROWS]])
     rows = jnp.concatenate([rows, move(rows, xl_target)])
     rows = jnp.concatenate([rows, move(rows, core_target)])
-    right = gather_right(spread_right(right_factors, levels, z, tensor))
+    right = gather_right(chunk)
     keep, give = call(
         functools.partial(update_kernel, members),
         (shape(160, IN_BLOCK), shape(160, IN_BLOCK)),

time: 157 us -> 163 us (1.038)
  the two profiles are of different devices: /device:TPU:1 before, /device:TPU:67 now
where the time goes in v9:
time: 163 us; the launch traced here: 162 us
  starting transfers between devices  87.8 us (54%)
  waiting for transfers between devices  27.9 us (17%)
  between operations  17 us (10%)
  Pallas kernels  8.72 us (5%)
  other arithmetic  6.93 us (4%)
  blocking collectives  6.83 us (4%)
  local copies, waits for them, and re-layouts  6.76 us (4%)
    ppermute x14, starting transfers between devices, move(): lax.ppermute(value, AXES, [(flat(p), flat(target(*p))) for p in places])  83.7 us
    ppermute x14, waiting for transfers between devices, move(): lax.ppermute(value, AXES, [(flat(p), flat(target(*p))) for p in places])  27.8 us
    pallas_call x5, Pallas kernels, call(): pl.pallas_call(kernel, out_shape=outs, in_specs=[SMEM] + [VMEM] * len(arr...  8.72 us
    all_gather x1, blocking collectives, rank_row(): every = lax.all_gather(own, ('xl', 'core'), axis=1, tiled=True)  6.83 us
    all_to_all x1, starting transfers between devices, on_device(): got = lax.all_to_all(give, 'y', split_axis=0, concat_axis=0, tiled=True)  4.08 us
  transfers between devices with their start and end apart: 16, of which 8 were waited for; matrix products, arithmetic and copies ran while one was open for 7% of the time, Pallas kernels for 2%

profile of v9, /device:TPU:67, one launch (start us, length us, event | category | flops | bytes accessed | tf_op | source)
XLA Modules:
  0.0 161.9 jit_solution(9734895471112140714)
XLA Ops:
  8.2 2.8 %collective-permute-start.5 = (bf16[80,640]{1,0:T(8,128)(2,1)S(1)}, bf16[80,640]{1,0:T(8,128)(2,1)S(1)}, u32[]{:S(2)}, u32[]{:S(2)}) collective-permute-start(bf16[80,640]{1,0:T(8,128)(2,1)S(1)} %convert_bitcast_fusion), channel_id=1, source_target_pairs={{0,0},{1,64},{2,2},{3,66},{4,4},{5,68},{6,6},{7,70},{8,8},{9,72},{... | collective-permute-start | bytes 307208 | tf_op jit(solution)/shard_map/ppermute | solution.py:43
  12.0 5.0 %collective-permute-done.5 = bf16[80,640]{1,0:T(8,128)(2,1)S(1)} collective-permute-done((bf16[80,640]{1,0:T(8,128)(2,1)S(1)}, bf16[80,640]{1,0:T(8,128)(2,1)S(1)}, u32[]{:S(2)}, u32[]{:S(2)}) %collective-permute-start.5) | collective-permute-done | bytes 102432 | tf_op jit(solution)/shard_map/ppermute | solution.py:43
  19.5 6.8 %all_gather.6 = bf16[16,512]{1,0:T(8,128)(2,1)S(1)} all-gather(bf16[16,128]{1,0:T(8,128)(2,1)S(1)} %pad.15), channel_id=1, replica_groups=mesh['z'=16,'xl'=2,'core'=2,'y'=4,'xh'=2] {'xl','core'}, dimensions={1}, use_global_device_ids=true | all-gather | bytes 20480 | tf_op jit(solution)/shard_map/all_gather | solution.py:201
  29.0 12.5 %collective-permute-start.6 = (bf16[224,640]{1,0:T(8,128)(2,1)S(1)}, bf16[224,640]{1,0:T(8,128)(2,1)}, u32[]{:S(2)}, u32[]{:S(2)}) collective-permute-start(bf16[224,640]{1,0:T(8,128)(2,1)S(1)} %maximum_select_fusion), channel_id=1, source_target_pairs={{0,1},{1,0},{2,3},{3,2},{4,5},{5,4},{6,7},{7,6},{8,9},{9,8},{10,11... | collective-permute-start | bytes 860168 | tf_op jit(solution)/shard_map/ppermute | solution.py:43
  41.6 6.2 %collective-permute-done.6 = bf16[224,640]{1,0:T(8,128)(2,1)} collective-permute-done((bf16[224,640]{1,0:T(8,128)(2,1)S(1)}, bf16[224,640]{1,0:T(8,128)(2,1)}, u32[]{:S(2)}, u32[]{:S(2)}) %collective-permute-start.6) | collective-permute-done | bytes 286752 | tf_op jit(solution)/shard_map/ppermute | solution.py:43
  48.8 3.1 %collective-permute-start.7 = (bf16[384,640]{1,0:T(8,128)(2,1)S(1)}, bf16[384,640]{1,0:T(8,128)(2,1)S(1)}, u32[]{:S(2)}, u32[]{:S(2)}) collective-permute-start(bf16[384,640]{1,0:T(8,128)(2,1)S(1)} %pad_maximum_fusion.4), channel_id=1, source_target_pairs={{0,16},{1,17},{2,18},{3,19},{4,20},{5,21},{6,22},{7,23},{8,24},{9,... | collective-permute-start | bytes 1474568 | tf_op jit(solution)/shard_map/ppermute | solution.py:43
  51.9 1.9 %collective-permute-start.1 = (bf16[80,320]{1,0:T(8,128)(2,1)S(1)}, bf16[80,320]{1,0:T(8,128)(2,1)S(1)}, u32[]{:S(2)}, u32[]{:S(2)}) collective-permute-start(bf16[80,320]{1,0:T(8,128)(2,1)S(1)} %get-tuple-element.31), channel_id=1, source_target_pairs={{0,32},{1,97},{2,162},{3,227},{4,292},{5,357},{6,422},{7,487},{8,4... | collective-permute-start | bytes 153608 | tf_op jit(solution)/shard_map/ppermute | solution.py:43
  53.8 3.5 %collective-permute-done.1 = bf16[80,320]{1,0:T(8,128)(2,1)S(1)} collective-permute-done((bf16[80,320]{1,0:T(8,128)(2,1)S(1)}, bf16[80,320]{1,0:T(8,128)(2,1)S(1)}, u32[]{:S(2)}, u32[]{:S(2)}) %collective-permute-start.1) | collective-permute-done | bytes 51232 | tf_op jit(solution)/shard_map/ppermute | solution.py:43
  57.4 6.7 %collective-permute-start.2 = (bf16[80,768]{1,0:T(8,128)(2,1)S(1)}, bf16[80,768]{1,0:T(8,128)(2,1)S(1)}, u32[]{:S(2)}, u32[]{:S(2)}) collective-permute-start(bf16[80,768]{1,0:T(8,128)(2,1)S(1)} %pad_maximum_fusion.7), channel_id=1, source_target_pairs={{0,1},{1,0},{2,3},{3,2},{4,5},{5,4},{6,7},{7,6},{8,9},{9,8},{10,11... | collective-permute-start | bytes 368648 | tf_op jit(solution)/shard_map/ppermute | solution.py:43
  64.1 2.6 %collective-permute-done.2 = bf16[80,768]{1,0:T(8,128)(2,1)S(1)} collective-permute-done((bf16[80,768]{1,0:T(8,128)(2,1)S(1)}, bf16[80,768]{1,0:T(8,128)(2,1)S(1)}, u32[]{:S(2)}, u32[]{:S(2)}) %collective-permute-start.2) | collective-permute-done | bytes 122912 | tf_op jit(solution)/shard_map/ppermute | solution.py:43
  66.7 21.3 %collective-permute-start.3 = (bf16[160,768]{1,0:T(8,128)(2,1)S(1)}, bf16[160,768]{1,0:T(8,128)(2,1)S(1)}, u32[]{:S(2)}, u32[]{:S(2)}) collective-permute-start(bf16[160,768]{1,0:T(8,128)(2,1)S(1)} %pad_maximum_fusion.5), channel_id=1, source_target_pairs={{0,2},{1,3},{2,0},{3,1},{4,6},{5,7},{6,4},{7,5},{8,10},{9,11},{10,... | collective-permute-start | bytes 737288 | tf_op jit(solution)/shard_map/ppermute | solution.py:43
  88.2 4.6 %collective-permute-start.8 = (bf16[768,640]{1,0:T(8,128)(2,1)S(1)}, bf16[768,640]{1,0:T(8,128)(2,1)}, u32[]{:S(2)}, u32[]{:S(2)}) collective-permute-start(bf16[768,640]{1,0:T(8,128)(2,1)S(1)} %pad_maximum_fusion.1), channel_id=1, source_target_pairs={{0,8},{1,9},{2,10},{3,11},{4,12},{5,13},{6,14},{7,15},{8,0},{9,1},... | collective-permute-start | bytes 2949128 | tf_op jit(solution)/shard_map/ppermute | solution.py:43
  92.8 12.3 %collective-permute-start.4 = (bf16[320,768]{1,0:T(8,128)(2,1)S(1)}, bf16[320,768]{1,0:T(8,128)(2,1)}, u32[]{:S(2)}, u32[]{:S(2)}) collective-permute-start(bf16[320,768]{1,0:T(8,128)(2,1)S(1)} %pad_maximum_fusion.3), channel_id=1, source_target_pairs={{0,4},{1,5},{2,6},{3,7},{4,0},{5,1},{6,2},{7,3},{8,12},{9,13},{10,... | collective-permute-start | bytes 1474568 | tf_op jit(solution)/shard_map/ppermute | solution.py:43
  106.0 8.5 %collective-permute-done.4 = bf16[320,768]{1,0:T(8,128)(2,1)} collective-permute-done((bf16[320,768]{1,0:T(8,128)(2,1)S(1)}, bf16[320,768]{1,0:T(8,128)(2,1)}, u32[]{:S(2)}, u32[]{:S(2)}) %collective-permute-start.4) | collective-permute-done | bytes 491552 | tf_op jit(solution)/shard_map/ppermute | solution.py:43
  117.1 1.4 pad_maximum_fusion.rows
  118.6 3.6 %shard_map.77 = bf16[4,176,768]{2,1,0:T(8,128)(2,1)S(1)} custom-call(s32[7]{0:T(128)S(1)} %broadcast_add_fusion.place, bf16[1792,640]{1,0:T(8,128)(2,1)} %all-gather.2.cloned.1.call-done.slots, bf16[1536,640]{1,0:T(8,128)(2,1)S(1)} %pad_maximum_fusion.rows, bf16[32,640]{1,0:T(8,128)(2,1)S(1)} %reshape.23.left, bf16[32,640]{1,0:T(8,128)(2,1)S(1)} %slice.42.other_left, ...), custom_call_target="tpu_custom_call" | custom-call | flops 1258291200 | bytes 6291456 | tf_op jit(solution)/shard_map/pallas_call | solution.py:125
  123.2 4.1 %all-to-all-start = ((bf16[4,176,768]{2,1,0:T(8,128)(2,1)}), bf16[4,176,768]{2,1,0:T(8,128)(2,1)S(1)}, u32[]{:S(2)}, u32[]{:S(2)}) async-start(bf16[4,176,768]{2,1,0:T(8,128)(2,1)} %copy-done.1), calls=%async_computation | async-start | bytes 2162688 | tf_op jit(solution)/shard_map/all_to_all | solution.py:319
  128.5 1.9 %shard_map.80 = (f32[160,640]{1,0:T(8,128)S(1)}, f32[160,640]{1,0:T(8,128)S(1)}) custom-call(s32[7]{0:T(128)S(1)} %stack.31.place, bf16[1792,640]{1,0:T(8,128)(2,1)S(1)} %copy-done, bf16[640,768]{1,0:T(8,128)(2,1)S(1)} %pad_maximum_fusion.2.right), custom_call_target="tpu_custom_call" | custom-call | flops 503316480 | bytes 4194304 | tf_op jit(solution)/shard_map/pallas_call | solution.py:125
  130.4 5.3 %collective-permute-start.12 = (f32[160,640]{1,0:T(8,128)S(1)}, f32[160,640]{1,0:T(8,128)S(1)}, u32[]{:S(2)}, u32[]{:S(2)}) collective-permute-start(f32[160,640]{1,0:T(8,128)S(1)} %get-tuple-element.17), channel_id=1, source_target_pairs={{0,8},{1,9},{2,10},{3,11},{4,12},{5,13},{6,14},{7,15},{8,0},{9,1},... | collective-permute-start | bytes 1228808 | tf_op jit(solution)/shard_map/ppermute | solution.py:43
  137.7 2.4 %collective-permute-start.13 = (f32[80,640]{1,0:T(8,128)S(1)}, f32[80,640]{1,0:T(8,128)S(1)}, u32[]{:S(2)}, u32[]{:S(2)}) collective-permute-start(f32[80,640]{1,0:T(8,128)S(1)} %get-tuple-element.19), channel_id=1, source_target_pairs={{0,16},{1,17},{2,18},{3,19},{4,20},{5,21},{6,22},{7,23},{8,24},{9,... | collective-permute-start | bytes 614408 | tf_op jit(solution)/shard_map/ppermute | solution.py:43
  141.8 2.9 %collective-permute-start.10 = (bf16[160,256]{1,0:T(8,128)(2,1)S(1)}, bf16[160,256]{1,0:T(8,128)(2,1)S(1)}, u32[]{:S(2)}, u32[]{:S(2)}) collective-permute-start(bf16[160,256]{1,0:T(8,128)(2,1)S(1)} %get-tuple-element.13), channel_id=1, source_target_pairs={{0,16},{1,17},{2,18},{3,19},{4,20},{5,21},{6,22},{7,23},{8,24},{9,... | collective-permute-start | bytes 245768 | tf_op jit(solution)/shard_map/ppermute | solution.py:43
  144.7 5.2 %collective-permute-start.11 = (bf16[160,256]{1,0:T(8,128)(2,1)S(1)}, bf16[160,256]{1,0:T(8,128)(2,1)S(1)}, u32[]{:S(2)}, u32[]{:S(2)}) collective-permute-start(bf16[160,256]{1,0:T(8,128)(2,1)S(1)} %get-tuple-element.14), channel_id=1, source_target_pairs={{0,24},{1,25},{2,26},{3,27},{4,28},{5,29},{6,30},{7,31},{8,16},{9,... | collective-permute-start | bytes 245768 | tf_op jit(solution)/shard_map/ppermute | solution.py:43
  149.8 1.9 %collective-permute-start.9 = (f32[160,256]{1,0:T(8,128)S(1)}, f32[160,256]{1,0:T(8,128)S(1)}, u32[]{:S(2)}, u32[]{:S(2)}) collective-permute-start(f32[160,256]{1,0:T(8,128)S(1)} %get-tuple-element.12), channel_id=1, source_target_pairs={{0,8},{1,9},{2,10},{3,11},{4,12},{5,13},{6,14},{7,15},{8,0},{9,1},... | collective-permute-start | bytes 491528 | tf_op jit(solution)/shard_map/ppermute | solution.py:43
  153.1 1.9 %shard_map.79 = f32[192,640]{1,0:T(8,128)} custom-call(s32[7]{0:T(128)S(1)} %stack.31.place, f32[160,256]{1,0:T(8,128)S(1)} %get-tuple-element.11.mine, f32[160,256]{1,0:T(8,128)S(1)} %collective-permute-done.9.from_core, bf16[160,256]{1,0:T(8,128)(2,1)S(1)} %collective-permute-done.10.from_xl, bf16[160,256]{1,0:T(8,128)(2,1)S(1)} %collective-permute-done.11.from_diagonal, ...), custom_call_target="tpu_custom_call" | custom-call | flops 47185920 | bytes 4194304 | tf_op jit(solution)/shard_map/pallas_call | solution.py:125
  (59 shorter events, 16.4 us)
Async XLA Ops:
  7.2 21.8 %copy-start.3 = (bf16[192,640]{1,0:T(8,128)(2,1)S(1)}, bf16[192,640]{1,0:T(8,128)(2,1)}, u32[]{:S(2)}) copy-start(bf16[192,640]{1,0:T(8,128)(2,1)} %param.6) | copy-start | bytes 737284
  7.2 111.4 %all-gather.2.cloned.1.call-start = ((), (), s32[]{:S(2)}) async-start(), calls=%async_computation.1 | async-start | bytes 2437120 | tf_op jit(solution)/shard_map/all_gather | solution.py:280
  8.2 8.8 %collective-permute-start.5 = (bf16[80,640]{1,0:T(8,128)(2,1)S(1)}, bf16[80,640]{1,0:T(8,128)(2,1)S(1)}, u32[]{:S(2)}, u32[]{:S(2)}) collective-permute-start(bf16[80,640]{1,0:T(8,128)(2,1)S(1)} %convert_bitcast_fusion), channel_id=1, source_target_pairs={{0,0},{1,64},{2,2},{3,66},{4,4},{5,68},{6,6},{7,70},{8,8},{9,72},{... | collective-permute-start | bytes 307208 | tf_op jit(solution)/shard_map/ppermute | solution.py:43
  26.5 0.7 collective-permute-start
  29.0 18.8 %collective-permute-start.6 = (bf16[224,640]{1,0:T(8,128)(2,1)S(1)}, bf16[224,640]{1,0:T(8,128)(2,1)}, u32[]{:S(2)}, u32[]{:S(2)}) collective-permute-start(bf16[224,640]{1,0:T(8,128)(2,1)S(1)} %maximum_select_fusion), channel_id=1, source_target_pairs={{0,1},{1,0},{2,3},{3,2},{4,5},{5,4},{6,7},{7,6},{8,9},{9,8},{10,11... | collective-permute-start | bytes 860168 | tf_op jit(solution)/shard_map/ppermute | solution.py:43
  48.8 39.2 %collective-permute-start.7 = (bf16[384,640]{1,0:T(8,128)(2,1)S(1)}, bf16[384,640]{1,0:T(8,128)(2,1)S(1)}, u32[]{:S(2)}, u32[]{:S(2)}) collective-permute-start(bf16[384,640]{1,0:T(8,128)(2,1)S(1)} %pad_maximum_fusion.4), channel_id=1, source_target_pairs={{0,16},{1,17},{2,18},{3,19},{4,20},{5,21},{6,22},{7,23},{8,24},{9,... | collective-permute-start | bytes 1474568 | tf_op jit(solution)/shard_map/ppermute | solution.py:43
  51.9 5.4 %collective-permute-start.1 = (bf16[80,320]{1,0:T(8,128)(2,1)S(1)}, bf16[80,320]{1,0:T(8,128)(2,1)S(1)}, u32[]{:S(2)}, u32[]{:S(2)}) collective-permute-start(bf16[80,320]{1,0:T(8,128)(2,1)S(1)} %get-tuple-element.31), channel_id=1, source_target_pairs={{0,32},{1,97},{2,162},{3,227},{4,292},{5,357},{6,422},{7,487},{8,4... | collective-permute-start | bytes 153608 | tf_op jit(solution)/shard_map/ppermute | solution.py:43
  57.4 9.3 %collective-permute-start.2 = (bf16[80,768]{1,0:T(8,128)(2,1)S(1)}, bf16[80,768]{1,0:T(8,128)(2,1)S(1)}, u32[]{:S(2)}, u32[]{:S(2)}) collective-permute-start(bf16[80,768]{1,0:T(8,128)(2,1)S(1)} %pad_maximum_fusion.7), channel_id=1, source_target_pairs={{0,1},{1,0},{2,3},{3,2},{4,5},{5,4},{6,7},{7,6},{8,9},{9,8},{10,11... | collective-permute-start | bytes 368648 | tf_op jit(solution)/shard_map/ppermute | solution.py:43
  66.7 51.8 %copy-start.4 = (bf16[80,768]{1,0:T(8,128)(2,1)}, bf16[80,768]{1,0:T(8,128)(2,1)S(1)}, u32[]{:S(2)}) copy-start(bf16[80,768]{1,0:T(8,128)(2,1)S(1)} %collective-permute-done.2) | copy-start | bytes 368644
  66.7 26.0 %collective-permute-start.3 = (bf16[160,768]{1,0:T(8,128)(2,1)S(1)}, bf16[160,768]{1,0:T(8,128)(2,1)S(1)}, u32[]{:S(2)}, u32[]{:S(2)}) collective-permute-start(bf16[160,768]{1,0:T(8,128)(2,1)S(1)} %pad_maximum_fusion.5), channel_id=1, source_target_pairs={{0,2},{1,3},{2,0},{3,1},{4,6},{5,7},{6,4},{7,5},{8,10},{9,11},{10,... | collective-permute-start | bytes 737288 | tf_op jit(solution)/shard_map/ppermute | solution.py:43
  88.2 29.0 %collective-permute-start.8 = (bf16[768,640]{1,0:T(8,128)(2,1)S(1)}, bf16[768,640]{1,0:T(8,128)(2,1)}, u32[]{:S(2)}, u32[]{:S(2)}) collective-permute-start(bf16[768,640]{1,0:T(8,128)(2,1)S(1)} %pad_maximum_fusion.1), channel_id=1, source_target_pairs={{0,8},{1,9},{2,10},{3,11},{4,12},{5,13},{6,14},{7,15},{8,0},{9,1},... | collective-permute-start | bytes 2949128 | tf_op jit(solution)/shard_map/ppermute | solution.py:43
  92.8 24.3 %copy-start.5 = (bf16[160,768]{1,0:T(8,128)(2,1)}, bf16[160,768]{1,0:T(8,128)(2,1)S(1)}, u32[]{:S(2)}) copy-start(bf16[160,768]{1,0:T(8,128)(2,1)S(1)} %collective-permute-done.3) | copy-start | bytes 737284
  92.8 21.7 %collective-permute-start.4 = (bf16[320,768]{1,0:T(8,128)(2,1)S(1)}, bf16[320,768]{1,0:T(8,128)(2,1)}, u32[]{:S(2)}, u32[]{:S(2)}) collective-permute-start(bf16[320,768]{1,0:T(8,128)(2,1)S(1)} %pad_maximum_fusion.3), channel_id=1, source_target_pairs={{0,4},{1,5},{2,6},{3,7},{4,0},{5,1},{6,2},{7,3},{8,12},{9,13},{10,... | collective-permute-start | bytes 1474568 | tf_op jit(solution)/shard_map/ppermute | solution.py:43
  117.1 1.4 copy-start.2
  122.1 1.0 copy-start.1
  123.2 5.3 %copy-start = (bf16[1792,640]{1,0:T(8,128)(2,1)S(1)}, bf16[1792,640]{1,0:T(8,128)(2,1)}, u32[]{:S(2)}) copy-start(bf16[1792,640]{1,0:T(8,128)(2,1)} %all-gather.2.cloned.1.call-done.slots) | copy-start | bytes 6881284
  123.2 17.9 %all-to-all-start = ((bf16[4,176,768]{2,1,0:T(8,128)(2,1)}), bf16[4,176,768]{2,1,0:T(8,128)(2,1)S(1)}, u32[]{:S(2)}, u32[]{:S(2)}) async-start(bf16[4,176,768]{2,1,0:T(8,128)(2,1)} %copy-done.1), calls=%async_computation | async-start | bytes 2162688 | tf_op jit(solution)/shard_map/all_to_all | solution.py:319
  130.4 6.7 %collective-permute-start.12 = (f32[160,640]{1,0:T(8,128)S(1)}, f32[160,640]{1,0:T(8,128)S(1)}, u32[]{:S(2)}, u32[]{:S(2)}) collective-permute-start(f32[160,640]{1,0:T(8,128)S(1)} %get-tuple-element.17), channel_id=1, source_target_pairs={{0,8},{1,9},{2,10},{3,11},{4,12},{5,13},{6,14},{7,15},{8,0},{9,1},... | collective-permute-start | bytes 1228808 | tf_op jit(solution)/shard_map/ppermute | solution.py:43
  137.7 14.1 %collective-permute-start.13 = (f32[80,640]{1,0:T(8,128)S(1)}, f32[80,640]{1,0:T(8,128)S(1)}, u32[]{:S(2)}, u32[]{:S(2)}) collective-permute-start(f32[80,640]{1,0:T(8,128)S(1)} %get-tuple-element.19), channel_id=1, source_target_pairs={{0,16},{1,17},{2,18},{3,19},{4,20},{5,21},{6,22},{7,23},{8,24},{9,... | collective-permute-start | bytes 614408 | tf_op jit(solution)/shard_map/ppermute | solution.py:43
  141.8 10.7 %collective-permute-start.10 = (bf16[160,256]{1,0:T(8,128)(2,1)S(1)}, bf16[160,256]{1,0:T(8,128)(2,1)S(1)}, u32[]{:S(2)}, u32[]{:S(2)}) collective-permute-start(bf16[160,256]{1,0:T(8,128)(2,1)S(1)} %get-tuple-element.13), channel_id=1, source_target_pairs={{0,16},{1,17},{2,18},{3,19},{4,20},{5,21},{6,22},{7,23},{8,24},{9,... | collective-permute-start | bytes 245768 | tf_op jit(solution)/shard_map/ppermute | solution.py:43
  144.7 8.1 %collective-permute-start.11 = (bf16[160,256]{1,0:T(8,128)(2,1)S(1)}, bf16[160,256]{1,0:T(8,128)(2,1)S(1)}, u32[]{:S(2)}, u32[]{:S(2)}) collective-permute-start(bf16[160,256]{1,0:T(8,128)(2,1)S(1)} %get-tuple-element.14), channel_id=1, source_target_pairs={{0,24},{1,25},{2,26},{3,27},{4,28},{5,29},{6,30},{7,31},{8,16},{9,... | collective-permute-start | bytes 245768 | tf_op jit(solution)/shard_map/ppermute | solution.py:43
  149.8 3.3 %collective-permute-start.9 = (f32[160,256]{1,0:T(8,128)S(1)}, f32[160,256]{1,0:T(8,128)S(1)}, u32[]{:S(2)}, u32[]{:S(2)}) collective-permute-start(f32[160,256]{1,0:T(8,128)S(1)} %get-tuple-element.12), channel_id=1, source_target_pairs={{0,8},{1,9},{2,10},{3,11},{4,12},{5,13},{6,14},{7,15},{8,0},{9,1},... | collective-permute-start | bytes 491528 | tf_op jit(solution)/shard_map/ppermute | solution.py:43
Sparse Core Ops, SparseCore 0:
  17.8 71.4 all-gather.1
